TPU v7x, 256 devices: a whole 4x4x8 slice. The times are simulated.
256 devices in a mesh: enc: 4 (over y), seq: 16 (over z, core), mp: 4 (over x).
Axes of the slice: x: 4, y: 4, z: 8, core: 2. Of those that a mesh axis runs over, the one named last changes fastest.
Arguments:
- queries: bfloat16 [4, 2048, 4096], P('enc', 'seq', 'mp'), may hold values from -6 to 6
- keys_in: bfloat16 [4, 2048, 4096], P('enc', 'seq', 'mp'), may hold values from -6 to 6
- values_in: bfloat16 [4, 2048, 4096], P('enc', 'seq', 'mp'), may hold values from -6 to 6
- memory: bfloat16 [128, 128, 1024], P('enc', None, 'mp'), may hold values from -11 to 11
- enc_wq: bfloat16 [1024, 1024], P(None, 'mp'), may hold values from -1 to 1
- enc_wk: bfloat16 [1024, 1024], P(None, 'mp'), may hold values from -2 to 2
- enc_wv: bfloat16 [1024, 1024], P(None, 'mp'), may hold values from -0.1875 to 0.1875
- enc_wo: bfloat16 [1024, 1024], P('mp'), may hold values from -0.75 to 0.75
- cross_wk: bfloat16 [1024, 4096], P(None, 'mp'), may hold values from -0.1875 to 0.1875
- cross_wv: bfloat16 [1024, 4096], P(None, 'mp'), may hold values from -0.1875 to 0.1875
- cross_wq: bfloat16 [32, 128, 128], P('mp'), may hold values from -0.5 to 0.5
- nbr_rows: int32 [4, 32, 2], P('enc', 'seq'), may hold values from 0 to 31
- nbr_owner: int32 [4, 32, 2], P('enc', 'seq'), may hold values from 0 to 3, as said below
- nbr_count: int32 [4, 32], P('enc'), may hold values from 0 to 2, as said below
Outputs:
- attended: bfloat16 [4, 2048, 4096], P('enc', 'seq', 'mp')
Inputs may be any that keep to these rules, and one draw needn't show every extreme that they name: `nbr_owner`: the 2 neighbours of a span have different owners; within the spans of one index of seq (aligned blocks of 2 spans of a sequence) no owner holds more than 2 neighbours, and some owner holds exactly 2 in every block. `nbr_count`: the spans of each sequence's first 128 tokens have 2 live neighbours.
All inputs are finite; a program needn't handle non-finite values.
Results may differ from a plain program's by a relative error of at most 0.029.
The roundings to bfloat16 on the way count: a program that leaves them out, or rounds other values in their place, can miss the bound.
Values may be sent and summed in bfloat16 or wider, within the bound.
No kernel may reach another device: no remote copies, remote signals or barrier semaphores. Data moves between devices by JAX's collectives and lax.ppermute only.
A program may use at most 128 MiB of HBM per device.

v0:
```python
import math

import jax
import jax.numpy as jnp
from jax import lax
from jax.experimental import pallas as pl
from jax.experimental.pallas import tpu as pltpu
from jax.sharding import PartitionSpec as P

HEAD_DIM = 128
SPAN = 64
K_NB = 2
NT = 128
DB = 32
N_ENC = 4
N_MP = 4
N_Z = 8
NEG_BIG = -1e30
SCALE = 1.0 / math.sqrt(HEAD_DIM)
EXP2_SCALE = SCALE * math.log2(math.e)
BF = jnp.bfloat16
F32 = jnp.float32

ANY = pl.BlockSpec(memory_space=pl.ANY)
SMEM = pl.BlockSpec(memory_space=pltpu.SMEM)
VMEM = pl.BlockSpec(memory_space=pltpu.VMEM)
MB = 1024 * 1024


def shifted(block, axis, distance):
    size = lax.axis_size(axis)
    return lax.ppermute(block, axis, [(i, (i + distance) % size) for i in range(size)])


def to_sides(block):
    seqs, mps = lax.axis_size("seq"), lax.axis_size("mp")
    route = [
        (s * mps + m, s * mps + (m + (1 if s % 2 == 0 else -1)) % mps)
        for s in range(seqs)
        for m in range(mps)
    ]
    return lax.ppermute(block, ("seq", "mp"), route)


def core_swap(block):
    size = lax.axis_size("seq")
    return lax.ppermute(block, "seq", [(i, i ^ 1) for i in range(size)])


def over_z(blocks):
    groups = [[2 * z + core for z in range(N_Z)] for core in range(2)]
    return lax.all_to_all(blocks, "seq", 0, 0, axis_index_groups=groups, tiled=True)


def in_hbm(x):
    return pltpu.with_memory_space_constraint(x, pltpu.HBM)


def after(x, *others):
    def kernel(*refs):
        pass

    return pl.pallas_call(
        kernel,
        out_shape=sds(x.shape, x.dtype),
        in_specs=[ANY] * (1 + len(others)),
        out_specs=ANY,
        input_output_aliases={0: 0},
        compiler_params=params(1),
        cost_estimate=cost(0, 1024),
        name="after",
    )(x, *others)


def sds(shape, dtype=BF):
    return jax.ShapeDtypeStruct(shape, dtype)


def params(limit_mb):
    return pltpu.CompilerParams(vmem_limit_bytes=limit_mb * MB)


def cost(flops, nbytes, trans=0):
    return pl.CostEstimate(flops=flops, bytes_accessed=nbytes, transcendentals=trans)


def dot(a, b):
    return jnp.dot(a, b, preferred_element_type=F32)


def dot_t(a, b):
    return lax.dot_general(a, b, (((1,), (1,)), ((), ())), preferred_element_type=F32)


def run_copies(pairs, sems):
    copies = [pltpu.make_async_copy(s, d, sems.at[n]) for n, (s, d) in enumerate(pairs)]
    for c in copies:
        c.start()
    return copies


def fetch_kernel(idx0, idx1, idx2, idx3, memory, s0, s1, s2, s3, sems):
    me = lax.axis_index("enc")
    pairs = []
    for idx, out in ((idx0, s0), (idx1, s1), (idx2, s2), (idx3, s3)):
        for span in range(2):
            row = jnp.int32(0)
            for j in range(K_NB):
                flat = idx[span * K_NB + j]
                row = jnp.where(flat // DB == me, flat % DB, row)
            pairs.append((memory.at[row], out.at[pl.ds(span * NT, NT)]))
    for c in run_copies(pairs, sems):
        c.wait()


def fetch(idx, memory):
    cols = memory.shape[2]
    return pl.pallas_call(
        fetch_kernel,
        out_shape=[sds((2 * NT, cols))] * 4,
        in_specs=[SMEM] * 4 + [ANY],
        out_specs=[ANY] * 4,
        scratch_shapes=[pltpu.SemaphoreType.DMA((8,))],
        compiler_params=params(1),
        cost_estimate=cost(20 * 10**9, 1024),
        name="fetch",
    )(*idx, in_hbm(memory))


def compact_kernel(idx, r0, r1, r2, r3, w1, w2, out, sems):
    me = lax.axis_index("enc")

    def each(act):
        for span in range(2):
            for j in range(K_NB):
                at = (idx[span * K_NB + j] // DB - me + N_ENC) % N_ENC
                for k, r in enumerate((r0, r1, r2, r3)):

                    @pl.when(at == k)
                    def _():
                        act(
                            pltpu.make_async_copy(
                                r.at[pl.ds(span * NT, NT)],
                                out.at[pl.ds((span * K_NB + j) * NT, NT)],
                                sems.at[span * K_NB + j],
                            )
                        )

    each(lambda c: c.start())
    each(lambda c: c.wait())


def compact(idx, received, others):
    rows, cols = received[0].shape
    return pl.pallas_call(
        compact_kernel,
        out_shape=pltpu.HBM((K_NB * rows, cols), BF),
        in_specs=[SMEM] + [ANY] * 6,
        out_specs=ANY,
        scratch_shapes=[pltpu.SemaphoreType.DMA((4,))],
        compiler_params=params(1),
        cost_estimate=cost(1 * 10**9, 1024),
        name="compact",
    )(idx, *received, *others)


def source_columns(k, width):
    col = (lax.axis_index("mp") - k + N_MP) % N_MP
    return pl.ds(pl.multiple_of(col * width, width), width)


def encode_kernel(x0, x1, x2, x3, wq, wk, wv, second, first, src_out, src, w, sems):
    width = x0.shape[1]
    pairs = [(x, src.at[:, source_columns(k, width)]) for k, x in enumerate((x0, x1, x2, x3))]
    pairs += [(ref, w.at[n]) for n, ref in enumerate((wq, wk, wv))]
    copies = run_copies(pairs, sems)
    for c in copies[:5]:
        c.wait()
    kept = pltpu.make_async_copy(src, src_out, sems.at[0])
    kept.start()
    source = src[...]
    q = dot(source, w[0]).astype(BF)
    copies[5].wait()
    k = dot(source, w[1]).astype(BF)
    copies[6].wait()
    v = dot(source, w[2]).astype(BF)
    for n in range(src.shape[0] // NT):
        rows = slice(n * NT, (n + 1) * NT)
        out = (first, second)[n // K_NB]
        out_rows = slice(n % K_NB * NT, (n % K_NB + 1) * NT)
        for h in range(width // HEAD_DIM):
            cols = slice(h * HEAD_DIM, (h + 1) * HEAD_DIM)
            s = dot_t(q[rows, cols], k[rows, cols])
            p = jnp.exp2((s - jnp.max(s, axis=-1, keepdims=True)) * EXP2_SCALE)
            total = jnp.sum(p, axis=-1, keepdims=True)
            out[out_rows, cols] = (dot(p.astype(BF), v[rows, cols]) / total).astype(BF)
    kept.wait()


def encode(pieces, wq, wk, wv):
    rows, width = pieces[0].shape
    depth = wq.shape[0]
    return pl.pallas_call(
        encode_kernel,
        out_shape=[sds((rows // 2, width))] * 2 + [pltpu.HBM((rows, depth), BF)],
        in_specs=[ANY] * 7,
        out_specs=[VMEM, VMEM, ANY],
        scratch_shapes=[
            pltpu.VMEM((rows, depth), BF),
            pltpu.VMEM((3, depth, width), BF),
            pltpu.SemaphoreType.DMA((7,)),
        ],
        compiler_params=params(12),
        cost_estimate=cost(30 * 10**9, 1024),
        name="encode",
    )(*pieces, *map(in_hbm, (wq, wk, wv)))


def load_kernel(w0, w_near, w2, w_swapped, wk, wv, tie, wo_out, wk_out, wv_out, sems):
    width = w0.shape[0]
    near = 1 + 2 * (lax.axis_index("seq") % 2)
    pairs = []
    for k, w in ((0, w0), (near, w_near), (2, w2), (4 - near, w_swapped)):
        pairs.append((w, wo_out.at[pl.ds(pl.multiple_of(k * width, width), width)]))
    for c in run_copies(pairs + [(wk, wk_out), (wv, wv_out)], sems):
        c.wait()


def load(wo, wk, wv, tie):
    depth, cols = wk.shape
    return pl.pallas_call(
        load_kernel,
        out_shape=[pltpu.VMEM((depth, depth), BF), pltpu.VMEM((depth, cols), BF), pltpu.VMEM((depth, cols), BF)],
        in_specs=[ANY] * 7,
        out_specs=[ANY] * 3,
        scratch_shapes=[pltpu.SemaphoreType.DMA((6,))],
        compiler_params=params(1),
        cost_estimate=cost(3 * 10**9, 1024),
        name="load",
    )(*map(in_hbm, (*wo, wk, wv)), tie)


def cross_kernel(
    which, counts, src, a0, a1, a2, a3, wo, wk, wv, cq, so,
    out, src_s, attn, sems,
):
    nbrs, width = a0.shape
    pairs = [(src.at[pl.ds(which * nbrs, nbrs)], src_s)]
    pairs += [(a, attn.at[:, pl.ds(k * width, width)]) for k, a in enumerate((a0, a1, a2, a3))]
    copies = run_copies(pairs, sems)
    seq = lax.axis_index("seq")
    count = counts[0, seq * 2 + which]
    shape = (SPAN, nbrs)
    alive = lax.broadcasted_iota(jnp.int32, shape, 1) < count * NT
    if which == 1:
        past = (lax.broadcasted_iota(jnp.int32, shape, 0) > 0) & (seq == lax.axis_size("seq") - 1)
        alive = alive & jnp.logical_not(past)
    for c in copies:
        c.wait()
    encoded = (src_s[...].astype(F32) + dot(attn[...], wo[...])).astype(BF)
    keys = dot(encoded, wk[...]).astype(BF)
    values = dot(encoded, wv[...]).astype(BF)
    rows = slice(which * SPAN, (which + 1) * SPAN)
    for h in range(cq.shape[1] // HEAD_DIM):
        cols = slice(h * HEAD_DIM, (h + 1) * HEAD_DIM)
        s = dot_t(cq[rows, cols], keys[:, cols])
        s = jnp.where(alive, s, NEG_BIG)
        p = jnp.exp2((s - jnp.max(s, axis=-1, keepdims=True)) * EXP2_SCALE)
        p = jnp.where(alive, p, 0.0)
        total = jnp.maximum(jnp.sum(p, axis=-1, keepdims=True), 1.0)
        mix = dot(p.astype(BF), values[:, cols]) / total
        out[:, cols] = (so[rows, cols].astype(F32) + mix).astype(BF)


def cross(which, counts, source, attn, wo, wk, wv, cq, so):
    rows, depth = source.shape
    cols = cq.shape[1]

    def body(*refs):
        cross_kernel(which, *refs)

    return pl.pallas_call(
        body,
        out_shape=sds((SPAN, cols)),
        in_specs=[SMEM] + [ANY] * 5 + [VMEM] * 5,
        out_specs=VMEM,
        scratch_shapes=[
            pltpu.VMEM((rows // 2, depth), BF),
            pltpu.VMEM((rows // 2, depth), BF),
            pltpu.SemaphoreType.DMA((5,)),
        ],
        compiler_params=params(12),
        cost_estimate=cost(5 * 10**9, 1024),
        name="cross",
    )(counts, in_hbm(source), *attn, wo, wk, wv, cq, so)


def pack_kernel(q, k, v, out, rows, sems):
    tok = q.shape[1]
    copies = run_copies([(ref.at[0], rows.at[n]) for n, ref in enumerate((q, k, v))], sems)
    for n, c in enumerate(copies):
        c.wait()
        for head in range(N_Z):
            cols = slice(head * HEAD_DIM, (head + 1) * HEAD_DIM)
            out[head, n * tok : (n + 1) * tok, :] = rows[n, :, cols]


def pack(q, k, v):
    _, tok, cols = q.shape
    return pl.pallas_call(
        pack_kernel,
        out_shape=sds((N_Z, 3 * tok, HEAD_DIM)),
        in_specs=[ANY] * 3,
        out_specs=VMEM,
        scratch_shapes=[pltpu.VMEM((3, tok, cols), BF), pltpu.SemaphoreType.DMA((3,))],
        compiler_params=params(4),
        cost_estimate=cost(1 * 10**9, 1024),
        name="pack",
    )(in_hbm(q), in_hbm(k), in_hbm(v))


def attend_kernel(own, other, out):
    core = lax.axis_index("seq") % 2
    tok = out.shape[1]
    tokens = 2 * N_Z * tok
    for z in range(N_Z):
        after = (z + 1) % N_Z
        nxt = jnp.where(core == 0, other[z, :SPAN].astype(F32), other[after, :SPAN].astype(F32))
        both = jnp.concatenate([own[z, :tok].astype(F32), nxt], axis=0)
        rolled = pltpu.roll(both, both.shape[0] - (SPAN - 1), 0)[:tok].astype(BF)
        block = 2 * z + core
        pos = block * tok + SPAN - 1 + lax.broadcasted_iota(jnp.int32, (tok, 1), 0)
        pos = jnp.where(pos >= tokens, pos - tokens, pos)
        col = lax.broadcasted_iota(jnp.int32, (1, tok), 1)
        parts, values = [], []
        for n, ref, parity in ((z + 1, own, core), (min(z + 2, N_Z), other, 1 - core)):
            s = dot_t(rolled, ref[:n, tok : 2 * tok].reshape(n * tok, HEAD_DIM))
            values.append(ref[:n, 2 * tok :].reshape(n * tok, HEAD_DIM))
            for b in range(n):
                piece = s[:, b * tok : (b + 1) * tok]
                if b >= z or z == N_Z - 1:
                    piece = jnp.where((2 * b + parity) * tok + col <= pos, piece, NEG_BIG)
                parts.append(piece)
        s = jnp.concatenate(parts, axis=1)
        p = jnp.exp2((s - jnp.max(s, axis=-1, keepdims=True)) * EXP2_SCALE)
        norm = jnp.sum(p, axis=-1, keepdims=True)
        p = p.astype(BF)
        split = values[0].shape[0]
        mix = dot(p[:, :split], values[0]) + dot(p[:, split:], values[1])
        out[z] = (mix / norm).astype(BF)


def attend(own, other):
    tok = own.shape[1] // 3
    total = N_Z * tok
    return pl.pallas_call(
        attend_kernel,
        out_shape=sds((N_Z, tok, HEAD_DIM)),
        in_specs=[VMEM] * 2,
        out_specs=VMEM,
        compiler_params=params(12),
        cost_estimate=cost(10 * 10**9, 1024),
        name="attend",
    )(own, other)


def query_kernel(heads, wq, so, cq):
    for h in range(N_Z):
        cols = slice(h * HEAD_DIM, (h + 1) * HEAD_DIM)
        so[:, cols] = heads[h]
        cq[:, cols] = dot(heads[h], wq[h]).astype(BF)


def cross_queries(heads, wq):
    tok = heads.shape[1]
    cols = N_Z * HEAD_DIM
    return pl.pallas_call(
        query_kernel,
        out_shape=[sds((tok, cols))] * 2,
        in_specs=[VMEM] * 2,
        out_specs=[VMEM] * 2,
        compiler_params=params(4),
        cost_estimate=cost(1 * 10**9, 1024),
        name="cross_queries",
    )(heads, wq)


def place_kernel(received, first, second, out):
    rows = jnp.concatenate([received[...], first[...], second[...]], axis=0).astype(F32)
    out[0] = pltpu.roll(rows, rows.shape[0] - 1, 0)[: out.shape[1]].astype(BF)


def place(received, first, second):
    cols = first.shape[1]
    return pl.pallas_call(
        place_kernel,
        out_shape=sds((1, 2 * SPAN, cols)),
        in_specs=[VMEM] * 3,
        out_specs=VMEM,
        compiler_params=params(4),
        cost_estimate=cost(1 * 10**9, 1024),
        name="place",
    )(received, first, second)


def per_device(
    queries, keys_in, values_in, memory, enc_wq, enc_wk, enc_wv, enc_wo,
    cross_wk, cross_wv, cross_wq, nbr_rows, nbr_owner, nbr_count,
):
    idx = (nbr_owner * DB + nbr_rows).reshape(-1)
    asked = [idx] + [shifted(idx, "enc", k) for k in range(1, N_ENC)]
    near, far = to_sides(enc_wo), shifted(enc_wo, "mp", 2)

    packed = over_z(pack(queries, keys_in, values_in))
    sent = fetch(asked, memory)
    received = [sent[0]] + [shifted(sent[k], "enc", -k) for k in range(1, N_ENC)]
    mine = compact(idx, received, (near, far))
    pieces = [mine] + [shifted(mine, "mp", k) for k in range(1, N_MP)]

    packed = after(packed, pieces[1], pieces[3])
    heads = over_z(attend(packed, core_swap(packed)))
    so, cq = cross_queries(heads, cross_wq)

    *values, source = encode(pieces, enc_wq, enc_wk, enc_wv)
    attn = [[v] + [shifted(v, "mp", k) for k in range(1, N_MP)] for v in values]
    wo, wk, wv = load((enc_wo, near, far, core_swap(near)), cross_wk, cross_wv, cq)
    second = cross(1, nbr_count, source, attn[0], wo, wk, wv, cq, so)
    passed = shifted(second, "seq", 1)
    first = cross(0, nbr_count, source, attn[1], wo, wk, wv, cq, so)
    return place(passed, first, second)


def solution(mesh):
    return jax.shard_map(
        per_device,
        mesh=mesh,
        in_specs=(
            P("enc", "seq", "mp"),
            P("enc", "seq", "mp"),
            P("enc", "seq", "mp"),
            P("enc", None, "mp"),
            P(None, "mp"),
            P(None, "mp"),
            P(None, "mp"),
            P("mp", None),
            P(None, "mp"),
            P(None, "mp"),
            P("mp", None, None),
            P("enc", "seq", None),
            P("enc", "seq", None),
            P("enc", None),
        ),
        out_specs=P("enc", "seq", "mp"),
        check_vma=False,
    )
```

profile of v0, /device:TPU:1, one launch (start us, length us, event | category | flops | bytes accessed | tf_op | source)
XLA Modules:
  0.0 90.5 jit_solution(12462839959796318746)
XLA Ops:
  0.8 2.1 %collective-permute-start = (s32[4]{0:T(128)S(1)}, s32[4]{0:T(128)S(1)}, u32[]{:S(2)}, u32[]{:S(2)}) collective-permute-start(s32[4]{0:T(128)S(1)} %reshape.3.idx0.idx), channel_id=1, source_target_pairs={{0,64},{64,128},{128,192},{192,0},{1,65},{65,129},{129,193},{193,1... | collective-permute-start | bytes 56 | tf_op jit(solution)/shard_map/ppermute | solution.py:32
  2.9 2.6 %collective-permute-start.1 = (s32[4]{0:T(128)S(1)}, s32[4]{0:T(128)S(1)}, u32[]{:S(2)}, u32[]{:S(2)}) collective-permute-start(s32[4]{0:T(128)S(1)} %reshape.3.idx0.idx), channel_id=1, source_target_pairs={{0,128},{64,192},{128,0},{192,64},{1,129},{65,193},{129,1},{193,65... | collective-permute-start | bytes 56 | tf_op jit(solution)/shard_map/ppermute | solution.py:32
  5.5 1.1 %collective-permute-start.2 = (s32[4]{0:T(128)S(1)}, s32[4]{0:T(128)S(1)}, u32[]{:S(2)}, u32[]{:S(2)}) collective-permute-start(s32[4]{0:T(128)S(1)} %reshape.3.idx0.idx), channel_id=1, source_target_pairs={{0,192},{64,0},{128,64},{192,128},{1,193},{65,1},{129,65},{193,129... | collective-permute-start | bytes 56 | tf_op jit(solution)/shard_map/ppermute | solution.py:32
  6.6 2.5 %collective-permute-start.6 = (bf16[256,1024]{1,0:T(8,128)(2,1)}, bf16[256,1024]{1,0:T(8,128)(2,1)S(1)}, u32[]{:S(2)}, u32[]{:S(2)}) collective-permute-start(bf16[256,1024]{1,0:T(8,128)(2,1)} %w0.1), channel_id=1, source_target_pairs={{0,1},{1,2},{2,3},{3,0},{4,7},{5,4},{6,5},{7,6},{8,9},{9,10},{10,1... | collective-permute-start | bytes 1572872 | tf_op jit(solution)/shard_map/ppermute | solution.py:42
  9.6 2.1 %pack.1 = bf16[8,384,128]{2,1,0:T(8,128)(2,1)} custom-call(bf16[1,128,1024]{2,1,0:T(8,128)(2,1)} %q.1, bf16[1,128,1024]{2,1,0:T(8,128)(2,1)} %k.1, bf16[1,128,1024]{2,1,0:T(8,128)(2,1)} %v.1), custom_call_target="tpu_custom_call" | custom-call | flops 1000000000 | bytes 1024 | tf_op jit(solution)/shard_map/pack/pallas_call | solution.py:310
  11.7 8.2 %all-to-all-start = ((bf16[8,384,128]{2,1,0:T(8,128)(2,1)}), bf16[8,384,128]{2,1,0:T(8,128)(2,1)S(1)}, u32[]{:S(2)}, u32[]{:S(2)}) async-start(bf16[8,384,128]{2,1,0:T(8,128)(2,1)} %pack.1), calls=%async_computation | async-start | bytes 1572864 | tf_op jit(solution)/shard_map/all_to_all | solution.py:52
  19.9 1.7 %fetch.1 = (bf16[256,256]{1,0:T(8,128)(2,1)S(1)}, bf16[256,256]{1,0:T(8,128)(2,1)S(1)}, bf16[256,256]{1,0:T(8,128)(2,1)S(1)}, bf16[256,256]{1,0:T(8,128)(2,1)S(1)}) custom-call(s32[4]{0:T(128)S(1)} %reshape.3.idx0.idx, s32[4]{0:T(128)S(1)} %collective-permute-done.idx1, s32[4]{0:T(128)S(1)} %collective-permute-done.1.idx2, ...), custom_call_target="tpu_custom_call" | custom-call | flops 20000000000 | bytes 1024 | tf_op jit(solution)/shard_map/fetch/pallas_call | solution.py:118
  21.8 2.1 %collective-permute-start.4 = (bf16[256,256]{1,0:T(8,128)(2,1)S(1)}, bf16[256,256]{1,0:T(8,128)(2,1)S(1)}, u32[]{:S(2)}, u32[]{:S(2)}) collective-permute-start(bf16[256,256]{1,0:T(8,128)(2,1)S(1)} %get-tuple-element.19), channel_id=1, source_target_pairs={{0,128},{64,192},{128,0},{192,64},{1,129},{65,193},{129,1},{193,65... | collective-permute-start | bytes 393224 | tf_op jit(solution)/shard_map/ppermute | solution.py:32
  23.9 1.9 %collective-permute-done.3.r1 = bf16[256,256]{1,0:T(8,128)(2,1)S(1)} collective-permute-done((bf16[256,256]{1,0:T(8,128)(2,1)S(1)}, bf16[256,256]{1,0:T(8,128)(2,1)S(1)}, u32[]{:S(2)}, u32[]{:S(2)}) %collective-permute-start.3) | collective-permute-done | bytes 131104 | tf_op jit(solution)/shard_map/ppermute | solution.py:32
  25.8 1.6 %collective-permute-done.4.r2 = bf16[256,256]{1,0:T(8,128)(2,1)S(1)} collective-permute-done((bf16[256,256]{1,0:T(8,128)(2,1)S(1)}, bf16[256,256]{1,0:T(8,128)(2,1)S(1)}, u32[]{:S(2)}, u32[]{:S(2)}) %collective-permute-start.4) | collective-permute-done | bytes 131104 | tf_op jit(solution)/shard_map/ppermute | solution.py:32
  27.4 1.8 %collective-permute-done.5.r3 = bf16[256,256]{1,0:T(8,128)(2,1)S(1)} collective-permute-done((bf16[256,256]{1,0:T(8,128)(2,1)S(1)}, bf16[256,256]{1,0:T(8,128)(2,1)S(1)}, u32[]{:S(2)}, u32[]{:S(2)}) %collective-permute-start.5) | collective-permute-done | bytes 131104 | tf_op jit(solution)/shard_map/ppermute | solution.py:32
  29.3 1.3 %compact.1.x0 = bf16[512,256]{1,0:T(8,128)(2,1)} custom-call(s32[4]{0:T(128)S(1)} %reshape.3.idx0.idx, bf16[256,256]{1,0:T(8,128)(2,1)S(1)} %get-tuple-element.17.r0, bf16[256,256]{1,0:T(8,128)(2,1)S(1)} %collective-permute-done.3.r1, bf16[256,256]{1,0:T(8,128)(2,1)S(1)} %collective-permute-done.4.r2, bf16[256,256]{1,0:T(8,128)(2,1)S(1)} %collective-permute-done.5.r3, ...), custom_call_target="tpu_custom_call" | custom-call | flops 1000000000 | bytes 1024 | tf_op jit(solution)/shard_map/compact/pallas_call | solution.py:155
  31.2 0.9 collective-permute-start.8
  32.1 4.3 %collective-permute-done.10.x3.refs_2_ = bf16[512,256]{1,0:T(8,128)(2,1)S(1)} collective-permute-done((bf16[512,256]{1,0:T(8,128)(2,1)}, bf16[512,256]{1,0:T(8,128)(2,1)S(1)}, u32[]{:S(2)}, u32[]{:S(2)}) %collective-permute-start.10) | collective-permute-done | bytes 262176 | tf_op jit(solution)/shard_map/ppermute | solution.py:32
  36.4 2.6 %collective-permute-done.8.x1.refs_1_ = bf16[512,256]{1,0:T(8,128)(2,1)S(1)} collective-permute-done((bf16[512,256]{1,0:T(8,128)(2,1)}, bf16[512,256]{1,0:T(8,128)(2,1)S(1)}, u32[]{:S(2)}, u32[]{:S(2)}) %collective-permute-start.8) | collective-permute-done | bytes 262176 | tf_op jit(solution)/shard_map/ppermute | solution.py:32
  39.0 1.6 %all-to-all-done.refs_0_ = bf16[8,384,128]{2,1,0:T(8,128)(2,1)S(1)} async-done(((bf16[8,384,128]{2,1,0:T(8,128)(2,1)}), bf16[8,384,128]{2,1,0:T(8,128)(2,1)S(1)}, u32[]{:S(2)}, u32[]{:S(2)}) %all-to-all-start) | async-done | bytes 786464 | tf_op jit(solution)/shard_map/all_to_all | solution.py:52
  40.6 3.7 %collective-permute-start.15 = (bf16[8,384,128]{2,1,0:T(8,128)(2,1)S(1)}, bf16[8,384,128]{2,1,0:T(8,128)(2,1)S(1)}, u32[]{:S(2)}, u32[]{:S(2)}) collective-permute-start(bf16[8,384,128]{2,1,0:T(8,128)(2,1)S(1)} %after.1.own), channel_id=1, source_target_pairs={{0,4},{4,0},{8,12},{12,8},{16,20},{20,16},{24,28},{28,24},{32,36},... | collective-permute-start | bytes 2359304 | tf_op jit(solution)/shard_map/ppermute | solution.py:47
  44.3 2.1 %collective-permute-start.9 = (bf16[512,256]{1,0:T(8,128)(2,1)S(1)}, bf16[512,256]{1,0:T(8,128)(2,1)S(1)}, u32[]{:S(2)}, u32[]{:S(2)}) collective-permute-start(bf16[512,256]{1,0:T(8,128)(2,1)S(1)} %copy-done.3), channel_id=1, source_target_pairs={{0,2},{1,3},{2,0},{3,1},{4,6},{5,7},{6,4},{7,5},{8,10},{9,11},{10,... | collective-permute-start | bytes 786440 | tf_op jit(solution)/shard_map/ppermute | solution.py:32
  46.8 4.2 %attend.1 = bf16[8,128,128]{2,1,0:T(8,128)(2,1)} custom-call(bf16[8,384,128]{2,1,0:T(8,128)(2,1)S(1)} %after.1.own, bf16[8,384,128]{2,1,0:T(8,128)(2,1)S(1)} %collective-permute-done.15.other), custom_call_target="tpu_custom_call" | custom-call | flops 10000000000 | bytes 1024 | tf_op jit(solution)/shard_map/attend/pallas_call | solution.py:356
  51.0 6.6 %all-to-all-start.1 = ((bf16[8,128,128]{2,1,0:T(8,128)(2,1)}), bf16[8,128,128]{2,1,0:T(8,128)(2,1)S(1)}, u32[]{:S(2)}, u32[]{:S(2)}) async-start(bf16[8,128,128]{2,1,0:T(8,128)(2,1)} %attend.1), calls=%async_computation.1 | async-start | bytes 524288 | tf_op jit(solution)/shard_map/all_to_all | solution.py:52
  57.5 5.0 %encode.1 = (bf16[256,256]{1,0:T(8,128)(2,1)S(1)}, bf16[256,256]{1,0:T(8,128)(2,1)S(1)}, bf16[512,1024]{1,0:T(8,128)(2,1)}) custom-call(bf16[512,256]{1,0:T(8,128)(2,1)S(1)} %copy-done.3, bf16[512,256]{1,0:T(8,128)(2,1)S(1)} %collective-permute-done.8.x1.refs_1_, bf16[512,256]{1,0:T(8,128)(2,1)S(1)} %collective-permute-done.9.x2, ...), custom_call_target="tpu_custom_call" | custom-call | flops 30000001024 | bytes 1024 | tf_op jit(solution)/shard_map/encode/pallas_call | solution.py:203
  62.6 1.5 %collective-permute-start.18 = (bf16[256,256]{1,0:T(8,128)(2,1)S(1)}, bf16[256,256]{1,0:T(8,128)(2,1)S(1)}, u32[]{:S(2)}, u32[]{:S(2)}) collective-permute-start(bf16[256,256]{1,0:T(8,128)(2,1)S(1)} %get-tuple-element.28.refs_2_), channel_id=1, source_target_pairs={{0,2},{1,3},{2,0},{3,1},{4,6},{5,7},{6,4},{7,5},{8,10},{9,11},{10,... | collective-permute-start | bytes 393224 | tf_op jit(solution)/shard_map/ppermute | solution.py:32
  64.1 1.7 %collective-permute-start.11 = (bf16[256,256]{1,0:T(8,128)(2,1)S(1)}, bf16[256,256]{1,0:T(8,128)(2,1)S(1)}, u32[]{:S(2)}, u32[]{:S(2)}) collective-permute-start(bf16[256,256]{1,0:T(8,128)(2,1)S(1)} %get-tuple-element.22.refs_2_), channel_id=1, source_target_pairs={{0,1},{1,2},{2,3},{3,0},{4,5},{5,6},{6,7},{7,4},{8,9},{9,10},{10,1... | collective-permute-start | bytes 393224 | tf_op jit(solution)/shard_map/ppermute | solution.py:32
  65.8 1.5 %collective-permute-start.12 = (bf16[256,256]{1,0:T(8,128)(2,1)S(1)}, bf16[256,256]{1,0:T(8,128)(2,1)S(1)}, u32[]{:S(2)}, u32[]{:S(2)}) collective-permute-start(bf16[256,256]{1,0:T(8,128)(2,1)S(1)} %get-tuple-element.22.refs_2_), channel_id=1, source_target_pairs={{0,2},{1,3},{2,0},{3,1},{4,6},{5,7},{6,4},{7,5},{8,10},{9,11},{10,... | collective-permute-start | bytes 393224 | tf_op jit(solution)/shard_map/ppermute | solution.py:32
  67.3 1.3 %all-to-all-done.1.heads = bf16[8,128,128]{2,1,0:T(8,128)(2,1)S(1)} async-done(((bf16[8,128,128]{2,1,0:T(8,128)(2,1)}), bf16[8,128,128]{2,1,0:T(8,128)(2,1)S(1)}, u32[]{:S(2)}, u32[]{:S(2)}) %all-to-all-start.1) | async-done | bytes 262176 | tf_op jit(solution)/shard_map/all_to_all | solution.py:52
  68.9 1.2 %collective-permute-start.13 = (bf16[256,256]{1,0:T(8,128)(2,1)S(1)}, bf16[256,256]{1,0:T(8,128)(2,1)S(1)}, u32[]{:S(2)}, u32[]{:S(2)}) collective-permute-start(bf16[256,256]{1,0:T(8,128)(2,1)S(1)} %get-tuple-element.22.refs_2_), channel_id=1, source_target_pairs={{0,3},{1,0},{2,1},{3,2},{4,7},{5,4},{6,5},{7,6},{8,11},{9,8},{10,9... | collective-permute-start | bytes 393224 | tf_op jit(solution)/shard_map/ppermute | solution.py:32
  70.1 2.9 %load.1 = (bf16[1024,1024]{1,0:T(8,128)(2,1)S(1)}, bf16[1024,1024]{1,0:T(8,128)(2,1)S(1)}, bf16[1024,1024]{1,0:T(8,128)(2,1)S(1)}) custom-call(bf16[256,1024]{1,0:T(8,128)(2,1)} %w0.1, bf16[256,1024]{1,0:T(8,128)(2,1)} %copy-done, bf16[256,1024]{1,0:T(8,128)(2,1)} %copy-done.1, bf16[256,1024]{1,0:T(8,128)(2,1)} %copy-done.5, bf16[1024,1024]{1,0:T(8,128)(2,1)} %wk.3, ...), custom_call_target="tpu_custom_call" | custom-call | flops 3000000000 | bytes 1024 | tf_op jit(solution)/shard_map/load/pallas_call | solution.py:231
  73.0 3.7 %collective-permute-done.11.refs_3_ = bf16[256,256]{1,0:T(8,128)(2,1)S(1)} collective-permute-done((bf16[256,256]{1,0:T(8,128)(2,1)S(1)}, bf16[256,256]{1,0:T(8,128)(2,1)S(1)}, u32[]{:S(2)}, u32[]{:S(2)}) %collective-permute-start.11) | collective-permute-done | bytes 131104 | tf_op jit(solution)/shard_map/ppermute | solution.py:32
  76.7 5.1 %cross.2.second = bf16[64,1024]{1,0:T(8,128)(2,1)S(1)} custom-call(s32[1,32]{1,0:T(1,128)S(1)} %copy-done.4, bf16[512,1024]{1,0:T(8,128)(2,1)} %get-tuple-element.21.refs_1_, bf16[256,256]{1,0:T(8,128)(2,1)S(1)} %get-tuple-element.22.refs_2_, bf16[256,256]{1,0:T(8,128)(2,1)S(1)} %collective-permute-done.11.refs_3_, ...), custom_call_target="tpu_custom_call" | custom-call | flops 5000000000 | bytes 1024 | tf_op jit(solution)/shard_map/cross/pallas_call | solution.py:282
  81.8 2.8 %collective-permute-start.16 = (bf16[64,1024]{1,0:T(8,128)(2,1)S(1)}, bf16[64,1024]{1,0:T(8,128)(2,1)S(1)}, u32[]{:S(2)}, u32[]{:S(2)}) collective-permute-start(bf16[64,1024]{1,0:T(8,128)(2,1)S(1)} %cross.2.second), channel_id=1, source_target_pairs={{0,4},{4,8},{8,12},{12,16},{16,20},{20,24},{24,28},{28,32},{32,36}... | collective-permute-start | bytes 393224 | tf_op jit(solution)/shard_map/ppermute | solution.py:32
  84.6 5.1 %cross.3.first = bf16[64,1024]{1,0:T(8,128)(2,1)S(1)} custom-call(s32[1,32]{1,0:T(1,128)S(1)} %copy-done.4, bf16[512,1024]{1,0:T(8,128)(2,1)} %get-tuple-element.21.refs_1_, bf16[256,256]{1,0:T(8,128)(2,1)S(1)} %get-tuple-element.28.refs_2_, bf16[256,256]{1,0:T(8,128)(2,1)S(1)} %collective-permute-done.17.refs_3_, ...), custom_call_target="tpu_custom_call" | custom-call | flops 5000000000 | bytes 1024 | tf_op jit(solution)/shard_map/cross/pallas_call | solution.py:282
  89.8 0.8 place.1
  (37 shorter events, 2.9 us)
Async XLA Ops:
  0.8 19.1 %collective-permute-start = (s32[4]{0:T(128)S(1)}, s32[4]{0:T(128)S(1)}, u32[]{:S(2)}, u32[]{:S(2)}) collective-permute-start(s32[4]{0:T(128)S(1)} %reshape.3.idx0.idx), channel_id=1, source_target_pairs={{0,64},{64,128},{128,192},{192,0},{1,65},{65,129},{129,193},{193,1... | collective-permute-start | bytes 56 | tf_op jit(solution)/shard_map/ppermute | solution.py:32
  2.9 17.0 %collective-permute-start.1 = (s32[4]{0:T(128)S(1)}, s32[4]{0:T(128)S(1)}, u32[]{:S(2)}, u32[]{:S(2)}) collective-permute-start(s32[4]{0:T(128)S(1)} %reshape.3.idx0.idx), channel_id=1, source_target_pairs={{0,128},{64,192},{128,0},{192,64},{1,129},{65,193},{129,1},{193,65... | collective-permute-start | bytes 56 | tf_op jit(solution)/shard_map/ppermute | solution.py:32
  5.5 14.4 %collective-permute-start.2 = (s32[4]{0:T(128)S(1)}, s32[4]{0:T(128)S(1)}, u32[]{:S(2)}, u32[]{:S(2)}) collective-permute-start(s32[4]{0:T(128)S(1)} %reshape.3.idx0.idx), channel_id=1, source_target_pairs={{0,192},{64,0},{128,64},{192,128},{1,193},{65,1},{129,65},{193,129... | collective-permute-start | bytes 56 | tf_op jit(solution)/shard_map/ppermute | solution.py:32
  6.6 22.6 %collective-permute-start.6 = (bf16[256,1024]{1,0:T(8,128)(2,1)}, bf16[256,1024]{1,0:T(8,128)(2,1)S(1)}, u32[]{:S(2)}, u32[]{:S(2)}) collective-permute-start(bf16[256,1024]{1,0:T(8,128)(2,1)} %w0.1), channel_id=1, source_target_pairs={{0,1},{1,2},{2,3},{3,0},{4,7},{5,4},{6,5},{7,6},{8,9},{9,10},{10,1... | collective-permute-start | bytes 1572872 | tf_op jit(solution)/shard_map/ppermute | solution.py:42
  9.1 20.2 %collective-permute-start.7 = (bf16[256,1024]{1,0:T(8,128)(2,1)}, bf16[256,1024]{1,0:T(8,128)(2,1)S(1)}, u32[]{:S(2)}, u32[]{:S(2)}) collective-permute-start(bf16[256,1024]{1,0:T(8,128)(2,1)} %w0.1), channel_id=1, source_target_pairs={{0,2},{1,3},{2,0},{3,1},{4,6},{5,7},{6,4},{7,5},{8,10},{9,11},{10,... | collective-permute-start | bytes 1572872 | tf_op jit(solution)/shard_map/ppermute | solution.py:32
  11.7 28.9 %all-to-all-start = ((bf16[8,384,128]{2,1,0:T(8,128)(2,1)}), bf16[8,384,128]{2,1,0:T(8,128)(2,1)S(1)}, u32[]{:S(2)}, u32[]{:S(2)}) async-start(bf16[8,384,128]{2,1,0:T(8,128)(2,1)} %pack.1), calls=%async_computation | async-start | bytes 1572864 | tf_op jit(solution)/shard_map/all_to_all | solution.py:52
  21.7 4.2 %collective-permute-start.3 = (bf16[256,256]{1,0:T(8,128)(2,1)S(1)}, bf16[256,256]{1,0:T(8,128)(2,1)S(1)}, u32[]{:S(2)}, u32[]{:S(2)}) collective-permute-start(bf16[256,256]{1,0:T(8,128)(2,1)S(1)} %get-tuple-element.18), channel_id=1, source_target_pairs={{0,192},{64,0},{128,64},{192,128},{1,193},{65,1},{129,65},{193,129... | collective-permute-start | bytes 393224 | tf_op jit(solution)/shard_map/ppermute | solution.py:32
  21.8 5.6 %collective-permute-start.4 = (bf16[256,256]{1,0:T(8,128)(2,1)S(1)}, bf16[256,256]{1,0:T(8,128)(2,1)S(1)}, u32[]{:S(2)}, u32[]{:S(2)}) collective-permute-start(bf16[256,256]{1,0:T(8,128)(2,1)S(1)} %get-tuple-element.19), channel_id=1, source_target_pairs={{0,128},{64,192},{128,0},{192,64},{1,129},{65,193},{129,1},{193,65... | collective-permute-start | bytes 393224 | tf_op jit(solution)/shard_map/ppermute | solution.py:32
  23.9 5.3 %collective-permute-start.5 = (bf16[256,256]{1,0:T(8,128)(2,1)S(1)}, bf16[256,256]{1,0:T(8,128)(2,1)S(1)}, u32[]{:S(2)}, u32[]{:S(2)}) collective-permute-start(bf16[256,256]{1,0:T(8,128)(2,1)S(1)} %get-tuple-element.20), channel_id=1, source_target_pairs={{0,64},{64,128},{128,192},{192,0},{1,65},{65,129},{129,193},{193,1... | collective-permute-start | bytes 393224 | tf_op jit(solution)/shard_map/ppermute | solution.py:32
  29.2 17.2 %copy-start = (bf16[256,1024]{1,0:T(8,128)(2,1)}, bf16[256,1024]{1,0:T(8,128)(2,1)S(1)}, u32[]{:S(2)}) copy-start(bf16[256,1024]{1,0:T(8,128)(2,1)S(1)} %collective-permute-done.6.w1.w_near) | copy-start | bytes 1572868
  29.3 11.3 %copy-start.1 = (bf16[256,1024]{1,0:T(8,128)(2,1)}, bf16[256,1024]{1,0:T(8,128)(2,1)S(1)}, u32[]{:S(2)}) copy-start(bf16[256,1024]{1,0:T(8,128)(2,1)S(1)} %collective-permute-done.7.w2) | copy-start | bytes 1572868
  30.6 13.8 %copy-start.3 = (bf16[512,256]{1,0:T(8,128)(2,1)S(1)}, bf16[512,256]{1,0:T(8,128)(2,1)}, u32[]{:S(2)}) copy-start(bf16[512,256]{1,0:T(8,128)(2,1)} %compact.1.x0) | copy-start | bytes 786436
  30.6 5.8 %collective-permute-start.10 = (bf16[512,256]{1,0:T(8,128)(2,1)}, bf16[512,256]{1,0:T(8,128)(2,1)S(1)}, u32[]{:S(2)}, u32[]{:S(2)}) collective-permute-start(bf16[512,256]{1,0:T(8,128)(2,1)} %compact.1.x0), channel_id=1, source_target_pairs={{0,3},{1,0},{2,1},{3,2},{4,7},{5,4},{6,5},{7,6},{8,11},{9,8},{10,9... | collective-permute-start | bytes 786440 | tf_op jit(solution)/shard_map/ppermute | solution.py:32
  31.2 7.8 %collective-permute-start.8 = (bf16[512,256]{1,0:T(8,128)(2,1)}, bf16[512,256]{1,0:T(8,128)(2,1)S(1)}, u32[]{:S(2)}, u32[]{:S(2)}) collective-permute-start(bf16[512,256]{1,0:T(8,128)(2,1)} %compact.1.x0), channel_id=1, source_target_pairs={{0,1},{1,2},{2,3},{3,0},{4,5},{5,6},{6,7},{7,4},{8,9},{9,10},{10,1... | collective-permute-start | bytes 786440 | tf_op jit(solution)/shard_map/ppermute | solution.py:32
  40.6 6.2 %collective-permute-start.15 = (bf16[8,384,128]{2,1,0:T(8,128)(2,1)S(1)}, bf16[8,384,128]{2,1,0:T(8,128)(2,1)S(1)}, u32[]{:S(2)}, u32[]{:S(2)}) collective-permute-start(bf16[8,384,128]{2,1,0:T(8,128)(2,1)S(1)} %after.1.own), channel_id=1, source_target_pairs={{0,4},{4,0},{8,12},{12,8},{16,20},{20,16},{24,28},{28,24},{32,36},... | collective-permute-start | bytes 2359304 | tf_op jit(solution)/shard_map/ppermute | solution.py:47
  44.3 13.2 %collective-permute-start.9 = (bf16[512,256]{1,0:T(8,128)(2,1)S(1)}, bf16[512,256]{1,0:T(8,128)(2,1)S(1)}, u32[]{:S(2)}, u32[]{:S(2)}) collective-permute-start(bf16[512,256]{1,0:T(8,128)(2,1)S(1)} %copy-done.3), channel_id=1, source_target_pairs={{0,2},{1,3},{2,0},{3,1},{4,6},{5,7},{6,4},{7,5},{8,10},{9,11},{10,... | collective-permute-start | bytes 786440 | tf_op jit(solution)/shard_map/ppermute | solution.py:32
  46.4 22.4 %collective-permute-start.14 = (bf16[256,1024]{1,0:T(8,128)(2,1)S(1)}, bf16[256,1024]{1,0:T(8,128)(2,1)S(1)}, u32[]{:S(2)}, u32[]{:S(2)}) collective-permute-start(bf16[256,1024]{1,0:T(8,128)(2,1)S(1)} %collective-permute-done.6.w1.w_near), channel_id=1, source_target_pairs={{0,4},{4,0},{8,12},{12,8},{16,20},{20,16},{24,28},{28,24},{32,36},... | collective-permute-start | bytes 1572872 | tf_op jit(solution)/shard_map/ppermute | solution.py:47
  51.0 17.6 %all-to-all-start.1 = ((bf16[8,128,128]{2,1,0:T(8,128)(2,1)}), bf16[8,128,128]{2,1,0:T(8,128)(2,1)S(1)}, u32[]{:S(2)}, u32[]{:S(2)}) async-start(bf16[8,128,128]{2,1,0:T(8,128)(2,1)} %attend.1), calls=%async_computation.1 | async-start | bytes 524288 | tf_op jit(solution)/shard_map/all_to_all | solution.py:52
  57.5 11.1 %copy-start.2 = (bf16[8,128,128]{2,1,0:T(8,128)(2,1)S(1)}, bf16[8,128,128]{2,1,0:T(8,128)(2,1)}, u32[]{:S(2)}) copy-start(bf16[8,128,128]{2,1,0:T(8,128)(2,1)} %wq.3) | copy-start | bytes 786436
  62.5 22.1 %collective-permute-start.17 = (bf16[256,256]{1,0:T(8,128)(2,1)S(1)}, bf16[256,256]{1,0:T(8,128)(2,1)S(1)}, u32[]{:S(2)}, u32[]{:S(2)}) collective-permute-start(bf16[256,256]{1,0:T(8,128)(2,1)S(1)} %get-tuple-element.28.refs_2_), channel_id=1, source_target_pairs={{0,1},{1,2},{2,3},{3,0},{4,5},{5,6},{6,7},{7,4},{8,9},{9,10},{10,1... | collective-permute-start | bytes 393224 | tf_op jit(solution)/shard_map/ppermute | solution.py:32
  62.6 22.0 %collective-permute-start.18 = (bf16[256,256]{1,0:T(8,128)(2,1)S(1)}, bf16[256,256]{1,0:T(8,128)(2,1)S(1)}, u32[]{:S(2)}, u32[]{:S(2)}) collective-permute-start(bf16[256,256]{1,0:T(8,128)(2,1)S(1)} %get-tuple-element.28.refs_2_), channel_id=1, source_target_pairs={{0,2},{1,3},{2,0},{3,1},{4,6},{5,7},{6,4},{7,5},{8,10},{9,11},{10,... | collective-permute-start | bytes 393224 | tf_op jit(solution)/shard_map/ppermute | solution.py:32
  64.1 12.5 %collective-permute-start.11 = (bf16[256,256]{1,0:T(8,128)(2,1)S(1)}, bf16[256,256]{1,0:T(8,128)(2,1)S(1)}, u32[]{:S(2)}, u32[]{:S(2)}) collective-permute-start(bf16[256,256]{1,0:T(8,128)(2,1)S(1)} %get-tuple-element.22.refs_2_), channel_id=1, source_target_pairs={{0,1},{1,2},{2,3},{3,0},{4,5},{5,6},{6,7},{7,4},{8,9},{9,10},{10,1... | collective-permute-start | bytes 393224 | tf_op jit(solution)/shard_map/ppermute | solution.py:32
  65.8 10.8 %collective-permute-start.12 = (bf16[256,256]{1,0:T(8,128)(2,1)S(1)}, bf16[256,256]{1,0:T(8,128)(2,1)S(1)}, u32[]{:S(2)}, u32[]{:S(2)}) collective-permute-start(bf16[256,256]{1,0:T(8,128)(2,1)S(1)} %get-tuple-element.22.refs_2_), channel_id=1, source_target_pairs={{0,2},{1,3},{2,0},{3,1},{4,6},{5,7},{6,4},{7,5},{8,10},{9,11},{10,... | collective-permute-start | bytes 393224 | tf_op jit(solution)/shard_map/ppermute | solution.py:32
  68.9 1.2 %copy-start.5 = (bf16[256,1024]{1,0:T(8,128)(2,1)}, bf16[256,1024]{1,0:T(8,128)(2,1)S(1)}, u32[]{:S(2)}) copy-start(bf16[256,1024]{1,0:T(8,128)(2,1)S(1)} %collective-permute-done.14.w_swapped) | copy-start | bytes 1572868
  68.9 7.8 %collective-permute-start.13 = (bf16[256,256]{1,0:T(8,128)(2,1)S(1)}, bf16[256,256]{1,0:T(8,128)(2,1)S(1)}, u32[]{:S(2)}, u32[]{:S(2)}) collective-permute-start(bf16[256,256]{1,0:T(8,128)(2,1)S(1)} %get-tuple-element.22.refs_2_), channel_id=1, source_target_pairs={{0,3},{1,0},{2,1},{3,2},{4,7},{5,4},{6,5},{7,6},{8,11},{9,8},{10,9... | collective-permute-start | bytes 393224 | tf_op jit(solution)/shard_map/ppermute | solution.py:32
  70.1 6.6 %copy-start.4 = (s32[1,32]{1,0:T(1,128)S(1)}, s32[1,32]{1,0:T(1,128)}, u32[]{:S(2)}) copy-start(s32[1,32]{1,0:T(1,128)} %refs_0_.3) | copy-start | bytes 388
  76.7 8.0 %collective-permute-start.19 = (bf16[256,256]{1,0:T(8,128)(2,1)S(1)}, bf16[256,256]{1,0:T(8,128)(2,1)S(1)}, u32[]{:S(2)}, u32[]{:S(2)}) collective-permute-start(bf16[256,256]{1,0:T(8,128)(2,1)S(1)} %get-tuple-element.28.refs_2_), channel_id=1, source_target_pairs={{0,3},{1,0},{2,1},{3,2},{4,7},{5,4},{6,5},{7,6},{8,11},{9,8},{10,9... | collective-permute-start | bytes 393224 | tf_op jit(solution)/shard_map/ppermute | solution.py:32
  81.8 7.9 %collective-permute-start.16 = (bf16[64,1024]{1,0:T(8,128)(2,1)S(1)}, bf16[64,1024]{1,0:T(8,128)(2,1)S(1)}, u32[]{:S(2)}, u32[]{:S(2)}) collective-permute-start(bf16[64,1024]{1,0:T(8,128)(2,1)S(1)} %cross.2.second), channel_id=1, source_target_pairs={{0,4},{4,8},{8,12},{12,16},{16,20},{20,24},{24,28},{28,32},{32,36}... | collective-permute-start | bytes 393224 | tf_op jit(solution)/shard_map/ppermute | solution.py:32
where the time goes:
time: 91 us; the launch traced here: 90.5 us
  starting transfers between devices  42.3 us (46%)
  Pallas kernels  28.4 us (31%)
  waiting for transfers between devices  18.8 us (21%)
    ppermute x17, starting transfers between devices, shifted(): lax.ppermute(block, axis, [(i, (i + distance) % size) for i in range(size)])  21 us
    ppermute x17, waiting for transfers between devices, shifted(): lax.ppermute(block, axis, [(i, (i + distance) % size) for i in range(size)])  15.9 us
    all_to_all x2, starting transfers between devices, over_z(): lax.all_to_all(blocks, 'seq', 0, 0, axis_index_groups=groups, tiled=True)  14.7 us
    pallas_call x2, Pallas kernels, cross(): pl.pallas_call(body, out_shape=sds((SPAN, cols)), in_specs=[SMEM] + [ANY]...  10.2 us
    pallas_call x1, Pallas kernels, encode(): pl.pallas_call(encode_kernel, out_shape=[sds((rows // 2, width))] * 2 + [...  4.96 us
    pallas_call x1, Pallas kernels, attend(): pl.pallas_call(attend_kernel, out_shape=sds((N_Z, tok, HEAD_DIM)), in_spe...  4.18 us
    ppermute x2, starting transfers between devices, core_swap(): return lax.ppermute(block, 'seq', [(i, i ^ 1) for i in range(size)])  4.1 us
    pallas_call x1, Pallas kernels, load(): pl.pallas_call(load_kernel, out_shape=[pltpu.VMEM((depth, depth), BF), pl...  2.94 us
  transfers between devices with their start and end apart: 22, of which 8 were waited for; matrix products, arithmetic and copies ran while one was open for 0% of the time, Pallas kernels for 31%

commit v1 on v0

--- a/solution.py
+++ b/solution.py
@@ -1,3 +1,4 @@
+import functools
 import math
 
 import jax
@@ -122,7 +123,7 @@
         out_specs=[ANY] * 4,
         scratch_shapes=[pltpu.SemaphoreType.DMA((8,))],
         compiler_params=params(1),
-        cost_estimate=cost(20 * 10**9, 1024),
+        cost_estimate=cost(5 * 10**9, 1024),
         name="fetch",
     )(*idx, in_hbm(memory))
 
@@ -169,7 +170,16 @@
     return pl.ds(pl.multiple_of(col * width, width), width)
 
 
-def encode_kernel(x0, x1, x2, x3, wq, wk, wv, second, first, src_out, src, w, sems):
+def attention(blocks):
+    scores = [dot_t(q, k) for q, k, _ in blocks]
+    tops = [jnp.max(s, axis=-1, keepdims=True) for s in scores]
+    weights = [jnp.exp2((s - m) * EXP2_SCALE) for s, m in zip(scores, tops)]
+    mixes = [dot(p.astype(BF), v) for p, (_, _, v) in zip(weights, blocks)]
+    totals = [jnp.sum(p, axis=-1, keepdims=True) for p in weights]
+    return [mix / total for mix, total in zip(mixes, totals)]
+
+
+def encode_kernel(x0, x1, x2, x3, wq, wk, wv, first, second, src_out, src, w, sems):
     width = x0.shape[1]
     pairs = [(x, src.at[:, source_columns(k, width)]) for k, x in enumerate((x0, x1, x2, x3))]
     pairs += [(ref, w.at[n]) for n, ref in enumerate((wq, wk, wv))]
@@ -184,16 +194,16 @@
     k = dot(source, w[1]).astype(BF)
     copies[6].wait()
     v = dot(source, w[2]).astype(BF)
-    for n in range(src.shape[0] // NT):
-        rows = slice(n * NT, (n + 1) * NT)
-        out = (first, second)[n // K_NB]
-        out_rows = slice(n % K_NB * NT, (n % K_NB + 1) * NT)
-        for h in range(width // HEAD_DIM):
-            cols = slice(h * HEAD_DIM, (h + 1) * HEAD_DIM)
-            s = dot_t(q[rows, cols], k[rows, cols])
-            p = jnp.exp2((s - jnp.max(s, axis=-1, keepdims=True)) * EXP2_SCALE)
-            total = jnp.sum(p, axis=-1, keepdims=True)
-            out[out_rows, cols] = (dot(p.astype(BF), v[rows, cols]) / total).astype(BF)
+    places = [
+        (slice(n * NT, (n + 1) * NT), slice(h * HEAD_DIM, (h + 1) * HEAD_DIM))
+        for n in range(src.shape[0] // NT)
+        for h in range(width // HEAD_DIM)
+    ]
+    for at, mix in zip(places, attention([(q[at], k[at], v[at]) for at in places])):
+        rows, cols = at
+        out = (first, second)[rows.start // (K_NB * NT)]
+        begin = rows.start % (K_NB * NT)
+        out[begin : begin + NT, cols] = mix.astype(BF)
     kept.wait()
 
 
@@ -216,38 +226,38 @@
     )(*pieces, *map(in_hbm, (wq, wk, wv)))
 
 
-def load_kernel(w0, w_near, w2, w_swapped, wk, wv, tie, wo_out, wk_out, wv_out, sems):
+def load_kernel(w0, w_near, w_half, s_near, s_half, tie, wo_out, sems):
     width = w0.shape[0]
-    near = 1 + 2 * (lax.axis_index("seq") % 2)
+    half = width // 2
+    core = lax.axis_index("seq") % 2
+    begins = [(w0, 0), (w_near, (1 + 2 * core) * width), (s_near, (3 - 2 * core) * width)]
+    begins += [(w_half, 2 * width + core * half), (s_half, 2 * width + (1 - core) * half)]
     pairs = []
-    for k, w in ((0, w0), (near, w_near), (2, w2), (4 - near, w_swapped)):
-        pairs.append((w, wo_out.at[pl.ds(pl.multiple_of(k * width, width), width)]))
-    for c in run_copies(pairs + [(wk, wk_out), (wv, wv_out)], sems):
-        c.wait()
-
-
-def load(wo, wk, wv, tie):
-    depth, cols = wk.shape
+    for w, begin in begins:
+        rows = w.shape[0]
+        pairs.append((w, wo_out.at[pl.ds(pl.multiple_of(begin, half), rows)]))
+    for c in run_copies(pairs, sems):
+        c.wait()
+
+
+def load(wo, tie):
+    depth = wo[0].shape[1]
     return pl.pallas_call(
         load_kernel,
-        out_shape=[pltpu.VMEM((depth, depth), BF), pltpu.VMEM((depth, cols), BF), pltpu.VMEM((depth, cols), BF)],
-        in_specs=[ANY] * 7,
-        out_specs=[ANY] * 3,
-        scratch_shapes=[pltpu.SemaphoreType.DMA((6,))],
+        out_shape=pltpu.VMEM((depth, depth), BF),
+        in_specs=[ANY] * 6,
+        out_specs=ANY,
+        scratch_shapes=[pltpu.SemaphoreType.DMA((5,))],
         compiler_params=params(1),
         cost_estimate=cost(3 * 10**9, 1024),
         name="load",
-    )(*map(in_hbm, (*wo, wk, wv)), tie)
-
-
-def cross_kernel(
-    which, counts, src, a0, a1, a2, a3, wo, wk, wv, cq, so,
-    out, src_s, attn, sems,
-):
+    )(*map(in_hbm, wo), tie)
+
+
+def cross_kernel(which, counts, src, a0, a1, a2, a3, wo, wk, wv, cq, so, out, src_s, attn, sems):
     nbrs, width = a0.shape
-    pairs = [(src.at[pl.ds(which * nbrs, nbrs)], src_s)]
-    pairs += [(a, attn.at[:, pl.ds(k * width, width)]) for k, a in enumerate((a0, a1, a2, a3))]
-    copies = run_copies(pairs, sems)
+    pairs = [(a, attn.at[:, pl.ds(k * width, width)]) for k, a in enumerate((a0, a1, a2, a3))]
+    copies = run_copies(pairs + [(src.at[pl.ds(which * nbrs, nbrs)], src_s)], sems)
     seq = lax.axis_index("seq")
     count = counts[0, seq * 2 + which]
     shape = (SPAN, nbrs)
@@ -255,21 +265,23 @@
     if which == 1:
         past = (lax.broadcasted_iota(jnp.int32, shape, 0) > 0) & (seq == lax.axis_size("seq") - 1)
         alive = alive & jnp.logical_not(past)
-    for c in copies:
-        c.wait()
-    encoded = (src_s[...].astype(F32) + dot(attn[...], wo[...])).astype(BF)
+    for c in copies[:4]:
+        c.wait()
+    mixed = dot(attn[...], wo[...])
+    copies[4].wait()
+    encoded = (src_s[...].astype(F32) + mixed).astype(BF)
     keys = dot(encoded, wk[...]).astype(BF)
     values = dot(encoded, wv[...]).astype(BF)
     rows = slice(which * SPAN, (which + 1) * SPAN)
-    for h in range(cq.shape[1] // HEAD_DIM):
-        cols = slice(h * HEAD_DIM, (h + 1) * HEAD_DIM)
-        s = dot_t(cq[rows, cols], keys[:, cols])
-        s = jnp.where(alive, s, NEG_BIG)
-        p = jnp.exp2((s - jnp.max(s, axis=-1, keepdims=True)) * EXP2_SCALE)
-        p = jnp.where(alive, p, 0.0)
-        total = jnp.maximum(jnp.sum(p, axis=-1, keepdims=True), 1.0)
-        mix = dot(p.astype(BF), values[:, cols]) / total
-        out[:, cols] = (so[rows, cols].astype(F32) + mix).astype(BF)
+    heads = [slice(h * HEAD_DIM, (h + 1) * HEAD_DIM) for h in range(cq.shape[1] // HEAD_DIM)]
+    scores = [jnp.where(alive, dot_t(cq[rows, c], keys[:, c]), NEG_BIG) for c in heads]
+    tops = [jnp.max(s, axis=-1, keepdims=True) for s in scores]
+    weights = [jnp.exp2((s - m) * EXP2_SCALE) for s, m in zip(scores, tops)]
+    weights = [jnp.where(alive, p, 0.0) for p in weights]
+    mixes = [dot(p.astype(BF), values[:, c]) for p, c in zip(weights, heads)]
+    totals = [jnp.sum(p, axis=-1, keepdims=True) for p in weights]
+    for c, mix, total in zip(heads, mixes, totals):
+        out[:, c] = (so[rows, c].astype(F32) + mix / jnp.maximum(total, 1.0)).astype(BF)
 
 
 def cross(which, counts, source, attn, wo, wk, wv, cq, so):
@@ -295,41 +307,61 @@
     )(counts, in_hbm(source), *attn, wo, wk, wv, cq, so)
 
 
-def pack_kernel(q, k, v, out, rows, sems):
+def pack_kernel(q, k, v, wo, nbr_rows, nbr_owner, out, idx, half, rows, at_row, at_owner, sems):
     tok = q.shape[1]
-    copies = run_copies([(ref.at[0], rows.at[n]) for n, ref in enumerate((q, k, v))], sems)
-    for n, c in enumerate(copies):
+    places = run_copies([(nbr_rows, at_row), (nbr_owner, at_owner)], sems)
+    pairs = [(ref.at[0], rows.at[n]) for n, ref in enumerate((q, k, v))]
+    count = half.shape[0]
+    core = lax.axis_index("seq") % 2
+    pairs.append((wo.at[pl.ds(pl.multiple_of(core * count, count), count)], half))
+    copies = run_copies(pairs, sems.at[pl.ds(2, 4)])
+    for c in places:
+        c.wait()
+    for span in range(2):
+        for j in range(K_NB):
+            idx[span * K_NB + j] = at_owner[0, span, j] * DB + at_row[0, span, j]
+    for n, c in enumerate(copies[:3]):
         c.wait()
         for head in range(N_Z):
             cols = slice(head * HEAD_DIM, (head + 1) * HEAD_DIM)
             out[head, n * tok : (n + 1) * tok, :] = rows[n, :, cols]
-
-
-def pack(q, k, v):
+    copies[3].wait()
+
+
+def pack(q, k, v, wo, nbr_rows, nbr_owner):
     _, tok, cols = q.shape
     return pl.pallas_call(
         pack_kernel,
-        out_shape=sds((N_Z, 3 * tok, HEAD_DIM)),
-        in_specs=[ANY] * 3,
-        out_specs=VMEM,
-        scratch_shapes=[pltpu.VMEM((3, tok, cols), BF), pltpu.SemaphoreType.DMA((3,))],
+        out_shape=[
+            sds((N_Z, 3 * tok, HEAD_DIM)),
+            sds((2 * K_NB,), jnp.int32),
+            sds((wo.shape[0] // 2, wo.shape[1])),
+        ],
+        in_specs=[ANY] * 6,
+        out_specs=[VMEM, SMEM, VMEM],
+        scratch_shapes=[
+            pltpu.VMEM((3, tok, cols), BF),
+            pltpu.SMEM(nbr_rows.shape, jnp.int32),
+            pltpu.SMEM(nbr_owner.shape, jnp.int32),
+            pltpu.SemaphoreType.DMA((6,)),
+        ],
         compiler_params=params(4),
-        cost_estimate=cost(1 * 10**9, 1024),
+        cost_estimate=cost(10**9, 1024),
         name="pack",
-    )(in_hbm(q), in_hbm(k), in_hbm(v))
+    )(*map(in_hbm, (q, k, v, wo, nbr_rows, nbr_owner)))
 
 
 def attend_kernel(own, other, out):
     core = lax.axis_index("seq") % 2
     tok = out.shape[1]
     tokens = 2 * N_Z * tok
-    for z in range(N_Z):
-        after = (z + 1) % N_Z
-        nxt = jnp.where(core == 0, other[z, :SPAN].astype(F32), other[after, :SPAN].astype(F32))
+
+    def block_parts(z):
+        after_z = (z + 1) % N_Z
+        nxt = jnp.where(core == 0, other[z, :SPAN].astype(F32), other[after_z, :SPAN].astype(F32))
         both = jnp.concatenate([own[z, :tok].astype(F32), nxt], axis=0)
         rolled = pltpu.roll(both, both.shape[0] - (SPAN - 1), 0)[:tok].astype(BF)
-        block = 2 * z + core
-        pos = block * tok + SPAN - 1 + lax.broadcasted_iota(jnp.int32, (tok, 1), 0)
+        pos = (2 * z + core) * tok + SPAN - 1 + lax.broadcasted_iota(jnp.int32, (tok, 1), 0)
         pos = jnp.where(pos >= tokens, pos - tokens, pos)
         col = lax.broadcasted_iota(jnp.int32, (1, tok), 1)
         parts, values = [], []
@@ -341,13 +373,20 @@
                 if b >= z or z == N_Z - 1:
                     piece = jnp.where((2 * b + parity) * tok + col <= pos, piece, NEG_BIG)
                 parts.append(piece)
-        s = jnp.concatenate(parts, axis=1)
-        p = jnp.exp2((s - jnp.max(s, axis=-1, keepdims=True)) * EXP2_SCALE)
-        norm = jnp.sum(p, axis=-1, keepdims=True)
-        p = p.astype(BF)
-        split = values[0].shape[0]
-        mix = dot(p[:, :split], values[0]) + dot(p[:, split:], values[1])
-        out[z] = (mix / norm).astype(BF)
+        return parts, values
+
+    for group in ((0, 7, 3, 4), (1, 6, 2, 5)):
+        made = [block_parts(z) for z in group]
+        tops = [jnp.max(functools.reduce(jnp.maximum, parts), axis=-1, keepdims=True) for parts, _ in made]
+        weights = [[jnp.exp2((s - m) * EXP2_SCALE) for s in parts] for (parts, _), m in zip(made, tops)]
+        totals = [jnp.sum(functools.reduce(jnp.add, ps), axis=-1, keepdims=True) for ps in weights]
+        mixes = []
+        for ps, (_, (mine, theirs)) in zip(weights, made):
+            p = jnp.concatenate([part.astype(BF) for part in ps], axis=1)
+            split = mine.shape[0]
+            mixes.append(dot(p[:, :split], mine) + dot(p[:, split:], theirs))
+        for z, mix, total in zip(group, mixes, totals):
+            out[z] = (mix / total).astype(BF)
 
 
 def attend(own, other):
@@ -407,26 +446,28 @@
     queries, keys_in, values_in, memory, enc_wq, enc_wk, enc_wv, enc_wo,
     cross_wk, cross_wv, cross_wq, nbr_rows, nbr_owner, nbr_count,
 ):
-    idx = (nbr_owner * DB + nbr_rows).reshape(-1)
+    packed, idx, wo_half = pack(queries, keys_in, values_in, enc_wo, nbr_rows, nbr_owner)
+    packed = over_z(packed)
     asked = [idx] + [shifted(idx, "enc", k) for k in range(1, N_ENC)]
-    near, far = to_sides(enc_wo), shifted(enc_wo, "mp", 2)
-
-    packed = over_z(pack(queries, keys_in, values_in))
+    near, far = to_sides(enc_wo), shifted(wo_half, "mp", 2)
+
     sent = fetch(asked, memory)
     received = [sent[0]] + [shifted(sent[k], "enc", -k) for k in range(1, N_ENC)]
     mine = compact(idx, received, (near, far))
     pieces = [mine] + [shifted(mine, "mp", k) for k in range(1, N_MP)]
 
-    packed = after(packed, pieces[1], pieces[3])
+    packed = after(packed, in_hbm(mine))
     heads = over_z(attend(packed, core_swap(packed)))
     so, cq = cross_queries(heads, cross_wq)
 
-    *values, source = encode(pieces, enc_wq, enc_wk, enc_wv)
-    attn = [[v] + [shifted(v, "mp", k) for k in range(1, N_MP)] for v in values]
-    wo, wk, wv = load((enc_wo, near, far, core_swap(near)), cross_wk, cross_wv, cq)
-    second = cross(1, nbr_count, source, attn[0], wo, wk, wv, cq, so)
+    early, late, source = encode(pieces, enc_wq, enc_wk, enc_wv)
+    late = [late] + [shifted(late, "mp", k) for k in range(1, N_MP)]
+    early = after(early, late[1])
+    early = [early] + [shifted(early, "mp", k) for k in range(1, N_MP)]
+    wo = load((enc_wo, near, far, core_swap(near), core_swap(far)), cq)
+    second = cross(1, nbr_count, source, late, wo, cross_wk, cross_wv, cq, so)
     passed = shifted(second, "seq", 1)
-    first = cross(0, nbr_count, source, attn[1], wo, wk, wv, cq, so)
+    first = cross(0, nbr_count, source, early, wo, cross_wk, cross_wv, cq, so)
     return place(passed, first, second)
 
 

time: 91 us -> 80.1 us (0.88)
  Pallas kernels: 28.4 us -> 21.1 us
  waiting for transfers between devices: 18.8 us -> 15.5 us
  starting transfers between devices: 42.3 us -> 40.9 us
  local copies, waits for them, and re-layouts: 0.11 us -> 1.14 us
    ppermute x17, waiting for transfers between devices: 15.9 us -> 10.7 us  [shifted(): lax.ppermute(block, axis, [(i, (i + distance) % size) for i in range(size)])]
    pallas_call x2, Pallas kernels: 10.2 us -> 6.77 us  [cross(): pl.pallas_call(body, out_shape=sds((SPAN, cols)), in_specs=[SMEM] + [ANY]...]
    ppermute x1, waiting for transfers between devices: 0.01 us -> 1.78 us  [to_sides(): return lax.ppermute(block, ('seq', 'mp'), route)]
    ppermute x2 -> x3, starting transfers between devices: 4.1 us -> 2.55 us  [core_swap(): return lax.ppermute(block, 'seq', [(i, i ^ 1) for i in range(size)])]
    pallas_call x1, Pallas kernels: 4.96 us -> 3.44 us  [encode(): pl.pallas_call(encode_kernel, out_shape=[sds((rows // 2, width))] * 2 + [...]
    pallas_call x1, Pallas kernels: 4.18 us -> 2.75 us  [attend(): pl.pallas_call(attend_kernel, out_shape=sds((N_Z, tok, HEAD_DIM)), in_spe...]
    pallas_call x2, Pallas kernels: 5.02 us -> 3.89 us  [the longest x1 2.19 us: pack(): pl.pallas_call(pack_kernel, out_shape=[sds((N_Z, 3 * tok, HEAD_DIM)), sds...]
    unnamed x12 -> x20, local copies, waits for them, and re-layouts: 0.03 us -> 1.14 us
  transfers between devices with their start and end apart: 22 -> 23, of which waited for: 8 -> 7; matrix products, arithmetic and copies ran while one was open for 0% -> 0% of each run, Pallas kernels for 31% -> 23%
where the time goes in v1:
time: 80.1 us; the launch traced here: 78.8 us
  starting transfers between devices  40.9 us (51%)
  Pallas kernels  21.1 us (26%)
  waiting for transfers between devices  15.5 us (19%)
  local copies, waits for them, and re-layouts  1.14 us (1%)
    ppermute x17, starting transfers between devices, shifted(): lax.ppermute(block, axis, [(i, (i + distance) % size) for i in range(size)])  21.5 us
    all_to_all x2, starting transfers between devices, over_z(): lax.all_to_all(blocks, 'seq', 0, 0, axis_index_groups=groups, tiled=True)  14.3 us
    ppermute x17, waiting for transfers between devices, shifted(): lax.ppermute(block, axis, [(i, (i + distance) % size) for i in range(size)])  10.7 us
    pallas_call x2, Pallas kernels, cross(): pl.pallas_call(body, out_shape=sds((SPAN, cols)), in_specs=[SMEM] + [ANY]...  6.77 us
    pallas_call x1, Pallas kernels, encode(): pl.pallas_call(encode_kernel, out_shape=[sds((rows // 2, width))] * 2 + [...  3.44 us
    all_to_all x2, waiting for transfers between devices, over_z(): lax.all_to_all(blocks, 'seq', 0, 0, axis_index_groups=groups, tiled=True)  3.04 us
    pallas_call x1, Pallas kernels, attend(): pl.pallas_call(attend_kernel, out_shape=sds((N_Z, tok, HEAD_DIM)), in_spe...  2.75 us
    ppermute x3, starting transfers between devices, core_swap(): return lax.ppermute(block, 'seq', [(i, i ^ 1) for i in range(size)])  2.55 us
  transfers between devices with their start and end apart: 23, of which 7 were waited for; matrix products, arithmetic and copies ran while one was open for 0% of the time, Pallas kernels for 23%

profile of v1, /device:TPU:1, one launch (start us, length us, event | category | flops | bytes accessed | tf_op | source)
XLA Modules:
  0.0 78.8 jit_solution(11441557674341644386)
XLA Ops:
  0.0 2.2 %pack.1 = (bf16[8,384,128]{2,1,0:T(8,128)(2,1)}, s32[4]{0:T(128)S(1)}, bf16[128,1024]{1,0:T(8,128)(2,1)S(1)}) custom-call(bf16[1,128,1024]{2,1,0:T(8,128)(2,1)} %q.1, bf16[1,128,1024]{2,1,0:T(8,128)(2,1)} %k.1, bf16[1,128,1024]{2,1,0:T(8,128)(2,1)} %v.1, bf16[256,1024]{1,0:T(8,128)(2,1)} %w0.1, s32[1,2,2]{2,1,0:T(2,128)} %nbr_rows.1, s32[1,2,2]{2,1,0:T(2,128)} %nbr_owner.1), custom_call_target="tpu_custom_call" | custom-call | flops 1000000000 | bytes 1024 | tf_op jit(solution)/shard_map/pack/pallas_call | solution.py:333
  2.2 9.0 %all-to-all-start = ((bf16[8,384,128]{2,1,0:T(8,128)(2,1)}), bf16[8,384,128]{2,1,0:T(8,128)(2,1)S(1)}, u32[]{:S(2)}, u32[]{:S(2)}) async-start(bf16[8,384,128]{2,1,0:T(8,128)(2,1)} %get-tuple-element.25), calls=%async_computation | async-start | bytes 1572864 | tf_op jit(solution)/shard_map/all_to_all | solution.py:53
  11.2 1.3 %collective-permute-start = (s32[4]{0:T(128)S(1)}, s32[4]{0:T(128)S(1)}, u32[]{:S(2)}, u32[]{:S(2)}) collective-permute-start(s32[4]{0:T(128)S(1)} %get-tuple-element.17.idx0.idx), channel_id=1, source_target_pairs={{0,64},{64,128},{128,192},{192,0},{1,65},{65,129},{129,193},{193,1... | collective-permute-start | bytes 56 | tf_op jit(solution)/shard_map/ppermute | solution.py:33
  12.5 2.6 %collective-permute-start.1 = (s32[4]{0:T(128)S(1)}, s32[4]{0:T(128)S(1)}, u32[]{:S(2)}, u32[]{:S(2)}) collective-permute-start(s32[4]{0:T(128)S(1)} %get-tuple-element.17.idx0.idx), channel_id=1, source_target_pairs={{0,128},{64,192},{128,0},{192,64},{1,129},{65,193},{129,1},{193,65... | collective-permute-start | bytes 56 | tf_op jit(solution)/shard_map/ppermute | solution.py:33
  15.1 1.1 %collective-permute-start.2 = (s32[4]{0:T(128)S(1)}, s32[4]{0:T(128)S(1)}, u32[]{:S(2)}, u32[]{:S(2)}) collective-permute-start(s32[4]{0:T(128)S(1)} %get-tuple-element.17.idx0.idx), channel_id=1, source_target_pairs={{0,192},{64,0},{128,64},{192,128},{1,193},{65,1},{129,65},{193,129... | collective-permute-start | bytes 56 | tf_op jit(solution)/shard_map/ppermute | solution.py:33
  16.2 2.5 %collective-permute-start.6 = (bf16[256,1024]{1,0:T(8,128)(2,1)S(1)}, bf16[256,1024]{1,0:T(8,128)(2,1)S(1)}, u32[]{:S(2)}, u32[]{:S(2)}) collective-permute-start(bf16[256,1024]{1,0:T(8,128)(2,1)S(1)} %copy-done.7), channel_id=1, source_target_pairs={{0,1},{1,2},{2,3},{3,0},{4,7},{5,4},{6,5},{7,6},{8,9},{9,10},{10,1... | collective-permute-start | bytes 1572872 | tf_op jit(solution)/shard_map/ppermute | solution.py:43
  19.2 1.9 %fetch.1 = (bf16[256,256]{1,0:T(8,128)(2,1)S(1)}, bf16[256,256]{1,0:T(8,128)(2,1)S(1)}, bf16[256,256]{1,0:T(8,128)(2,1)S(1)}, bf16[256,256]{1,0:T(8,128)(2,1)S(1)}) custom-call(s32[4]{0:T(128)S(1)} %get-tuple-element.17.idx0.idx, s32[4]{0:T(128)S(1)} %collective-permute-done.idx1, s32[4]{0:T(128)S(1)} %collective-permute-done.1.idx2, ...), custom_call_target="tpu_custom_call" | custom-call | flops 5000000000 | bytes 1024 | tf_op jit(solution)/shard_map/fetch/pallas_call | solution.py:119
  21.6 1.6 %collective-permute-start.4 = (bf16[256,256]{1,0:T(8,128)(2,1)S(1)}, bf16[256,256]{1,0:T(8,128)(2,1)S(1)}, u32[]{:S(2)}, u32[]{:S(2)}) collective-permute-start(bf16[256,256]{1,0:T(8,128)(2,1)S(1)} %get-tuple-element.20), channel_id=1, source_target_pairs={{0,128},{64,192},{128,0},{192,64},{1,129},{65,193},{129,1},{193,65... | collective-permute-start | bytes 393224 | tf_op jit(solution)/shard_map/ppermute | solution.py:33
  23.3 2.1 %collective-permute-done.3.r1 = bf16[256,256]{1,0:T(8,128)(2,1)S(1)} collective-permute-done((bf16[256,256]{1,0:T(8,128)(2,1)S(1)}, bf16[256,256]{1,0:T(8,128)(2,1)S(1)}, u32[]{:S(2)}, u32[]{:S(2)}) %collective-permute-start.3) | collective-permute-done | bytes 131104 | tf_op jit(solution)/shard_map/ppermute | solution.py:33
  25.3 1.9 %collective-permute-done.4.r2 = bf16[256,256]{1,0:T(8,128)(2,1)S(1)} collective-permute-done((bf16[256,256]{1,0:T(8,128)(2,1)S(1)}, bf16[256,256]{1,0:T(8,128)(2,1)S(1)}, u32[]{:S(2)}, u32[]{:S(2)}) %collective-permute-start.4) | collective-permute-done | bytes 131104 | tf_op jit(solution)/shard_map/ppermute | solution.py:33
  27.2 1.4 %collective-permute-done.5.r3 = bf16[256,256]{1,0:T(8,128)(2,1)S(1)} collective-permute-done((bf16[256,256]{1,0:T(8,128)(2,1)S(1)}, bf16[256,256]{1,0:T(8,128)(2,1)S(1)}, u32[]{:S(2)}, u32[]{:S(2)}) %collective-permute-start.5) | collective-permute-done | bytes 131104 | tf_op jit(solution)/shard_map/ppermute | solution.py:33
  28.7 1.8 %collective-permute-done.6.w1.w_near = bf16[256,1024]{1,0:T(8,128)(2,1)S(1)} collective-permute-done((bf16[256,1024]{1,0:T(8,128)(2,1)S(1)}, bf16[256,1024]{1,0:T(8,128)(2,1)S(1)}, u32[]{:S(2)}, u32[]{:S(2)}) %collective-permute-start.6) | collective-permute-done | bytes 524320 | tf_op jit(solution)/shard_map/ppermute | solution.py:43
  30.4 1.3 %compact.1.x0.refs_1_ = bf16[512,256]{1,0:T(8,128)(2,1)} custom-call(s32[4]{0:T(128)S(1)} %get-tuple-element.17.idx0.idx, bf16[256,256]{1,0:T(8,128)(2,1)S(1)} %get-tuple-element.18.r0, bf16[256,256]{1,0:T(8,128)(2,1)S(1)} %collective-permute-done.3.r1, bf16[256,256]{1,0:T(8,128)(2,1)S(1)} %collective-permute-done.4.r2, ...), custom_call_target="tpu_custom_call" | custom-call | flops 1000000000 | bytes 1024 | tf_op jit(solution)/shard_map/compact/pallas_call | solution.py:156
  31.8 3.0 %all-to-all-done.refs_0_ = bf16[8,384,128]{2,1,0:T(8,128)(2,1)S(1)} async-done(((bf16[8,384,128]{2,1,0:T(8,128)(2,1)}), bf16[8,384,128]{2,1,0:T(8,128)(2,1)S(1)}, u32[]{:S(2)}, u32[]{:S(2)}) %all-to-all-start) | async-done | bytes 786464 | tf_op jit(solution)/shard_map/all_to_all | solution.py:53
  34.8 1.2 %collective-permute-start.16 = (bf16[8,384,128]{2,1,0:T(8,128)(2,1)S(1)}, bf16[8,384,128]{2,1,0:T(8,128)(2,1)S(1)}, u32[]{:S(2)}, u32[]{:S(2)}) collective-permute-start(bf16[8,384,128]{2,1,0:T(8,128)(2,1)S(1)} %after.2.own), channel_id=1, source_target_pairs={{0,4},{4,0},{8,12},{12,8},{16,20},{20,16},{24,28},{28,24},{32,36},... | collective-permute-start | bytes 2359304 | tf_op jit(solution)/shard_map/ppermute | solution.py:48
  36.1 1.8 %collective-permute-start.10 = (bf16[512,256]{1,0:T(8,128)(2,1)}, bf16[512,256]{1,0:T(8,128)(2,1)S(1)}, u32[]{:S(2)}, u32[]{:S(2)}) collective-permute-start(bf16[512,256]{1,0:T(8,128)(2,1)} %compact.1.x0.refs_1_), channel_id=1, source_target_pairs={{0,3},{1,0},{2,1},{3,2},{4,7},{5,4},{6,5},{7,6},{8,11},{9,8},{10,9... | collective-permute-start | bytes 786440 | tf_op jit(solution)/shard_map/ppermute | solution.py:33
  37.9 1.7 %collective-permute-start.9 = (bf16[512,256]{1,0:T(8,128)(2,1)}, bf16[512,256]{1,0:T(8,128)(2,1)S(1)}, u32[]{:S(2)}, u32[]{:S(2)}) collective-permute-start(bf16[512,256]{1,0:T(8,128)(2,1)} %compact.1.x0.refs_1_), channel_id=1, source_target_pairs={{0,2},{1,3},{2,0},{3,1},{4,6},{5,7},{6,4},{7,5},{8,10},{9,11},{10,... | collective-permute-start | bytes 786440 | tf_op jit(solution)/shard_map/ppermute | solution.py:33
  39.6 1.3 %collective-permute-start.14 = (bf16[256,1024]{1,0:T(8,128)(2,1)S(1)}, bf16[256,1024]{1,0:T(8,128)(2,1)S(1)}, u32[]{:S(2)}, u32[]{:S(2)}) collective-permute-start(bf16[256,1024]{1,0:T(8,128)(2,1)S(1)} %collective-permute-done.6.w1.w_near), channel_id=1, source_target_pairs={{0,4},{4,0},{8,12},{12,8},{16,20},{20,16},{24,28},{28,24},{32,36},... | collective-permute-start | bytes 1572872 | tf_op jit(solution)/shard_map/ppermute | solution.py:48
  40.9 2.7 %attend.1 = bf16[8,128,128]{2,1,0:T(8,128)(2,1)} custom-call(bf16[8,384,128]{2,1,0:T(8,128)(2,1)S(1)} %after.2.own, bf16[8,384,128]{2,1,0:T(8,128)(2,1)S(1)} %collective-permute-done.16.other), custom_call_target="tpu_custom_call" | custom-call | flops 10000000000 | bytes 1024 | tf_op jit(solution)/shard_map/attend/pallas_call | solution.py:395
  43.6 5.3 %all-to-all-start.1 = ((bf16[8,128,128]{2,1,0:T(8,128)(2,1)}), bf16[8,128,128]{2,1,0:T(8,128)(2,1)S(1)}, u32[]{:S(2)}, u32[]{:S(2)}) async-start(bf16[8,128,128]{2,1,0:T(8,128)(2,1)} %attend.1), calls=%async_computation.1 | async-start | bytes 524288 | tf_op jit(solution)/shard_map/all_to_all | solution.py:53
  48.9 2.2 %collective-permute-done.9.x2 = bf16[512,256]{1,0:T(8,128)(2,1)S(1)} collective-permute-done((bf16[512,256]{1,0:T(8,128)(2,1)}, bf16[512,256]{1,0:T(8,128)(2,1)S(1)}, u32[]{:S(2)}, u32[]{:S(2)}) %collective-permute-start.9) | collective-permute-done | bytes 262176 | tf_op jit(solution)/shard_map/ppermute | solution.py:33
  51.2 3.4 %encode.1 = (bf16[256,256]{1,0:T(8,128)(2,1)S(1)}, bf16[256,256]{1,0:T(8,128)(2,1)S(1)}, bf16[512,1024]{1,0:T(8,128)(2,1)}) custom-call(bf16[512,256]{1,0:T(8,128)(2,1)S(1)} %copy-done, bf16[512,256]{1,0:T(8,128)(2,1)S(1)} %collective-permute-done.8.x1, bf16[512,256]{1,0:T(8,128)(2,1)S(1)} %collective-permute-done.9.x2, ...), custom_call_target="tpu_custom_call" | custom-call | flops 30000001024 | bytes 1024 | tf_op jit(solution)/shard_map/encode/pallas_call | solution.py:213
  54.7 1.9 %collective-permute-start.12 = (bf16[256,256]{1,0:T(8,128)(2,1)S(1)}, bf16[256,256]{1,0:T(8,128)(2,1)S(1)}, u32[]{:S(2)}, u32[]{:S(2)}) collective-permute-start(bf16[256,256]{1,0:T(8,128)(2,1)S(1)} %get-tuple-element.24.refs_2_), channel_id=1, source_target_pairs={{0,2},{1,3},{2,0},{3,1},{4,6},{5,7},{6,4},{7,5},{8,10},{9,11},{10,... | collective-permute-start | bytes 393224 | tf_op jit(solution)/shard_map/ppermute | solution.py:33
  56.6 1.8 %collective-permute-start.13 = (bf16[256,256]{1,0:T(8,128)(2,1)S(1)}, bf16[256,256]{1,0:T(8,128)(2,1)S(1)}, u32[]{:S(2)}, u32[]{:S(2)}) collective-permute-start(bf16[256,256]{1,0:T(8,128)(2,1)S(1)} %get-tuple-element.24.refs_2_), channel_id=1, source_target_pairs={{0,3},{1,0},{2,1},{3,2},{4,7},{5,4},{6,5},{7,6},{8,11},{9,8},{10,9... | collective-permute-start | bytes 393224 | tf_op jit(solution)/shard_map/ppermute | solution.py:33
  58.3 3.0 %collective-permute-done.11.refs_3_.refs_1_ = bf16[256,256]{1,0:T(8,128)(2,1)S(1)} collective-permute-done((bf16[256,256]{1,0:T(8,128)(2,1)S(1)}, bf16[256,256]{1,0:T(8,128)(2,1)S(1)}, u32[]{:S(2)}, u32[]{:S(2)}) %collective-permute-start.11) | collective-permute-done | bytes 131104 | tf_op jit(solution)/shard_map/ppermute | solution.py:33
  61.6 2.3 %collective-permute-start.19 = (bf16[256,256]{1,0:T(8,128)(2,1)S(1)}, bf16[256,256]{1,0:T(8,128)(2,1)S(1)}, u32[]{:S(2)}, u32[]{:S(2)}) collective-permute-start(bf16[256,256]{1,0:T(8,128)(2,1)S(1)} %after.3.refs_2_), channel_id=1, source_target_pairs={{0,2},{1,3},{2,0},{3,1},{4,6},{5,7},{6,4},{7,5},{8,10},{9,11},{10,... | collective-permute-start | bytes 393224 | tf_op jit(solution)/shard_map/ppermute | solution.py:33
  63.9 1.9 %collective-permute-start.20 = (bf16[256,256]{1,0:T(8,128)(2,1)S(1)}, bf16[256,256]{1,0:T(8,128)(2,1)S(1)}, u32[]{:S(2)}, u32[]{:S(2)}) collective-permute-start(bf16[256,256]{1,0:T(8,128)(2,1)S(1)} %after.3.refs_2_), channel_id=1, source_target_pairs={{0,3},{1,0},{2,1},{3,2},{4,7},{5,4},{6,5},{7,6},{8,11},{9,8},{10,9... | collective-permute-start | bytes 393224 | tf_op jit(solution)/shard_map/ppermute | solution.py:33
  65.9 1.7 %load.1.refs_6_ = bf16[1024,1024]{1,0:T(8,128)(2,1)S(1)} custom-call(bf16[256,1024]{1,0:T(8,128)(2,1)} %w0.1, bf16[256,1024]{1,0:T(8,128)(2,1)} %copy-done.3, bf16[128,1024]{1,0:T(8,128)(2,1)} %copy-done.5, bf16[256,1024]{1,0:T(8,128)(2,1)} %copy-done.8, bf16[128,1024]{1,0:T(8,128)(2,1)} %copy-done.9, bf16[128,1024]{1,0:T(8,128)(2,1)S(1)} %get-tuple-element.26.tie.refs_9_), custom_call_target="tpu_custom_call" | custom-call | flops 3000000000 | bytes 1024 | tf_op jit(solution)/shard_map/load/pallas_call | solution.py:245
  68.7 3.4 %cross.2.second = bf16[64,1024]{1,0:T(8,128)(2,1)S(1)} custom-call(s32[1,32]{1,0:T(1,128)S(1)} %copy-done.6, bf16[512,1024]{1,0:T(8,128)(2,1)} %get-tuple-element.23.refs_1_, bf16[256,256]{1,0:T(8,128)(2,1)S(1)} %get-tuple-element.24.refs_2_, bf16[256,256]{1,0:T(8,128)(2,1)S(1)} %collective-permute-done.11.refs_3_.refs_1_, ...), custom_call_target="tpu_custom_call" | custom-call | flops 5000000000 | bytes 1024 | tf_op jit(solution)/shard_map/cross/pallas_call | solution.py:294
  72.1 2.5 %collective-permute-start.17 = (bf16[64,1024]{1,0:T(8,128)(2,1)S(1)}, bf16[64,1024]{1,0:T(8,128)(2,1)S(1)}, u32[]{:S(2)}, u32[]{:S(2)}) collective-permute-start(bf16[64,1024]{1,0:T(8,128)(2,1)S(1)} %cross.2.second), channel_id=1, source_target_pairs={{0,4},{4,8},{8,12},{12,16},{16,20},{20,24},{24,28},{28,32},{32,36}... | collective-permute-start | bytes 393224 | tf_op jit(solution)/shard_map/ppermute | solution.py:33
  74.6 3.4 %cross.3.first = bf16[64,1024]{1,0:T(8,128)(2,1)S(1)} custom-call(s32[1,32]{1,0:T(1,128)S(1)} %copy-done.6, bf16[512,1024]{1,0:T(8,128)(2,1)} %get-tuple-element.23.refs_1_, bf16[256,256]{1,0:T(8,128)(2,1)S(1)} %after.3.refs_2_, bf16[256,256]{1,0:T(8,128)(2,1)S(1)} %collective-permute-done.18.refs_3_, bf16[256,256]{1,0:T(8,128)(2,1)S(1)} %collective-permute-done.19.refs_4_, ...), custom_call_target="tpu_custom_call" | custom-call | flops 5000000000 | bytes 1024 | tf_op jit(solution)/shard_map/cross/pallas_call | solution.py:294
  78.0 0.8 place.1
  (46 shorter events, 2.7 us)
Async XLA Ops:
  0.0 16.2 %copy-start.7 = (bf16[256,1024]{1,0:T(8,128)(2,1)S(1)}, bf16[256,1024]{1,0:T(8,128)(2,1)}, u32[]{:S(2)}) copy-start(bf16[256,1024]{1,0:T(8,128)(2,1)} %w0.1) | copy-start | bytes 1572868
  2.2 32.6 %all-to-all-start = ((bf16[8,384,128]{2,1,0:T(8,128)(2,1)}), bf16[8,384,128]{2,1,0:T(8,128)(2,1)S(1)}, u32[]{:S(2)}, u32[]{:S(2)}) async-start(bf16[8,384,128]{2,1,0:T(8,128)(2,1)} %get-tuple-element.25), calls=%async_computation | async-start | bytes 1572864 | tf_op jit(solution)/shard_map/all_to_all | solution.py:53
  11.2 8.0 %collective-permute-start = (s32[4]{0:T(128)S(1)}, s32[4]{0:T(128)S(1)}, u32[]{:S(2)}, u32[]{:S(2)}) collective-permute-start(s32[4]{0:T(128)S(1)} %get-tuple-element.17.idx0.idx), channel_id=1, source_target_pairs={{0,64},{64,128},{128,192},{192,0},{1,65},{65,129},{129,193},{193,1... | collective-permute-start | bytes 56 | tf_op jit(solution)/shard_map/ppermute | solution.py:33
  12.5 6.7 %collective-permute-start.1 = (s32[4]{0:T(128)S(1)}, s32[4]{0:T(128)S(1)}, u32[]{:S(2)}, u32[]{:S(2)}) collective-permute-start(s32[4]{0:T(128)S(1)} %get-tuple-element.17.idx0.idx), channel_id=1, source_target_pairs={{0,128},{64,192},{128,0},{192,64},{1,129},{65,193},{129,1},{193,65... | collective-permute-start | bytes 56 | tf_op jit(solution)/shard_map/ppermute | solution.py:33
  15.1 4.1 %collective-permute-start.2 = (s32[4]{0:T(128)S(1)}, s32[4]{0:T(128)S(1)}, u32[]{:S(2)}, u32[]{:S(2)}) collective-permute-start(s32[4]{0:T(128)S(1)} %get-tuple-element.17.idx0.idx), channel_id=1, source_target_pairs={{0,192},{64,0},{128,64},{192,128},{1,193},{65,1},{129,65},{193,129... | collective-permute-start | bytes 56 | tf_op jit(solution)/shard_map/ppermute | solution.py:33
  16.2 14.2 %collective-permute-start.6 = (bf16[256,1024]{1,0:T(8,128)(2,1)S(1)}, bf16[256,1024]{1,0:T(8,128)(2,1)S(1)}, u32[]{:S(2)}, u32[]{:S(2)}) collective-permute-start(bf16[256,1024]{1,0:T(8,128)(2,1)S(1)} %copy-done.7), channel_id=1, source_target_pairs={{0,1},{1,2},{2,3},{3,0},{4,7},{5,4},{6,5},{7,6},{8,9},{9,10},{10,1... | collective-permute-start | bytes 1572872 | tf_op jit(solution)/shard_map/ppermute | solution.py:43
  18.7 10.0 %collective-permute-start.7 = (bf16[128,1024]{1,0:T(8,128)(2,1)S(1)}, bf16[128,1024]{1,0:T(8,128)(2,1)S(1)}, u32[]{:S(2)}, u32[]{:S(2)}) collective-permute-start(bf16[128,1024]{1,0:T(8,128)(2,1)S(1)} %get-tuple-element.22), channel_id=1, source_target_pairs={{0,2},{1,3},{2,0},{3,1},{4,6},{5,7},{6,4},{7,5},{8,10},{9,11},{10,... | collective-permute-start | bytes 786440 | tf_op jit(solution)/shard_map/ppermute | solution.py:33
  21.1 4.2 %collective-permute-start.3 = (bf16[256,256]{1,0:T(8,128)(2,1)S(1)}, bf16[256,256]{1,0:T(8,128)(2,1)S(1)}, u32[]{:S(2)}, u32[]{:S(2)}) collective-permute-start(bf16[256,256]{1,0:T(8,128)(2,1)S(1)} %get-tuple-element.19), channel_id=1, source_target_pairs={{0,192},{64,0},{128,64},{192,128},{1,193},{65,1},{129,65},{193,129... | collective-permute-start | bytes 393224 | tf_op jit(solution)/shard_map/ppermute | solution.py:33
  21.6 5.6 %collective-permute-start.4 = (bf16[256,256]{1,0:T(8,128)(2,1)S(1)}, bf16[256,256]{1,0:T(8,128)(2,1)S(1)}, u32[]{:S(2)}, u32[]{:S(2)}) collective-permute-start(bf16[256,256]{1,0:T(8,128)(2,1)S(1)} %get-tuple-element.20), channel_id=1, source_target_pairs={{0,128},{64,192},{128,0},{192,64},{1,129},{65,193},{129,1},{193,65... | collective-permute-start | bytes 393224 | tf_op jit(solution)/shard_map/ppermute | solution.py:33
  23.2 5.4 %collective-permute-start.5 = (bf16[256,256]{1,0:T(8,128)(2,1)S(1)}, bf16[256,256]{1,0:T(8,128)(2,1)S(1)}, u32[]{:S(2)}, u32[]{:S(2)}) collective-permute-start(bf16[256,256]{1,0:T(8,128)(2,1)S(1)} %get-tuple-element.21), channel_id=1, source_target_pairs={{0,64},{64,128},{128,192},{192,0},{1,65},{65,129},{129,193},{193,1... | collective-permute-start | bytes 393224 | tf_op jit(solution)/shard_map/ppermute | solution.py:33
  28.7 7.3 %copy-start.5 = (bf16[128,1024]{1,0:T(8,128)(2,1)}, bf16[128,1024]{1,0:T(8,128)(2,1)S(1)}, u32[]{:S(2)}) copy-start(bf16[128,1024]{1,0:T(8,128)(2,1)S(1)} %collective-permute-done.7.w2.w_half) | copy-start | bytes 786436
  30.4 9.2 %copy-start.3 = (bf16[256,1024]{1,0:T(8,128)(2,1)}, bf16[256,1024]{1,0:T(8,128)(2,1)S(1)}, u32[]{:S(2)}) copy-start(bf16[256,1024]{1,0:T(8,128)(2,1)S(1)} %collective-permute-done.6.w1.w_near) | copy-start | bytes 1572868
  34.8 16.4 %copy-start = (bf16[512,256]{1,0:T(8,128)(2,1)S(1)}, bf16[512,256]{1,0:T(8,128)(2,1)}, u32[]{:S(2)}) copy-start(bf16[512,256]{1,0:T(8,128)(2,1)} %compact.1.x0.refs_1_) | copy-start | bytes 786436
  34.8 4.8 %collective-permute-start.16 = (bf16[8,384,128]{2,1,0:T(8,128)(2,1)S(1)}, bf16[8,384,128]{2,1,0:T(8,128)(2,1)S(1)}, u32[]{:S(2)}, u32[]{:S(2)}) collective-permute-start(bf16[8,384,128]{2,1,0:T(8,128)(2,1)S(1)} %after.2.own), channel_id=1, source_target_pairs={{0,4},{4,0},{8,12},{12,8},{16,20},{20,16},{24,28},{28,24},{32,36},... | collective-permute-start | bytes 2359304 | tf_op jit(solution)/shard_map/ppermute | solution.py:48
  36.0 25.6 %collective-permute-start.15 = (bf16[128,1024]{1,0:T(8,128)(2,1)S(1)}, bf16[128,1024]{1,0:T(8,128)(2,1)S(1)}, u32[]{:S(2)}, u32[]{:S(2)}) collective-permute-start(bf16[128,1024]{1,0:T(8,128)(2,1)S(1)} %collective-permute-done.7.w2.w_half), channel_id=1, source_target_pairs={{0,4},{4,0},{8,12},{12,8},{16,20},{20,16},{24,28},{28,24},{32,36},... | collective-permute-start | bytes 786440 | tf_op jit(solution)/shard_map/ppermute | solution.py:48
  36.1 12.8 %collective-permute-start.10 = (bf16[512,256]{1,0:T(8,128)(2,1)}, bf16[512,256]{1,0:T(8,128)(2,1)S(1)}, u32[]{:S(2)}, u32[]{:S(2)}) collective-permute-start(bf16[512,256]{1,0:T(8,128)(2,1)} %compact.1.x0.refs_1_), channel_id=1, source_target_pairs={{0,3},{1,0},{2,1},{3,2},{4,7},{5,4},{6,5},{7,6},{8,11},{9,8},{10,9... | collective-permute-start | bytes 786440 | tf_op jit(solution)/shard_map/ppermute | solution.py:33
  37.9 11.1 %collective-permute-start.8 = (bf16[512,256]{1,0:T(8,128)(2,1)}, bf16[512,256]{1,0:T(8,128)(2,1)S(1)}, u32[]{:S(2)}, u32[]{:S(2)}) collective-permute-start(bf16[512,256]{1,0:T(8,128)(2,1)} %compact.1.x0.refs_1_), channel_id=1, source_target_pairs={{0,1},{1,2},{2,3},{3,0},{4,5},{5,6},{6,7},{7,4},{8,9},{9,10},{10,1... | collective-permute-start | bytes 786440 | tf_op jit(solution)/shard_map/ppermute | solution.py:33
  37.9 13.3 %collective-permute-start.9 = (bf16[512,256]{1,0:T(8,128)(2,1)}, bf16[512,256]{1,0:T(8,128)(2,1)S(1)}, u32[]{:S(2)}, u32[]{:S(2)}) collective-permute-start(bf16[512,256]{1,0:T(8,128)(2,1)} %compact.1.x0.refs_1_), channel_id=1, source_target_pairs={{0,2},{1,3},{2,0},{3,1},{4,6},{5,7},{6,4},{7,5},{8,10},{9,11},{10,... | collective-permute-start | bytes 786440 | tf_op jit(solution)/shard_map/ppermute | solution.py:33
  39.6 24.3 %collective-permute-start.14 = (bf16[256,1024]{1,0:T(8,128)(2,1)S(1)}, bf16[256,1024]{1,0:T(8,128)(2,1)S(1)}, u32[]{:S(2)}, u32[]{:S(2)}) collective-permute-start(bf16[256,1024]{1,0:T(8,128)(2,1)S(1)} %collective-permute-done.6.w1.w_near), channel_id=1, source_target_pairs={{0,4},{4,0},{8,12},{12,8},{16,20},{20,16},{24,28},{28,24},{32,36},... | collective-permute-start | bytes 1572872 | tf_op jit(solution)/shard_map/ppermute | solution.py:48
  43.6 17.7 %all-to-all-start.1 = ((bf16[8,128,128]{2,1,0:T(8,128)(2,1)}), bf16[8,128,128]{2,1,0:T(8,128)(2,1)S(1)}, u32[]{:S(2)}, u32[]{:S(2)}) async-start(bf16[8,128,128]{2,1,0:T(8,128)(2,1)} %attend.1), calls=%async_computation.1 | async-start | bytes 524288 | tf_op jit(solution)/shard_map/all_to_all | solution.py:53
  48.9 12.4 %copy-start.4 = (bf16[8,128,128]{2,1,0:T(8,128)(2,1)S(1)}, bf16[8,128,128]{2,1,0:T(8,128)(2,1)}, u32[]{:S(2)}) copy-start(bf16[8,128,128]{2,1,0:T(8,128)(2,1)} %wq.3) | copy-start | bytes 786436
  54.6 6.7 %collective-permute-start.11 = (bf16[256,256]{1,0:T(8,128)(2,1)S(1)}, bf16[256,256]{1,0:T(8,128)(2,1)S(1)}, u32[]{:S(2)}, u32[]{:S(2)}) collective-permute-start(bf16[256,256]{1,0:T(8,128)(2,1)S(1)} %get-tuple-element.24.refs_2_), channel_id=1, source_target_pairs={{0,1},{1,2},{2,3},{3,0},{4,5},{5,6},{6,7},{7,4},{8,9},{9,10},{10,1... | collective-permute-start | bytes 393224 | tf_op jit(solution)/shard_map/ppermute | solution.py:33
  54.7 12.9 %collective-permute-start.12 = (bf16[256,256]{1,0:T(8,128)(2,1)S(1)}, bf16[256,256]{1,0:T(8,128)(2,1)S(1)}, u32[]{:S(2)}, u32[]{:S(2)}) collective-permute-start(bf16[256,256]{1,0:T(8,128)(2,1)S(1)} %get-tuple-element.24.refs_2_), channel_id=1, source_target_pairs={{0,2},{1,3},{2,0},{3,1},{4,6},{5,7},{6,4},{7,5},{8,10},{9,11},{10,... | collective-permute-start | bytes 393224 | tf_op jit(solution)/shard_map/ppermute | solution.py:33
  56.6 11.0 %collective-permute-start.13 = (bf16[256,256]{1,0:T(8,128)(2,1)S(1)}, bf16[256,256]{1,0:T(8,128)(2,1)S(1)}, u32[]{:S(2)}, u32[]{:S(2)}) collective-permute-start(bf16[256,256]{1,0:T(8,128)(2,1)S(1)} %get-tuple-element.24.refs_2_), channel_id=1, source_target_pairs={{0,3},{1,0},{2,1},{3,2},{4,7},{5,4},{6,5},{7,6},{8,11},{9,8},{10,9... | collective-permute-start | bytes 393224 | tf_op jit(solution)/shard_map/ppermute | solution.py:33
  61.4 13.2 %collective-permute-start.18 = (bf16[256,256]{1,0:T(8,128)(2,1)S(1)}, bf16[256,256]{1,0:T(8,128)(2,1)S(1)}, u32[]{:S(2)}, u32[]{:S(2)}) collective-permute-start(bf16[256,256]{1,0:T(8,128)(2,1)S(1)} %after.3.refs_2_), channel_id=1, source_target_pairs={{0,1},{1,2},{2,3},{3,0},{4,5},{5,6},{6,7},{7,4},{8,9},{9,10},{10,1... | collective-permute-start | bytes 393224 | tf_op jit(solution)/shard_map/ppermute | solution.py:33
  61.6 4.2 %copy-start.9 = (bf16[128,1024]{1,0:T(8,128)(2,1)}, bf16[128,1024]{1,0:T(8,128)(2,1)S(1)}, u32[]{:S(2)}) copy-start(bf16[128,1024]{1,0:T(8,128)(2,1)S(1)} %collective-permute-done.15.s_half) | copy-start | bytes 786436
  61.6 13.0 %collective-permute-start.19 = (bf16[256,256]{1,0:T(8,128)(2,1)S(1)}, bf16[256,256]{1,0:T(8,128)(2,1)S(1)}, u32[]{:S(2)}, u32[]{:S(2)}) collective-permute-start(bf16[256,256]{1,0:T(8,128)(2,1)S(1)} %after.3.refs_2_), channel_id=1, source_target_pairs={{0,2},{1,3},{2,0},{3,1},{4,6},{5,7},{6,4},{7,5},{8,10},{9,11},{10,... | collective-permute-start | bytes 393224 | tf_op jit(solution)/shard_map/ppermute | solution.py:33
  63.9 10.7 %collective-permute-start.20 = (bf16[256,256]{1,0:T(8,128)(2,1)S(1)}, bf16[256,256]{1,0:T(8,128)(2,1)S(1)}, u32[]{:S(2)}, u32[]{:S(2)}) collective-permute-start(bf16[256,256]{1,0:T(8,128)(2,1)S(1)} %after.3.refs_2_), channel_id=1, source_target_pairs={{0,3},{1,0},{2,1},{3,2},{4,7},{5,4},{6,5},{7,6},{8,11},{9,8},{10,9... | collective-permute-start | bytes 393224 | tf_op jit(solution)/shard_map/ppermute | solution.py:33
  65.9 2.2 %copy-start.1 = (bf16[1024,1024]{1,0:T(8,128)(2,1)S(1)}, bf16[1024,1024]{1,0:T(8,128)(2,1)}, u32[]{:S(2)}) copy-start(bf16[1024,1024]{1,0:T(8,128)(2,1)} %refs_7_.3) | copy-start | bytes 6291460
  65.9 2.9 %copy-start.2 = (bf16[1024,1024]{1,0:T(8,128)(2,1)S(1)}, bf16[1024,1024]{1,0:T(8,128)(2,1)}, u32[]{:S(2)}) copy-start(bf16[1024,1024]{1,0:T(8,128)(2,1)} %refs_8_.3) | copy-start | bytes 6291460
  65.9 2.8 %copy-start.6 = (s32[1,32]{1,0:T(1,128)S(1)}, s32[1,32]{1,0:T(1,128)}, u32[]{:S(2)}) copy-start(s32[1,32]{1,0:T(1,128)} %refs_0_.3) | copy-start | bytes 388
  72.1 5.9 %collective-permute-start.17 = (bf16[64,1024]{1,0:T(8,128)(2,1)S(1)}, bf16[64,1024]{1,0:T(8,128)(2,1)S(1)}, u32[]{:S(2)}, u32[]{:S(2)}) collective-permute-start(bf16[64,1024]{1,0:T(8,128)(2,1)S(1)} %cross.2.second), channel_id=1, source_target_pairs={{0,4},{4,8},{8,12},{12,16},{16,20},{20,24},{24,28},{28,32},{32,36}... | collective-permute-start | bytes 393224 | tf_op jit(solution)/shard_map/ppermute | solution.py:33
  (1 other events, 1.9 us)

commit v2 on v1

--- a/solution.py
+++ b/solution.py
@@ -155,7 +155,7 @@
     rows, cols = received[0].shape
     return pl.pallas_call(
         compact_kernel,
-        out_shape=pltpu.HBM((K_NB * rows, cols), BF),
+        out_shape=sds((K_NB * rows, cols)),
         in_specs=[SMEM] + [ANY] * 6,
         out_specs=ANY,
         scratch_shapes=[pltpu.SemaphoreType.DMA((4,))],
@@ -179,21 +179,15 @@
     return [mix / total for mix, total in zip(mixes, totals)]
 
 
-def encode_kernel(x0, x1, x2, x3, wq, wk, wv, first, second, src_out, src, w, sems):
+def encode_kernel(x0, x1, x2, x3, wq, wk, wv, first, second, src_out, src, sems):
     width = x0.shape[1]
     pairs = [(x, src.at[:, source_columns(k, width)]) for k, x in enumerate((x0, x1, x2, x3))]
-    pairs += [(ref, w.at[n]) for n, ref in enumerate((wq, wk, wv))]
-    copies = run_copies(pairs, sems)
-    for c in copies[:5]:
+    for c in run_copies(pairs, sems):
         c.wait()
     kept = pltpu.make_async_copy(src, src_out, sems.at[0])
     kept.start()
     source = src[...]
-    q = dot(source, w[0]).astype(BF)
-    copies[5].wait()
-    k = dot(source, w[1]).astype(BF)
-    copies[6].wait()
-    v = dot(source, w[2]).astype(BF)
+    q, k, v = (dot(source, w[...]).astype(BF) for w in (wq, wk, wv))
     places = [
         (slice(n * NT, (n + 1) * NT), slice(h * HEAD_DIM, (h + 1) * HEAD_DIM))
         for n in range(src.shape[0] // NT)
@@ -213,17 +207,13 @@
     return pl.pallas_call(
         encode_kernel,
         out_shape=[sds((rows // 2, width))] * 2 + [pltpu.HBM((rows, depth), BF)],
-        in_specs=[ANY] * 7,
+        in_specs=[ANY] * 4 + [VMEM] * 3,
         out_specs=[VMEM, VMEM, ANY],
-        scratch_shapes=[
-            pltpu.VMEM((rows, depth), BF),
-            pltpu.VMEM((3, depth, width), BF),
-            pltpu.SemaphoreType.DMA((7,)),
-        ],
+        scratch_shapes=[pltpu.VMEM((rows, depth), BF), pltpu.SemaphoreType.DMA((4,))],
         compiler_params=params(12),
         cost_estimate=cost(30 * 10**9, 1024),
         name="encode",
-    )(*pieces, *map(in_hbm, (wq, wk, wv)))
+    )(*pieces, wq, wk, wv)
 
 
 def load_kernel(w0, w_near, w_half, s_near, s_half, tie, wo_out, sems):
@@ -251,7 +241,7 @@
         compiler_params=params(1),
         cost_estimate=cost(3 * 10**9, 1024),
         name="load",
-    )(*map(in_hbm, wo), tie)
+    )(*map(in_hbm, wo[:3]), *wo[3:], tie)
 
 
 def cross_kernel(which, counts, src, a0, a1, a2, a3, wo, wk, wv, cq, so, out, src_s, attn, sems):
@@ -456,15 +446,15 @@
     mine = compact(idx, received, (near, far))
     pieces = [mine] + [shifted(mine, "mp", k) for k in range(1, N_MP)]
 
-    packed = after(packed, in_hbm(mine))
+    packed = after(packed, mine)
     heads = over_z(attend(packed, core_swap(packed)))
     so, cq = cross_queries(heads, cross_wq)
 
     early, late, source = encode(pieces, enc_wq, enc_wk, enc_wv)
     late = [late] + [shifted(late, "mp", k) for k in range(1, N_MP)]
-    early = after(early, late[1])
+    wo = load((enc_wo, near, far, core_swap(near), core_swap(far)), cq)
+    early = after(early, wo)
     early = [early] + [shifted(early, "mp", k) for k in range(1, N_MP)]
-    wo = load((enc_wo, near, far, core_swap(near), core_swap(far)), cq)
     second = cross(1, nbr_count, source, late, wo, cross_wk, cross_wv, cq, so)
     passed = shifted(second, "seq", 1)
     first = cross(0, nbr_count, source, early, wo, cross_wk, cross_wv, cq, so)

time: 80.1 us -> 77.1 us (0.963); the launches traced: 78.8 us -> 76.6 us
  Pallas kernels: 21.1 us -> 19.9 us
  waiting for transfers between devices: 15.5 us -> 16.6 us
  local copies, waits for them, and re-layouts: 1.14 us -> 0.04 us
  starting transfers between devices: 40.9 us -> 39.9 us
    all_to_all x2, waiting for transfers between devices: 3.04 us -> 6.97 us  [over_z(): lax.all_to_all(blocks, 'seq', 0, 0, axis_index_groups=groups, tiled=True)]
    ppermute x17, waiting for transfers between devices: 10.7 us -> 7.81 us  [shifted(): lax.ppermute(block, axis, [(i, (i + distance) % size) for i in range(size)])]
    unnamed x20, local copies, waits for them, and re-layouts: 1.14 us -> 0.04 us
    pallas_call x1, Pallas kernels: 3.44 us -> 2.57 us  [encode(): pl.pallas_call(encode_kernel, out_shape=[sds((rows // 2, width))] * 2 + [...]
  transfers between devices with their start and end apart: 23 -> 23, of which waited for: 7 -> 7; matrix products, arithmetic and copies ran while one was open for 0% -> 0% of each run, Pallas kernels for 23% -> 22%
where the time goes in v2:
time: 77.1 us; the launch traced here: 76.6 us
  starting transfers between devices  39.9 us (52%)
  Pallas kernels  19.9 us (26%)
  waiting for transfers between devices  16.6 us (22%)
    ppermute x17, starting transfers between devices, shifted(): lax.ppermute(block, axis, [(i, (i + distance) % size) for i in range(size)])  21 us
    all_to_all x2, starting transfers between devices, over_z(): lax.all_to_all(blocks, 'seq', 0, 0, axis_index_groups=groups, tiled=True)  14.1 us
    ppermute x17, waiting for transfers between devices, shifted(): lax.ppermute(block, axis, [(i, (i + distance) % size) for i in range(size)])  7.81 us
    all_to_all x2, waiting for transfers between devices, over_z(): lax.all_to_all(blocks, 'seq', 0, 0, axis_index_groups=groups, tiled=True)  6.97 us
    pallas_call x2, Pallas kernels, cross(): pl.pallas_call(body, out_shape=sds((SPAN, cols)), in_specs=[SMEM] + [ANY]...  6.71 us
    pallas_call x1, Pallas kernels, attend(): pl.pallas_call(attend_kernel, out_shape=sds((N_Z, tok, HEAD_DIM)), in_spe...  2.76 us
    pallas_call x1, Pallas kernels, encode(): pl.pallas_call(encode_kernel, out_shape=[sds((rows // 2, width))] * 2 + [...  2.57 us
    ppermute x1, starting transfers between devices, to_sides(): return lax.ppermute(block, ('seq', 'mp'), route)  2.48 us
  transfers between devices with their start and end apart: 23, of which 7 were waited for; matrix products, arithmetic and copies ran while one was open for 0% of the time, Pallas kernels for 22%

profile of v2, /device:TPU:1, one launch (start us, length us, event | category | flops | bytes accessed | tf_op | source)
XLA Modules:
  0.0 76.6 jit_solution(1743843392600163138)
XLA Ops:
  0.0 2.2 %pack.1 = (bf16[8,384,128]{2,1,0:T(8,128)(2,1)}, s32[4]{0:T(128)S(1)}, bf16[128,1024]{1,0:T(8,128)(2,1)S(1)}) custom-call(bf16[1,128,1024]{2,1,0:T(8,128)(2,1)} %q.1, bf16[1,128,1024]{2,1,0:T(8,128)(2,1)} %k.1, bf16[1,128,1024]{2,1,0:T(8,128)(2,1)} %v.1, bf16[256,1024]{1,0:T(8,128)(2,1)} %w0.1, s32[1,2,2]{2,1,0:T(2,128)} %nbr_rows.1, s32[1,2,2]{2,1,0:T(2,128)} %nbr_owner.1), custom_call_target="tpu_custom_call" | custom-call | flops 1000000000 | bytes 1024 | tf_op jit(solution)/shard_map/pack/pallas_call | solution.py:323
  2.2 9.0 %all-to-all-start = ((bf16[8,384,128]{2,1,0:T(8,128)(2,1)}), bf16[8,384,128]{2,1,0:T(8,128)(2,1)S(1)}, u32[]{:S(2)}, u32[]{:S(2)}) async-start(bf16[8,384,128]{2,1,0:T(8,128)(2,1)} %get-tuple-element.25), calls=%async_computation | async-start | bytes 1572864 | tf_op jit(solution)/shard_map/all_to_all | solution.py:53
  11.2 1.3 %collective-permute-start = (s32[4]{0:T(128)S(1)}, s32[4]{0:T(128)S(1)}, u32[]{:S(2)}, u32[]{:S(2)}) collective-permute-start(s32[4]{0:T(128)S(1)} %get-tuple-element.17.idx0.idx), channel_id=1, source_target_pairs={{0,64},{64,128},{128,192},{192,0},{1,65},{65,129},{129,193},{193,1... | collective-permute-start | bytes 56 | tf_op jit(solution)/shard_map/ppermute | solution.py:33
  12.5 2.6 %collective-permute-start.1 = (s32[4]{0:T(128)S(1)}, s32[4]{0:T(128)S(1)}, u32[]{:S(2)}, u32[]{:S(2)}) collective-permute-start(s32[4]{0:T(128)S(1)} %get-tuple-element.17.idx0.idx), channel_id=1, source_target_pairs={{0,128},{64,192},{128,0},{192,64},{1,129},{65,193},{129,1},{193,65... | collective-permute-start | bytes 56 | tf_op jit(solution)/shard_map/ppermute | solution.py:33
  15.1 1.1 %collective-permute-start.2 = (s32[4]{0:T(128)S(1)}, s32[4]{0:T(128)S(1)}, u32[]{:S(2)}, u32[]{:S(2)}) collective-permute-start(s32[4]{0:T(128)S(1)} %get-tuple-element.17.idx0.idx), channel_id=1, source_target_pairs={{0,192},{64,0},{128,64},{192,128},{1,193},{65,1},{129,65},{193,129... | collective-permute-start | bytes 56 | tf_op jit(solution)/shard_map/ppermute | solution.py:33
  16.2 2.5 %collective-permute-start.6 = (bf16[256,1024]{1,0:T(8,128)(2,1)S(1)}, bf16[256,1024]{1,0:T(8,128)(2,1)S(1)}, u32[]{:S(2)}, u32[]{:S(2)}) collective-permute-start(bf16[256,1024]{1,0:T(8,128)(2,1)S(1)} %copy-done.9), channel_id=1, source_target_pairs={{0,1},{1,2},{2,3},{3,0},{4,7},{5,4},{6,5},{7,6},{8,9},{9,10},{10,1... | collective-permute-start | bytes 1572872 | tf_op jit(solution)/shard_map/ppermute | solution.py:43
  19.2 1.8 %fetch.1 = (bf16[256,256]{1,0:T(8,128)(2,1)S(1)}, bf16[256,256]{1,0:T(8,128)(2,1)S(1)}, bf16[256,256]{1,0:T(8,128)(2,1)S(1)}, bf16[256,256]{1,0:T(8,128)(2,1)S(1)}) custom-call(s32[4]{0:T(128)S(1)} %get-tuple-element.17.idx0.idx, s32[4]{0:T(128)S(1)} %collective-permute-done.idx1, s32[4]{0:T(128)S(1)} %collective-permute-done.1.idx2, ...), custom_call_target="tpu_custom_call" | custom-call | flops 5000000000 | bytes 1024 | tf_op jit(solution)/shard_map/fetch/pallas_call | solution.py:119
  21.6 1.6 %collective-permute-start.4 = (bf16[256,256]{1,0:T(8,128)(2,1)S(1)}, bf16[256,256]{1,0:T(8,128)(2,1)S(1)}, u32[]{:S(2)}, u32[]{:S(2)}) collective-permute-start(bf16[256,256]{1,0:T(8,128)(2,1)S(1)} %get-tuple-element.20), channel_id=1, source_target_pairs={{0,128},{64,192},{128,0},{192,64},{1,129},{65,193},{129,1},{193,65... | collective-permute-start | bytes 393224 | tf_op jit(solution)/shard_map/ppermute | solution.py:33
  23.2 2.0 %collective-permute-done.3.r1 = bf16[256,256]{1,0:T(8,128)(2,1)S(1)} collective-permute-done((bf16[256,256]{1,0:T(8,128)(2,1)S(1)}, bf16[256,256]{1,0:T(8,128)(2,1)S(1)}, u32[]{:S(2)}, u32[]{:S(2)}) %collective-permute-start.3) | collective-permute-done | bytes 131104 | tf_op jit(solution)/shard_map/ppermute | solution.py:33
  25.2 2.0 %collective-permute-done.4.r2 = bf16[256,256]{1,0:T(8,128)(2,1)S(1)} collective-permute-done((bf16[256,256]{1,0:T(8,128)(2,1)S(1)}, bf16[256,256]{1,0:T(8,128)(2,1)S(1)}, u32[]{:S(2)}, u32[]{:S(2)}) %collective-permute-start.4) | collective-permute-done | bytes 131104 | tf_op jit(solution)/shard_map/ppermute | solution.py:33
  27.3 1.4 %collective-permute-done.5.r3 = bf16[256,256]{1,0:T(8,128)(2,1)S(1)} collective-permute-done((bf16[256,256]{1,0:T(8,128)(2,1)S(1)}, bf16[256,256]{1,0:T(8,128)(2,1)S(1)}, u32[]{:S(2)}, u32[]{:S(2)}) %collective-permute-start.5) | collective-permute-done | bytes 131104 | tf_op jit(solution)/shard_map/ppermute | solution.py:33
  28.7 1.8 %collective-permute-done.6.w1.w_near = bf16[256,1024]{1,0:T(8,128)(2,1)S(1)} collective-permute-done((bf16[256,1024]{1,0:T(8,128)(2,1)S(1)}, bf16[256,1024]{1,0:T(8,128)(2,1)S(1)}, u32[]{:S(2)}, u32[]{:S(2)}) %collective-permute-start.6) | collective-permute-done | bytes 524320 | tf_op jit(solution)/shard_map/ppermute | solution.py:43
  30.4 1.1 %compact.1.x0.refs_1_ = bf16[512,256]{1,0:T(8,128)(2,1)S(1)} custom-call(s32[4]{0:T(128)S(1)} %get-tuple-element.17.idx0.idx, bf16[256,256]{1,0:T(8,128)(2,1)S(1)} %get-tuple-element.18.r0, bf16[256,256]{1,0:T(8,128)(2,1)S(1)} %collective-permute-done.3.r1, bf16[256,256]{1,0:T(8,128)(2,1)S(1)} %collective-permute-done.4.r2, ...), custom_call_target="tpu_custom_call" | custom-call | flops 1000000000 | bytes 1024 | tf_op jit(solution)/shard_map/compact/pallas_call | solution.py:156
  31.6 3.2 %all-to-all-done.refs_0_ = bf16[8,384,128]{2,1,0:T(8,128)(2,1)S(1)} async-done(((bf16[8,384,128]{2,1,0:T(8,128)(2,1)}), bf16[8,384,128]{2,1,0:T(8,128)(2,1)S(1)}, u32[]{:S(2)}, u32[]{:S(2)}) %all-to-all-start) | async-done | bytes 786464 | tf_op jit(solution)/shard_map/all_to_all | solution.py:53
  34.8 1.0 %collective-permute-start.16 = (bf16[8,384,128]{2,1,0:T(8,128)(2,1)S(1)}, bf16[8,384,128]{2,1,0:T(8,128)(2,1)S(1)}, u32[]{:S(2)}, u32[]{:S(2)}) collective-permute-start(bf16[8,384,128]{2,1,0:T(8,128)(2,1)S(1)} %after.2.own), channel_id=1, source_target_pairs={{0,4},{4,0},{8,12},{12,8},{16,20},{20,16},{24,28},{28,24},{32,36},... | collective-permute-start | bytes 2359304 | tf_op jit(solution)/shard_map/ppermute | solution.py:48
  35.9 2.0 %collective-permute-start.10 = (bf16[512,256]{1,0:T(8,128)(2,1)S(1)}, bf16[512,256]{1,0:T(8,128)(2,1)}, u32[]{:S(2)}, u32[]{:S(2)}) collective-permute-start(bf16[512,256]{1,0:T(8,128)(2,1)S(1)} %compact.1.x0.refs_1_), channel_id=1, source_target_pairs={{0,3},{1,0},{2,1},{3,2},{4,7},{5,4},{6,5},{7,6},{8,11},{9,8},{10,9... | collective-permute-start | bytes 786440 | tf_op jit(solution)/shard_map/ppermute | solution.py:33
  38.0 1.7 %collective-permute-start.9 = (bf16[512,256]{1,0:T(8,128)(2,1)S(1)}, bf16[512,256]{1,0:T(8,128)(2,1)}, u32[]{:S(2)}, u32[]{:S(2)}) collective-permute-start(bf16[512,256]{1,0:T(8,128)(2,1)S(1)} %compact.1.x0.refs_1_), channel_id=1, source_target_pairs={{0,2},{1,3},{2,0},{3,1},{4,6},{5,7},{6,4},{7,5},{8,10},{9,11},{10,... | collective-permute-start | bytes 786440 | tf_op jit(solution)/shard_map/ppermute | solution.py:33
  39.7 1.2 %collective-permute-start.14 = (bf16[256,1024]{1,0:T(8,128)(2,1)S(1)}, bf16[256,1024]{1,0:T(8,128)(2,1)}, u32[]{:S(2)}, u32[]{:S(2)}) collective-permute-start(bf16[256,1024]{1,0:T(8,128)(2,1)S(1)} %collective-permute-done.6.w1.w_near), channel_id=1, source_target_pairs={{0,4},{4,0},{8,12},{12,8},{16,20},{20,16},{24,28},{28,24},{32,36},... | collective-permute-start | bytes 1572872 | tf_op jit(solution)/shard_map/ppermute | solution.py:48
  41.0 2.8 %attend.1 = bf16[8,128,128]{2,1,0:T(8,128)(2,1)} custom-call(bf16[8,384,128]{2,1,0:T(8,128)(2,1)S(1)} %after.2.own, bf16[8,384,128]{2,1,0:T(8,128)(2,1)S(1)} %collective-permute-done.16.other), custom_call_target="tpu_custom_call" | custom-call | flops 10000000000 | bytes 1024 | tf_op jit(solution)/shard_map/attend/pallas_call | solution.py:385
  43.7 5.1 %all-to-all-start.1 = ((bf16[8,128,128]{2,1,0:T(8,128)(2,1)}), bf16[8,128,128]{2,1,0:T(8,128)(2,1)S(1)}, u32[]{:S(2)}, u32[]{:S(2)}) async-start(bf16[8,128,128]{2,1,0:T(8,128)(2,1)} %attend.1), calls=%async_computation.1 | async-start | bytes 524288 | tf_op jit(solution)/shard_map/all_to_all | solution.py:53
  48.8 2.4 %collective-permute-done.9.x2 = bf16[512,256]{1,0:T(8,128)(2,1)} collective-permute-done((bf16[512,256]{1,0:T(8,128)(2,1)S(1)}, bf16[512,256]{1,0:T(8,128)(2,1)}, u32[]{:S(2)}, u32[]{:S(2)}) %collective-permute-start.9) | collective-permute-done | bytes 262176 | tf_op jit(solution)/shard_map/ppermute | solution.py:33
  51.2 2.6 %encode.1 = (bf16[256,256]{1,0:T(8,128)(2,1)S(1)}, bf16[256,256]{1,0:T(8,128)(2,1)S(1)}, bf16[512,1024]{1,0:T(8,128)(2,1)}) custom-call(bf16[512,256]{1,0:T(8,128)(2,1)S(1)} %compact.1.x0.refs_1_, bf16[512,256]{1,0:T(8,128)(2,1)} %collective-permute-done.8.x1, bf16[512,256]{1,0:T(8,128)(2,1)} %collective-permute-done.9.x2, ...), custom_call_target="tpu_custom_call" | custom-call | flops 30000001024 | bytes 1024 | tf_op jit(solution)/shard_map/encode/pallas_call | solution.py:207
  53.9 1.6 %collective-permute-start.12 = (bf16[256,256]{1,0:T(8,128)(2,1)S(1)}, bf16[256,256]{1,0:T(8,128)(2,1)S(1)}, u32[]{:S(2)}, u32[]{:S(2)}) collective-permute-start(bf16[256,256]{1,0:T(8,128)(2,1)S(1)} %get-tuple-element.24.refs_2_), channel_id=1, source_target_pairs={{0,2},{1,3},{2,0},{3,1},{4,6},{5,7},{6,4},{7,5},{8,10},{9,11},{10,... | collective-permute-start | bytes 393224 | tf_op jit(solution)/shard_map/ppermute | solution.py:33
  55.5 2.0 %collective-permute-start.13 = (bf16[256,256]{1,0:T(8,128)(2,1)S(1)}, bf16[256,256]{1,0:T(8,128)(2,1)S(1)}, u32[]{:S(2)}, u32[]{:S(2)}) collective-permute-start(bf16[256,256]{1,0:T(8,128)(2,1)S(1)} %get-tuple-element.24.refs_2_), channel_id=1, source_target_pairs={{0,3},{1,0},{2,1},{3,2},{4,7},{5,4},{6,5},{7,6},{8,11},{9,8},{10,9... | collective-permute-start | bytes 393224 | tf_op jit(solution)/shard_map/ppermute | solution.py:33
  57.4 3.7 %all-to-all-done.1.heads = bf16[8,128,128]{2,1,0:T(8,128)(2,1)S(1)} async-done(((bf16[8,128,128]{2,1,0:T(8,128)(2,1)}), bf16[8,128,128]{2,1,0:T(8,128)(2,1)S(1)}, u32[]{:S(2)}, u32[]{:S(2)}) %all-to-all-start.1) | async-done | bytes 262176 | tf_op jit(solution)/shard_map/all_to_all | solution.py:53
  61.4 1.7 %load.1.refs_6_.refs_1_ = bf16[1024,1024]{1,0:T(8,128)(2,1)S(1)} custom-call(bf16[256,1024]{1,0:T(8,128)(2,1)} %w0.1, bf16[256,1024]{1,0:T(8,128)(2,1)} %copy-done.5, bf16[128,1024]{1,0:T(8,128)(2,1)} %copy-done.7, bf16[256,1024]{1,0:T(8,128)(2,1)} %collective-permute-done.14.s_near, bf16[128,1024]{1,0:T(8,128)(2,1)} %collective-permute-done.15.s_half, ...), custom_call_target="tpu_custom_call" | custom-call | flops 3000000000 | bytes 1024 | tf_op jit(solution)/shard_map/load/pallas_call | solution.py:235
  63.2 1.9 %collective-permute-start.18 = (bf16[256,256]{1,0:T(8,128)(2,1)S(1)}, bf16[256,256]{1,0:T(8,128)(2,1)S(1)}, u32[]{:S(2)}, u32[]{:S(2)}) collective-permute-start(bf16[256,256]{1,0:T(8,128)(2,1)S(1)} %after.3.refs_2_), channel_id=1, source_target_pairs={{0,1},{1,2},{2,3},{3,0},{4,5},{5,6},{6,7},{7,4},{8,9},{9,10},{10,1... | collective-permute-start | bytes 393224 | tf_op jit(solution)/shard_map/ppermute | solution.py:33
  65.8 1.8 %collective-permute-start.20 = (bf16[256,256]{1,0:T(8,128)(2,1)S(1)}, bf16[256,256]{1,0:T(8,128)(2,1)S(1)}, u32[]{:S(2)}, u32[]{:S(2)}) collective-permute-start(bf16[256,256]{1,0:T(8,128)(2,1)S(1)} %after.3.refs_2_), channel_id=1, source_target_pairs={{0,3},{1,0},{2,1},{3,2},{4,7},{5,4},{6,5},{7,6},{8,11},{9,8},{10,9... | collective-permute-start | bytes 393224 | tf_op jit(solution)/shard_map/ppermute | solution.py:33
  67.6 3.4 %cross.2.second = bf16[64,1024]{1,0:T(8,128)(2,1)S(1)} custom-call(s32[1,32]{1,0:T(1,128)S(1)} %copy-done.8, bf16[512,1024]{1,0:T(8,128)(2,1)} %get-tuple-element.23.refs_1_, bf16[256,256]{1,0:T(8,128)(2,1)S(1)} %get-tuple-element.24.refs_2_, bf16[256,256]{1,0:T(8,128)(2,1)S(1)} %collective-permute-done.11.refs_3_, ...), custom_call_target="tpu_custom_call" | custom-call | flops 5000000000 | bytes 1024 | tf_op jit(solution)/shard_map/cross/pallas_call | solution.py:284
  71.0 1.5 %collective-permute-start.17 = (bf16[64,1024]{1,0:T(8,128)(2,1)S(1)}, bf16[64,1024]{1,0:T(8,128)(2,1)S(1)}, u32[]{:S(2)}, u32[]{:S(2)}) collective-permute-start(bf16[64,1024]{1,0:T(8,128)(2,1)S(1)} %cross.2.second), channel_id=1, source_target_pairs={{0,4},{4,8},{8,12},{12,16},{16,20},{20,24},{24,28},{28,32},{32,36}... | collective-permute-start | bytes 393224 | tf_op jit(solution)/shard_map/ppermute | solution.py:33
  72.5 3.4 %cross.3.first = bf16[64,1024]{1,0:T(8,128)(2,1)S(1)} custom-call(s32[1,32]{1,0:T(1,128)S(1)} %copy-done.8, bf16[512,1024]{1,0:T(8,128)(2,1)} %get-tuple-element.23.refs_1_, bf16[256,256]{1,0:T(8,128)(2,1)S(1)} %after.3.refs_2_, bf16[256,256]{1,0:T(8,128)(2,1)S(1)} %collective-permute-done.18.refs_3_, bf16[256,256]{1,0:T(8,128)(2,1)S(1)} %collective-permute-done.19.refs_4_, ...), custom_call_target="tpu_custom_call" | custom-call | flops 5000000000 | bytes 1024 | tf_op jit(solution)/shard_map/cross/pallas_call | solution.py:284
  75.8 0.8 %place.1 = bf16[1,128,1024]{2,1,0:T(8,128)(2,1)} custom-call(bf16[64,1024]{1,0:T(8,128)(2,1)S(1)} %collective-permute-done.17.received, bf16[64,1024]{1,0:T(8,128)(2,1)S(1)} %cross.3.first, bf16[64,1024]{1,0:T(8,128)(2,1)S(1)} %cross.2.second), custom_call_target="tpu_custom_call" | custom-call | flops 1000000000 | bytes 1024 | tf_op jit(solution)/shard_map/place/pallas_call | solution.py:424
  (46 shorter events, 2.4 us)
Async XLA Ops:
  0.0 16.2 %copy-start.9 = (bf16[256,1024]{1,0:T(8,128)(2,1)S(1)}, bf16[256,1024]{1,0:T(8,128)(2,1)}, u32[]{:S(2)}) copy-start(bf16[256,1024]{1,0:T(8,128)(2,1)} %w0.1) | copy-start | bytes 1572868
  2.2 32.6 %all-to-all-start = ((bf16[8,384,128]{2,1,0:T(8,128)(2,1)}), bf16[8,384,128]{2,1,0:T(8,128)(2,1)S(1)}, u32[]{:S(2)}, u32[]{:S(2)}) async-start(bf16[8,384,128]{2,1,0:T(8,128)(2,1)} %get-tuple-element.25), calls=%async_computation | async-start | bytes 1572864 | tf_op jit(solution)/shard_map/all_to_all | solution.py:53
  11.2 8.0 %collective-permute-start = (s32[4]{0:T(128)S(1)}, s32[4]{0:T(128)S(1)}, u32[]{:S(2)}, u32[]{:S(2)}) collective-permute-start(s32[4]{0:T(128)S(1)} %get-tuple-element.17.idx0.idx), channel_id=1, source_target_pairs={{0,64},{64,128},{128,192},{192,0},{1,65},{65,129},{129,193},{193,1... | collective-permute-start | bytes 56 | tf_op jit(solution)/shard_map/ppermute | solution.py:33
  12.5 6.7 %collective-permute-start.1 = (s32[4]{0:T(128)S(1)}, s32[4]{0:T(128)S(1)}, u32[]{:S(2)}, u32[]{:S(2)}) collective-permute-start(s32[4]{0:T(128)S(1)} %get-tuple-element.17.idx0.idx), channel_id=1, source_target_pairs={{0,128},{64,192},{128,0},{192,64},{1,129},{65,193},{129,1},{193,65... | collective-permute-start | bytes 56 | tf_op jit(solution)/shard_map/ppermute | solution.py:33
  15.1 4.1 %collective-permute-start.2 = (s32[4]{0:T(128)S(1)}, s32[4]{0:T(128)S(1)}, u32[]{:S(2)}, u32[]{:S(2)}) collective-permute-start(s32[4]{0:T(128)S(1)} %get-tuple-element.17.idx0.idx), channel_id=1, source_target_pairs={{0,192},{64,0},{128,64},{192,128},{1,193},{65,1},{129,65},{193,129... | collective-permute-start | bytes 56 | tf_op jit(solution)/shard_map/ppermute | solution.py:33
  16.2 14.2 %collective-permute-start.6 = (bf16[256,1024]{1,0:T(8,128)(2,1)S(1)}, bf16[256,1024]{1,0:T(8,128)(2,1)S(1)}, u32[]{:S(2)}, u32[]{:S(2)}) collective-permute-start(bf16[256,1024]{1,0:T(8,128)(2,1)S(1)} %copy-done.9), channel_id=1, source_target_pairs={{0,1},{1,2},{2,3},{3,0},{4,7},{5,4},{6,5},{7,6},{8,9},{9,10},{10,1... | collective-permute-start | bytes 1572872 | tf_op jit(solution)/shard_map/ppermute | solution.py:43
  18.7 10.0 %collective-permute-start.7 = (bf16[128,1024]{1,0:T(8,128)(2,1)S(1)}, bf16[128,1024]{1,0:T(8,128)(2,1)S(1)}, u32[]{:S(2)}, u32[]{:S(2)}) collective-permute-start(bf16[128,1024]{1,0:T(8,128)(2,1)S(1)} %get-tuple-element.22), channel_id=1, source_target_pairs={{0,2},{1,3},{2,0},{3,1},{4,6},{5,7},{6,4},{7,5},{8,10},{9,11},{10,... | collective-permute-start | bytes 786440 | tf_op jit(solution)/shard_map/ppermute | solution.py:33
  21.0 4.2 %collective-permute-start.3 = (bf16[256,256]{1,0:T(8,128)(2,1)S(1)}, bf16[256,256]{1,0:T(8,128)(2,1)S(1)}, u32[]{:S(2)}, u32[]{:S(2)}) collective-permute-start(bf16[256,256]{1,0:T(8,128)(2,1)S(1)} %get-tuple-element.19), channel_id=1, source_target_pairs={{0,192},{64,0},{128,64},{192,128},{1,193},{65,1},{129,65},{193,129... | collective-permute-start | bytes 393224 | tf_op jit(solution)/shard_map/ppermute | solution.py:33
  21.6 5.6 %collective-permute-start.4 = (bf16[256,256]{1,0:T(8,128)(2,1)S(1)}, bf16[256,256]{1,0:T(8,128)(2,1)S(1)}, u32[]{:S(2)}, u32[]{:S(2)}) collective-permute-start(bf16[256,256]{1,0:T(8,128)(2,1)S(1)} %get-tuple-element.20), channel_id=1, source_target_pairs={{0,128},{64,192},{128,0},{192,64},{1,129},{65,193},{129,1},{193,65... | collective-permute-start | bytes 393224 | tf_op jit(solution)/shard_map/ppermute | solution.py:33
  23.2 5.4 %collective-permute-start.5 = (bf16[256,256]{1,0:T(8,128)(2,1)S(1)}, bf16[256,256]{1,0:T(8,128)(2,1)S(1)}, u32[]{:S(2)}, u32[]{:S(2)}) collective-permute-start(bf16[256,256]{1,0:T(8,128)(2,1)S(1)} %get-tuple-element.21), channel_id=1, source_target_pairs={{0,64},{64,128},{128,192},{192,0},{1,65},{65,129},{129,193},{193,1... | collective-permute-start | bytes 393224 | tf_op jit(solution)/shard_map/ppermute | solution.py:33
  28.7 7.2 %copy-start.7 = (bf16[128,1024]{1,0:T(8,128)(2,1)}, bf16[128,1024]{1,0:T(8,128)(2,1)S(1)}, u32[]{:S(2)}) copy-start(bf16[128,1024]{1,0:T(8,128)(2,1)S(1)} %collective-permute-done.7.w2.w_half) | copy-start | bytes 786436
  30.4 9.3 %copy-start.5 = (bf16[256,1024]{1,0:T(8,128)(2,1)}, bf16[256,1024]{1,0:T(8,128)(2,1)S(1)}, u32[]{:S(2)}) copy-start(bf16[256,1024]{1,0:T(8,128)(2,1)S(1)} %collective-permute-done.6.w1.w_near) | copy-start | bytes 1572868
  34.8 16.4 %copy-start.2 = (bf16[1024,256]{1,0:T(8,128)(2,1)S(1)}, bf16[1024,256]{1,0:T(8,128)(2,1)}, u32[]{:S(2)}) copy-start(bf16[1024,256]{1,0:T(8,128)(2,1)} %wq.2) | copy-start | bytes 1572868
  34.8 16.4 %copy-start.3 = (bf16[1024,256]{1,0:T(8,128)(2,1)S(1)}, bf16[1024,256]{1,0:T(8,128)(2,1)}, u32[]{:S(2)}) copy-start(bf16[1024,256]{1,0:T(8,128)(2,1)} %wk.1) | copy-start | bytes 1572868
  34.8 16.4 %copy-start.4 = (bf16[1024,256]{1,0:T(8,128)(2,1)S(1)}, bf16[1024,256]{1,0:T(8,128)(2,1)}, u32[]{:S(2)}) copy-start(bf16[1024,256]{1,0:T(8,128)(2,1)} %wv.1) | copy-start | bytes 1572868
  34.8 4.9 %collective-permute-start.16 = (bf16[8,384,128]{2,1,0:T(8,128)(2,1)S(1)}, bf16[8,384,128]{2,1,0:T(8,128)(2,1)S(1)}, u32[]{:S(2)}, u32[]{:S(2)}) collective-permute-start(bf16[8,384,128]{2,1,0:T(8,128)(2,1)S(1)} %after.2.own), channel_id=1, source_target_pairs={{0,4},{4,0},{8,12},{12,8},{16,20},{20,16},{24,28},{28,24},{32,36},... | collective-permute-start | bytes 2359304 | tf_op jit(solution)/shard_map/ppermute | solution.py:48
  35.8 25.6 %collective-permute-start.15 = (bf16[128,1024]{1,0:T(8,128)(2,1)S(1)}, bf16[128,1024]{1,0:T(8,128)(2,1)}, u32[]{:S(2)}, u32[]{:S(2)}) collective-permute-start(bf16[128,1024]{1,0:T(8,128)(2,1)S(1)} %collective-permute-done.7.w2.w_half), channel_id=1, source_target_pairs={{0,4},{4,0},{8,12},{12,8},{16,20},{20,16},{24,28},{28,24},{32,36},... | collective-permute-start | bytes 786440 | tf_op jit(solution)/shard_map/ppermute | solution.py:48
  35.9 12.9 %collective-permute-start.10 = (bf16[512,256]{1,0:T(8,128)(2,1)S(1)}, bf16[512,256]{1,0:T(8,128)(2,1)}, u32[]{:S(2)}, u32[]{:S(2)}) collective-permute-start(bf16[512,256]{1,0:T(8,128)(2,1)S(1)} %compact.1.x0.refs_1_), channel_id=1, source_target_pairs={{0,3},{1,0},{2,1},{3,2},{4,7},{5,4},{6,5},{7,6},{8,11},{9,8},{10,9... | collective-permute-start | bytes 786440 | tf_op jit(solution)/shard_map/ppermute | solution.py:33
  38.0 10.8 %collective-permute-start.8 = (bf16[512,256]{1,0:T(8,128)(2,1)S(1)}, bf16[512,256]{1,0:T(8,128)(2,1)}, u32[]{:S(2)}, u32[]{:S(2)}) collective-permute-start(bf16[512,256]{1,0:T(8,128)(2,1)S(1)} %compact.1.x0.refs_1_), channel_id=1, source_target_pairs={{0,1},{1,2},{2,3},{3,0},{4,5},{5,6},{6,7},{7,4},{8,9},{9,10},{10,1... | collective-permute-start | bytes 786440 | tf_op jit(solution)/shard_map/ppermute | solution.py:33
  38.0 13.2 %collective-permute-start.9 = (bf16[512,256]{1,0:T(8,128)(2,1)S(1)}, bf16[512,256]{1,0:T(8,128)(2,1)}, u32[]{:S(2)}, u32[]{:S(2)}) collective-permute-start(bf16[512,256]{1,0:T(8,128)(2,1)S(1)} %compact.1.x0.refs_1_), channel_id=1, source_target_pairs={{0,2},{1,3},{2,0},{3,1},{4,6},{5,7},{6,4},{7,5},{8,10},{9,11},{10,... | collective-permute-start | bytes 786440 | tf_op jit(solution)/shard_map/ppermute | solution.py:33
  39.7 21.7 %collective-permute-start.14 = (bf16[256,1024]{1,0:T(8,128)(2,1)S(1)}, bf16[256,1024]{1,0:T(8,128)(2,1)}, u32[]{:S(2)}, u32[]{:S(2)}) collective-permute-start(bf16[256,1024]{1,0:T(8,128)(2,1)S(1)} %collective-permute-done.6.w1.w_near), channel_id=1, source_target_pairs={{0,4},{4,0},{8,12},{12,8},{16,20},{20,16},{24,28},{28,24},{32,36},... | collective-permute-start | bytes 1572872 | tf_op jit(solution)/shard_map/ppermute | solution.py:48
  43.7 17.4 %all-to-all-start.1 = ((bf16[8,128,128]{2,1,0:T(8,128)(2,1)}), bf16[8,128,128]{2,1,0:T(8,128)(2,1)S(1)}, u32[]{:S(2)}, u32[]{:S(2)}) async-start(bf16[8,128,128]{2,1,0:T(8,128)(2,1)} %attend.1), calls=%async_computation.1 | async-start | bytes 524288 | tf_op jit(solution)/shard_map/all_to_all | solution.py:53
  48.8 12.4 %copy-start.6 = (bf16[8,128,128]{2,1,0:T(8,128)(2,1)S(1)}, bf16[8,128,128]{2,1,0:T(8,128)(2,1)}, u32[]{:S(2)}) copy-start(bf16[8,128,128]{2,1,0:T(8,128)(2,1)} %wq.3) | copy-start | bytes 786436
  53.8 12.1 %collective-permute-start.11 = (bf16[256,256]{1,0:T(8,128)(2,1)S(1)}, bf16[256,256]{1,0:T(8,128)(2,1)S(1)}, u32[]{:S(2)}, u32[]{:S(2)}) collective-permute-start(bf16[256,256]{1,0:T(8,128)(2,1)S(1)} %get-tuple-element.24.refs_2_), channel_id=1, source_target_pairs={{0,1},{1,2},{2,3},{3,0},{4,5},{5,6},{6,7},{7,4},{8,9},{9,10},{10,1... | collective-permute-start | bytes 393224 | tf_op jit(solution)/shard_map/ppermute | solution.py:33
  53.9 13.7 %collective-permute-start.12 = (bf16[256,256]{1,0:T(8,128)(2,1)S(1)}, bf16[256,256]{1,0:T(8,128)(2,1)S(1)}, u32[]{:S(2)}, u32[]{:S(2)}) collective-permute-start(bf16[256,256]{1,0:T(8,128)(2,1)S(1)} %get-tuple-element.24.refs_2_), channel_id=1, source_target_pairs={{0,2},{1,3},{2,0},{3,1},{4,6},{5,7},{6,4},{7,5},{8,10},{9,11},{10,... | collective-permute-start | bytes 393224 | tf_op jit(solution)/shard_map/ppermute | solution.py:33
  55.5 12.1 %collective-permute-start.13 = (bf16[256,256]{1,0:T(8,128)(2,1)S(1)}, bf16[256,256]{1,0:T(8,128)(2,1)S(1)}, u32[]{:S(2)}, u32[]{:S(2)}) collective-permute-start(bf16[256,256]{1,0:T(8,128)(2,1)S(1)} %get-tuple-element.24.refs_2_), channel_id=1, source_target_pairs={{0,3},{1,0},{2,1},{3,2},{4,7},{5,4},{6,5},{7,6},{8,11},{9,8},{10,9... | collective-permute-start | bytes 393224 | tf_op jit(solution)/shard_map/ppermute | solution.py:33
  61.4 6.1 %copy-start.1 = (bf16[1024,1024]{1,0:T(8,128)(2,1)S(1)}, bf16[1024,1024]{1,0:T(8,128)(2,1)}, u32[]{:S(2)}) copy-start(bf16[1024,1024]{1,0:T(8,128)(2,1)} %refs_8_.3) | copy-start | bytes 6291460
  63.1 4.4 %copy-start = (bf16[1024,1024]{1,0:T(8,128)(2,1)S(1)}, bf16[1024,1024]{1,0:T(8,128)(2,1)}, u32[]{:S(2)}) copy-start(bf16[1024,1024]{1,0:T(8,128)(2,1)} %refs_7_.3) | copy-start | bytes 6291460
  63.2 9.3 %collective-permute-start.18 = (bf16[256,256]{1,0:T(8,128)(2,1)S(1)}, bf16[256,256]{1,0:T(8,128)(2,1)S(1)}, u32[]{:S(2)}, u32[]{:S(2)}) collective-permute-start(bf16[256,256]{1,0:T(8,128)(2,1)S(1)} %after.3.refs_2_), channel_id=1, source_target_pairs={{0,1},{1,2},{2,3},{3,0},{4,5},{5,6},{6,7},{7,4},{8,9},{9,10},{10,1... | collective-permute-start | bytes 393224 | tf_op jit(solution)/shard_map/ppermute | solution.py:33
  65.1 7.4 %collective-permute-start.19 = (bf16[256,256]{1,0:T(8,128)(2,1)S(1)}, bf16[256,256]{1,0:T(8,128)(2,1)S(1)}, u32[]{:S(2)}, u32[]{:S(2)}) collective-permute-start(bf16[256,256]{1,0:T(8,128)(2,1)S(1)} %after.3.refs_2_), channel_id=1, source_target_pairs={{0,2},{1,3},{2,0},{3,1},{4,6},{5,7},{6,4},{7,5},{8,10},{9,11},{10,... | collective-permute-start | bytes 393224 | tf_op jit(solution)/shard_map/ppermute | solution.py:33
  65.8 6.6 %collective-permute-start.20 = (bf16[256,256]{1,0:T(8,128)(2,1)S(1)}, bf16[256,256]{1,0:T(8,128)(2,1)S(1)}, u32[]{:S(2)}, u32[]{:S(2)}) collective-permute-start(bf16[256,256]{1,0:T(8,128)(2,1)S(1)} %after.3.refs_2_), channel_id=1, source_target_pairs={{0,3},{1,0},{2,1},{3,2},{4,7},{5,4},{6,5},{7,6},{8,11},{9,8},{10,9... | collective-permute-start | bytes 393224 | tf_op jit(solution)/shard_map/ppermute | solution.py:33
  71.0 4.9 %collective-permute-start.17 = (bf16[64,1024]{1,0:T(8,128)(2,1)S(1)}, bf16[64,1024]{1,0:T(8,128)(2,1)S(1)}, u32[]{:S(2)}, u32[]{:S(2)}) collective-permute-start(bf16[64,1024]{1,0:T(8,128)(2,1)S(1)} %cross.2.second), channel_id=1, source_target_pairs={{0,4},{4,8},{8,12},{12,16},{16,20},{20,24},{24,28},{28,32},{32,36}... | collective-permute-start | bytes 393224 | tf_op jit(solution)/shard_map/ppermute | solution.py:33
  (1 other events, 4.4 us)

commit v3 on v2

--- a/solution.py
+++ b/solution.py
@@ -48,8 +48,12 @@
     return lax.ppermute(block, "seq", [(i, i ^ 1) for i in range(size)])
 
 
+def turned(z):
+    return (z + 1) % N_Z
+
+
 def over_z(blocks):
-    groups = [[2 * z + core for z in range(N_Z)] for core in range(2)]
+    groups = [[2 * (n - 1) % (2 * N_Z) + core for n in range(N_Z)] for core in range(2)]
     return lax.all_to_all(blocks, "seq", 0, 0, axis_index_groups=groups, tiled=True)
 
 
@@ -314,7 +318,7 @@
         c.wait()
         for head in range(N_Z):
             cols = slice(head * HEAD_DIM, (head + 1) * HEAD_DIM)
-            out[head, n * tok : (n + 1) * tok, :] = rows[n, :, cols]
+            out[turned(head), n * tok : (n + 1) * tok, :] = rows[n, :, cols]
     copies[3].wait()
 
 
@@ -346,18 +350,23 @@
     tok = out.shape[1]
     tokens = 2 * N_Z * tok
 
+    def rows_of(ref, n, kind):
+        at = slice(kind * tok, (kind + 1) * tok)
+        rows = ref[1 : n + 1, at].reshape(-1, HEAD_DIM)
+        return rows if n < N_Z else jnp.concatenate([rows, ref[0, at]], axis=0)
+
     def block_parts(z):
-        after_z = (z + 1) % N_Z
-        nxt = jnp.where(core == 0, other[z, :SPAN].astype(F32), other[after_z, :SPAN].astype(F32))
-        both = jnp.concatenate([own[z, :tok].astype(F32), nxt], axis=0)
+        here, after_z = turned(z), turned(turned(z))
+        nxt = jnp.where(core == 0, other[here, :SPAN].astype(F32), other[after_z, :SPAN].astype(F32))
+        both = jnp.concatenate([own[here, :tok].astype(F32), nxt], axis=0)
         rolled = pltpu.roll(both, both.shape[0] - (SPAN - 1), 0)[:tok].astype(BF)
         pos = (2 * z + core) * tok + SPAN - 1 + lax.broadcasted_iota(jnp.int32, (tok, 1), 0)
         pos = jnp.where(pos >= tokens, pos - tokens, pos)
         col = lax.broadcasted_iota(jnp.int32, (1, tok), 1)
         parts, values = [], []
         for n, ref, parity in ((z + 1, own, core), (min(z + 2, N_Z), other, 1 - core)):
-            s = dot_t(rolled, ref[:n, tok : 2 * tok].reshape(n * tok, HEAD_DIM))
-            values.append(ref[:n, 2 * tok :].reshape(n * tok, HEAD_DIM))
+            s = dot_t(rolled, rows_of(ref, n, 1))
+            values.append(rows_of(ref, n, 2))
             for b in range(n):
                 piece = s[:, b * tok : (b + 1) * tok]
                 if b >= z or z == N_Z - 1:
@@ -376,7 +385,7 @@
             split = mine.shape[0]
             mixes.append(dot(p[:, :split], mine) + dot(p[:, split:], theirs))
         for z, mix, total in zip(group, mixes, totals):
-            out[z] = (mix / total).astype(BF)
+            out[turned(z)] = (mix / total).astype(BF)
 
 
 def attend(own, other):
@@ -396,8 +405,9 @@
 def query_kernel(heads, wq, so, cq):
     for h in range(N_Z):
         cols = slice(h * HEAD_DIM, (h + 1) * HEAD_DIM)
-        so[:, cols] = heads[h]
-        cq[:, cols] = dot(heads[h], wq[h]).astype(BF)
+        value = heads[turned(h)]
+        so[:, cols] = value
+        cq[:, cols] = dot(value, wq[h]).astype(BF)
 
 
 def cross_queries(heads, wq):

time: 77.1 us -> 75.5 us (0.979)
  waiting for transfers between devices: 16.6 us -> 8.01 us
  starting transfers between devices: 39.9 us -> 47 us
    all_to_all x2, waiting for transfers between devices: 6.97 us -> 0.01 us  [over_z(): lax.all_to_all(blocks, 'seq', 0, 0, axis_index_groups=groups, tiled=True)]
    ppermute x3, starting transfers between devices: 2.36 us -> 5.54 us  [core_swap(): return lax.ppermute(block, 'seq', [(i, i ^ 1) for i in range(size)])]
    all_to_all x2, starting transfers between devices: 14.1 us -> 16.5 us  [over_z(): lax.all_to_all(blocks, 'seq', 0, 0, axis_index_groups=groups, tiled=True)]
    ppermute x17, waiting for transfers between devices: 7.81 us -> 6.21 us  [shifted(): lax.ppermute(block, axis, [(i, (i + distance) % size) for i in range(size)])]
    ppermute x17, starting transfers between devices: 21 us -> 22.4 us  [shifted(): lax.ppermute(block, axis, [(i, (i + distance) % size) for i in range(size)])]
  transfers between devices with their start and end apart: 23 -> 23, of which waited for: 7 -> 5; matrix products, arithmetic and copies ran while one was open for 0% -> 0% of each run, Pallas kernels for 22% -> 22%
where the time goes in v3:
time: 75.5 us; the launch traced here: 75.1 us
  starting transfers between devices  47 us (62%)
  Pallas kernels  19.8 us (26%)
  waiting for transfers between devices  8.01 us (11%)
    ppermute x17, starting transfers between devices, shifted(): lax.ppermute(block, axis, [(i, (i + distance) % size) for i in range(size)])  22.4 us
    all_to_all x2, starting transfers between devices, over_z(): lax.all_to_all(blocks, 'seq', 0, 0, axis_index_groups=groups, tiled=True)  16.5 us
    pallas_call x2, Pallas kernels, cross(): pl.pallas_call(body, out_shape=sds((SPAN, cols)), in_specs=[SMEM] + [ANY]...  6.72 us
    ppermute x17, waiting for transfers between devices, shifted(): lax.ppermute(block, axis, [(i, (i + distance) % size) for i in range(size)])  6.21 us
    ppermute x3, starting transfers between devices, core_swap(): return lax.ppermute(block, 'seq', [(i, i ^ 1) for i in range(size)])  5.54 us
    pallas_call x1, Pallas kernels, attend(): pl.pallas_call(attend_kernel, out_shape=sds((N_Z, tok, HEAD_DIM)), in_spe...  2.76 us
    pallas_call x1, Pallas kernels, encode(): pl.pallas_call(encode_kernel, out_shape=[sds((rows // 2, width))] * 2 + [...  2.57 us
    ppermute x1, starting transfers between devices, to_sides(): return lax.ppermute(block, ('seq', 'mp'), route)  2.48 us
  transfers between devices with their start and end apart: 23, of which 5 were waited for; matrix products, arithmetic and copies ran while one was open for 0% of the time, Pallas kernels for 22%

profile of v3, /device:TPU:1, one launch (start us, length us, event | category | flops | bytes accessed | tf_op | source)
XLA Modules:
  0.0 75.1 jit_solution(8269244311282851150)
XLA Ops:
  0.0 2.2 %pack.1 = (bf16[8,384,128]{2,1,0:T(8,128)(2,1)}, s32[4]{0:T(128)S(1)}, bf16[128,1024]{1,0:T(8,128)(2,1)S(1)}) custom-call(bf16[1,128,1024]{2,1,0:T(8,128)(2,1)} %q.1, bf16[1,128,1024]{2,1,0:T(8,128)(2,1)} %k.1, bf16[1,128,1024]{2,1,0:T(8,128)(2,1)} %v.1, bf16[256,1024]{1,0:T(8,128)(2,1)} %w0.1, s32[1,2,2]{2,1,0:T(2,128)} %nbr_rows.1, s32[1,2,2]{2,1,0:T(2,128)} %nbr_owner.1), custom_call_target="tpu_custom_call" | custom-call | flops 1000000000 | bytes 1024 | tf_op jit(solution)/shard_map/pack/pallas_call | solution.py:327
  2.2 9.9 %all-to-all-start = ((bf16[8,384,128]{2,1,0:T(8,128)(2,1)}), bf16[8,384,128]{2,1,0:T(8,128)(2,1)S(1)}, u32[]{:S(2)}, u32[]{:S(2)}) async-start(bf16[8,384,128]{2,1,0:T(8,128)(2,1)} %get-tuple-element.25), calls=%async_computation | async-start | bytes 1572864 | tf_op jit(solution)/shard_map/all_to_all | solution.py:57
  12.1 1.3 %collective-permute-start = (s32[4]{0:T(128)S(1)}, s32[4]{0:T(128)S(1)}, u32[]{:S(2)}, u32[]{:S(2)}) collective-permute-start(s32[4]{0:T(128)S(1)} %get-tuple-element.17.idx0.idx), channel_id=1, source_target_pairs={{0,64},{64,128},{128,192},{192,0},{1,65},{65,129},{129,193},{193,1... | collective-permute-start | bytes 56 | tf_op jit(solution)/shard_map/ppermute | solution.py:33
  13.4 2.6 %collective-permute-start.1 = (s32[4]{0:T(128)S(1)}, s32[4]{0:T(128)S(1)}, u32[]{:S(2)}, u32[]{:S(2)}) collective-permute-start(s32[4]{0:T(128)S(1)} %get-tuple-element.17.idx0.idx), channel_id=1, source_target_pairs={{0,128},{64,192},{128,0},{192,64},{1,129},{65,193},{129,1},{193,65... | collective-permute-start | bytes 56 | tf_op jit(solution)/shard_map/ppermute | solution.py:33
  16.0 1.1 %collective-permute-start.2 = (s32[4]{0:T(128)S(1)}, s32[4]{0:T(128)S(1)}, u32[]{:S(2)}, u32[]{:S(2)}) collective-permute-start(s32[4]{0:T(128)S(1)} %get-tuple-element.17.idx0.idx), channel_id=1, source_target_pairs={{0,192},{64,0},{128,64},{192,128},{1,193},{65,1},{129,65},{193,129... | collective-permute-start | bytes 56 | tf_op jit(solution)/shard_map/ppermute | solution.py:33
  17.1 2.5 %collective-permute-start.6 = (bf16[256,1024]{1,0:T(8,128)(2,1)S(1)}, bf16[256,1024]{1,0:T(8,128)(2,1)S(1)}, u32[]{:S(2)}, u32[]{:S(2)}) collective-permute-start(bf16[256,1024]{1,0:T(8,128)(2,1)S(1)} %copy-done.9), channel_id=1, source_target_pairs={{0,1},{1,2},{2,3},{3,0},{4,7},{5,4},{6,5},{7,6},{8,9},{9,10},{10,1... | collective-permute-start | bytes 1572872 | tf_op jit(solution)/shard_map/ppermute | solution.py:43
  20.1 1.8 %fetch.1 = (bf16[256,256]{1,0:T(8,128)(2,1)S(1)}, bf16[256,256]{1,0:T(8,128)(2,1)S(1)}, bf16[256,256]{1,0:T(8,128)(2,1)S(1)}, bf16[256,256]{1,0:T(8,128)(2,1)S(1)}) custom-call(s32[4]{0:T(128)S(1)} %get-tuple-element.17.idx0.idx, s32[4]{0:T(128)S(1)} %collective-permute-done.idx1, s32[4]{0:T(128)S(1)} %collective-permute-done.1.idx2, ...), custom_call_target="tpu_custom_call" | custom-call | flops 5000000000 | bytes 1024 | tf_op jit(solution)/shard_map/fetch/pallas_call | solution.py:123
  21.8 0.6 collective-permute-start.3
  22.5 1.6 %collective-permute-start.4 = (bf16[256,256]{1,0:T(8,128)(2,1)S(1)}, bf16[256,256]{1,0:T(8,128)(2,1)S(1)}, u32[]{:S(2)}, u32[]{:S(2)}) collective-permute-start(bf16[256,256]{1,0:T(8,128)(2,1)S(1)} %get-tuple-element.20), channel_id=1, source_target_pairs={{0,128},{64,192},{128,0},{192,64},{1,129},{65,193},{129,1},{193,65... | collective-permute-start | bytes 393224 | tf_op jit(solution)/shard_map/ppermute | solution.py:33
  24.1 1.9 %collective-permute-done.3.r1 = bf16[256,256]{1,0:T(8,128)(2,1)S(1)} collective-permute-done((bf16[256,256]{1,0:T(8,128)(2,1)S(1)}, bf16[256,256]{1,0:T(8,128)(2,1)S(1)}, u32[]{:S(2)}, u32[]{:S(2)}) %collective-permute-start.3) | collective-permute-done | bytes 131104 | tf_op jit(solution)/shard_map/ppermute | solution.py:33
  26.0 1.9 %collective-permute-done.4.r2 = bf16[256,256]{1,0:T(8,128)(2,1)S(1)} collective-permute-done((bf16[256,256]{1,0:T(8,128)(2,1)S(1)}, bf16[256,256]{1,0:T(8,128)(2,1)S(1)}, u32[]{:S(2)}, u32[]{:S(2)}) %collective-permute-start.4) | collective-permute-done | bytes 131104 | tf_op jit(solution)/shard_map/ppermute | solution.py:33
  27.9 1.6 %collective-permute-done.5.r3 = bf16[256,256]{1,0:T(8,128)(2,1)S(1)} collective-permute-done((bf16[256,256]{1,0:T(8,128)(2,1)S(1)}, bf16[256,256]{1,0:T(8,128)(2,1)S(1)}, u32[]{:S(2)}, u32[]{:S(2)}) %collective-permute-start.5) | collective-permute-done | bytes 131104 | tf_op jit(solution)/shard_map/ppermute | solution.py:33
  29.5 1.8 %collective-permute-done.6.w1.w_near = bf16[256,1024]{1,0:T(8,128)(2,1)S(1)} collective-permute-done((bf16[256,1024]{1,0:T(8,128)(2,1)S(1)}, bf16[256,1024]{1,0:T(8,128)(2,1)S(1)}, u32[]{:S(2)}, u32[]{:S(2)}) %collective-permute-start.6) | collective-permute-done | bytes 524320 | tf_op jit(solution)/shard_map/ppermute | solution.py:43
  31.3 1.1 %compact.1.x0.refs_1_ = bf16[512,256]{1,0:T(8,128)(2,1)S(1)} custom-call(s32[4]{0:T(128)S(1)} %get-tuple-element.17.idx0.idx, bf16[256,256]{1,0:T(8,128)(2,1)S(1)} %get-tuple-element.18.r0, bf16[256,256]{1,0:T(8,128)(2,1)S(1)} %collective-permute-done.3.r1, bf16[256,256]{1,0:T(8,128)(2,1)S(1)} %collective-permute-done.4.r2, ...), custom_call_target="tpu_custom_call" | custom-call | flops 1000000000 | bytes 1024 | tf_op jit(solution)/shard_map/compact/pallas_call | solution.py:160
  32.5 4.2 %collective-permute-start.16 = (bf16[8,384,128]{2,1,0:T(8,128)(2,1)S(1)}, bf16[8,384,128]{2,1,0:T(8,128)(2,1)S(1)}, u32[]{:S(2)}, u32[]{:S(2)}) collective-permute-start(bf16[8,384,128]{2,1,0:T(8,128)(2,1)S(1)} %after.2.own), channel_id=1, source_target_pairs={{0,4},{4,0},{8,12},{12,8},{16,20},{20,16},{24,28},{28,24},{32,36},... | collective-permute-start | bytes 2359304 | tf_op jit(solution)/shard_map/ppermute | solution.py:48
  37.2 1.1 %collective-permute-start.8 = (bf16[512,256]{1,0:T(8,128)(2,1)S(1)}, bf16[512,256]{1,0:T(8,128)(2,1)}, u32[]{:S(2)}, u32[]{:S(2)}) collective-permute-start(bf16[512,256]{1,0:T(8,128)(2,1)S(1)} %compact.1.x0.refs_1_), channel_id=1, source_target_pairs={{0,1},{1,2},{2,3},{3,0},{4,5},{5,6},{6,7},{7,4},{8,9},{9,10},{10,1... | collective-permute-start | bytes 786440 | tf_op jit(solution)/shard_map/ppermute | solution.py:33
  38.2 0.5 collective-permute-start.9
  38.8 1.2 %collective-permute-start.14 = (bf16[256,1024]{1,0:T(8,128)(2,1)S(1)}, bf16[256,1024]{1,0:T(8,128)(2,1)}, u32[]{:S(2)}, u32[]{:S(2)}) collective-permute-start(bf16[256,1024]{1,0:T(8,128)(2,1)S(1)} %collective-permute-done.6.w1.w_near), channel_id=1, source_target_pairs={{0,4},{4,0},{8,12},{12,8},{16,20},{20,16},{24,28},{28,24},{32,36},... | collective-permute-start | bytes 1572872 | tf_op jit(solution)/shard_map/ppermute | solution.py:48
  40.0 2.8 %attend.1 = bf16[8,128,128]{2,1,0:T(8,128)(2,1)} custom-call(bf16[8,384,128]{2,1,0:T(8,128)(2,1)S(1)} %after.2.own, bf16[8,384,128]{2,1,0:T(8,128)(2,1)S(1)} %collective-permute-done.16.other), custom_call_target="tpu_custom_call" | custom-call | flops 10000000000 | bytes 1024 | tf_op jit(solution)/shard_map/attend/pallas_call | solution.py:394
  42.8 6.7 %all-to-all-start.1 = ((bf16[8,128,128]{2,1,0:T(8,128)(2,1)}), bf16[8,128,128]{2,1,0:T(8,128)(2,1)S(1)}, u32[]{:S(2)}, u32[]{:S(2)}) async-start(bf16[8,128,128]{2,1,0:T(8,128)(2,1)} %attend.1), calls=%async_computation.1 | async-start | bytes 524288 | tf_op jit(solution)/shard_map/all_to_all | solution.py:57
  49.5 0.8 %collective-permute-done.9.x2 = bf16[512,256]{1,0:T(8,128)(2,1)} collective-permute-done((bf16[512,256]{1,0:T(8,128)(2,1)S(1)}, bf16[512,256]{1,0:T(8,128)(2,1)}, u32[]{:S(2)}, u32[]{:S(2)}) %collective-permute-start.9) | collective-permute-done | bytes 262176 | tf_op jit(solution)/shard_map/ppermute | solution.py:33
  50.3 2.6 %encode.1 = (bf16[256,256]{1,0:T(8,128)(2,1)S(1)}, bf16[256,256]{1,0:T(8,128)(2,1)S(1)}, bf16[512,1024]{1,0:T(8,128)(2,1)}) custom-call(bf16[512,256]{1,0:T(8,128)(2,1)S(1)} %compact.1.x0.refs_1_, bf16[512,256]{1,0:T(8,128)(2,1)} %collective-permute-done.8.x1, bf16[512,256]{1,0:T(8,128)(2,1)} %collective-permute-done.9.x2, ...), custom_call_target="tpu_custom_call" | custom-call | flops 30000001024 | bytes 1024 | tf_op jit(solution)/shard_map/encode/pallas_call | solution.py:211
  52.8 1.0 %collective-permute-start.11 = (bf16[256,256]{1,0:T(8,128)(2,1)S(1)}, bf16[256,256]{1,0:T(8,128)(2,1)S(1)}, u32[]{:S(2)}, u32[]{:S(2)}) collective-permute-start(bf16[256,256]{1,0:T(8,128)(2,1)S(1)} %get-tuple-element.24.refs_2_), channel_id=1, source_target_pairs={{0,1},{1,2},{2,3},{3,0},{4,5},{5,6},{6,7},{7,4},{8,9},{9,10},{10,1... | collective-permute-start | bytes 393224 | tf_op jit(solution)/shard_map/ppermute | solution.py:33
  53.8 2.4 %collective-permute-start.12 = (bf16[256,256]{1,0:T(8,128)(2,1)S(1)}, bf16[256,256]{1,0:T(8,128)(2,1)S(1)}, u32[]{:S(2)}, u32[]{:S(2)}) collective-permute-start(bf16[256,256]{1,0:T(8,128)(2,1)S(1)} %get-tuple-element.24.refs_2_), channel_id=1, source_target_pairs={{0,2},{1,3},{2,0},{3,1},{4,6},{5,7},{6,4},{7,5},{8,10},{9,11},{10,... | collective-permute-start | bytes 393224 | tf_op jit(solution)/shard_map/ppermute | solution.py:33
  56.2 1.1 %collective-permute-start.13 = (bf16[256,256]{1,0:T(8,128)(2,1)S(1)}, bf16[256,256]{1,0:T(8,128)(2,1)S(1)}, u32[]{:S(2)}, u32[]{:S(2)}) collective-permute-start(bf16[256,256]{1,0:T(8,128)(2,1)S(1)} %get-tuple-element.24.refs_2_), channel_id=1, source_target_pairs={{0,3},{1,0},{2,1},{3,2},{4,7},{5,4},{6,5},{7,6},{8,11},{9,8},{10,9... | collective-permute-start | bytes 393224 | tf_op jit(solution)/shard_map/ppermute | solution.py:33
  57.6 1.7 %load.1.refs_6_.refs_1_ = bf16[1024,1024]{1,0:T(8,128)(2,1)S(1)} custom-call(bf16[256,1024]{1,0:T(8,128)(2,1)} %w0.1, bf16[256,1024]{1,0:T(8,128)(2,1)} %copy-done.5, bf16[128,1024]{1,0:T(8,128)(2,1)} %copy-done.7, bf16[256,1024]{1,0:T(8,128)(2,1)} %collective-permute-done.14.s_near, bf16[128,1024]{1,0:T(8,128)(2,1)} %collective-permute-done.15.s_half, ...), custom_call_target="tpu_custom_call" | custom-call | flops 3000000000 | bytes 1024 | tf_op jit(solution)/shard_map/load/pallas_call | solution.py:239
  59.9 1.1 %collective-permute-start.19 = (bf16[256,256]{1,0:T(8,128)(2,1)S(1)}, bf16[256,256]{1,0:T(8,128)(2,1)S(1)}, u32[]{:S(2)}, u32[]{:S(2)}) collective-permute-start(bf16[256,256]{1,0:T(8,128)(2,1)S(1)} %after.3.refs_2_), channel_id=1, source_target_pairs={{0,2},{1,3},{2,0},{3,1},{4,6},{5,7},{6,4},{7,5},{8,10},{9,11},{10,... | collective-permute-start | bytes 393224 | tf_op jit(solution)/shard_map/ppermute | solution.py:33
  61.0 1.7 %collective-permute-start.20 = (bf16[256,256]{1,0:T(8,128)(2,1)S(1)}, bf16[256,256]{1,0:T(8,128)(2,1)S(1)}, u32[]{:S(2)}, u32[]{:S(2)}) collective-permute-start(bf16[256,256]{1,0:T(8,128)(2,1)S(1)} %after.3.refs_2_), channel_id=1, source_target_pairs={{0,3},{1,0},{2,1},{3,2},{4,7},{5,4},{6,5},{7,6},{8,11},{9,8},{10,9... | collective-permute-start | bytes 393224 | tf_op jit(solution)/shard_map/ppermute | solution.py:33
  62.8 3.4 %cross.2.second = bf16[64,1024]{1,0:T(8,128)(2,1)S(1)} custom-call(s32[1,32]{1,0:T(1,128)S(1)} %copy-done.8, bf16[512,1024]{1,0:T(8,128)(2,1)} %get-tuple-element.23.refs_1_, bf16[256,256]{1,0:T(8,128)(2,1)S(1)} %get-tuple-element.24.refs_2_, bf16[256,256]{1,0:T(8,128)(2,1)S(1)} %collective-permute-done.11.refs_3_, ...), custom_call_target="tpu_custom_call" | custom-call | flops 5000000000 | bytes 1024 | tf_op jit(solution)/shard_map/cross/pallas_call | solution.py:288
  66.2 4.7 %collective-permute-start.17 = (bf16[64,1024]{1,0:T(8,128)(2,1)S(1)}, bf16[64,1024]{1,0:T(8,128)(2,1)S(1)}, u32[]{:S(2)}, u32[]{:S(2)}) collective-permute-start(bf16[64,1024]{1,0:T(8,128)(2,1)S(1)} %cross.2.second), channel_id=1, source_target_pairs={{0,4},{4,8},{8,12},{12,16},{16,20},{20,24},{24,28},{28,32},{32,36}... | collective-permute-start | bytes 393224 | tf_op jit(solution)/shard_map/ppermute | solution.py:33
  70.9 3.4 %cross.3.first = bf16[64,1024]{1,0:T(8,128)(2,1)S(1)} custom-call(s32[1,32]{1,0:T(1,128)S(1)} %copy-done.8, bf16[512,1024]{1,0:T(8,128)(2,1)} %get-tuple-element.23.refs_1_, bf16[256,256]{1,0:T(8,128)(2,1)S(1)} %after.3.refs_2_, bf16[256,256]{1,0:T(8,128)(2,1)S(1)} %collective-permute-done.18.refs_3_, bf16[256,256]{1,0:T(8,128)(2,1)S(1)} %collective-permute-done.19.refs_4_, ...), custom_call_target="tpu_custom_call" | custom-call | flops 5000000000 | bytes 1024 | tf_op jit(solution)/shard_map/cross/pallas_call | solution.py:288
  74.3 0.8 %place.1 = bf16[1,128,1024]{2,1,0:T(8,128)(2,1)} custom-call(bf16[64,1024]{1,0:T(8,128)(2,1)S(1)} %collective-permute-done.17.received, bf16[64,1024]{1,0:T(8,128)(2,1)S(1)} %cross.3.first, bf16[64,1024]{1,0:T(8,128)(2,1)S(1)} %cross.2.second), custom_call_target="tpu_custom_call" | custom-call | flops 1000000000 | bytes 1024 | tf_op jit(solution)/shard_map/place/pallas_call | solution.py:434
  (46 shorter events, 1.9 us)
Async XLA Ops:
  0.0 17.1 %copy-start.9 = (bf16[256,1024]{1,0:T(8,128)(2,1)S(1)}, bf16[256,1024]{1,0:T(8,128)(2,1)}, u32[]{:S(2)}) copy-start(bf16[256,1024]{1,0:T(8,128)(2,1)} %w0.1) | copy-start | bytes 1572868
  2.2 30.2 %all-to-all-start = ((bf16[8,384,128]{2,1,0:T(8,128)(2,1)}), bf16[8,384,128]{2,1,0:T(8,128)(2,1)S(1)}, u32[]{:S(2)}, u32[]{:S(2)}) async-start(bf16[8,384,128]{2,1,0:T(8,128)(2,1)} %get-tuple-element.25), calls=%async_computation | async-start | bytes 1572864 | tf_op jit(solution)/shard_map/all_to_all | solution.py:57
  12.1 8.0 %collective-permute-start = (s32[4]{0:T(128)S(1)}, s32[4]{0:T(128)S(1)}, u32[]{:S(2)}, u32[]{:S(2)}) collective-permute-start(s32[4]{0:T(128)S(1)} %get-tuple-element.17.idx0.idx), channel_id=1, source_target_pairs={{0,64},{64,128},{128,192},{192,0},{1,65},{65,129},{129,193},{193,1... | collective-permute-start | bytes 56 | tf_op jit(solution)/shard_map/ppermute | solution.py:33
  13.4 6.7 %collective-permute-start.1 = (s32[4]{0:T(128)S(1)}, s32[4]{0:T(128)S(1)}, u32[]{:S(2)}, u32[]{:S(2)}) collective-permute-start(s32[4]{0:T(128)S(1)} %get-tuple-element.17.idx0.idx), channel_id=1, source_target_pairs={{0,128},{64,192},{128,0},{192,64},{1,129},{65,193},{129,1},{193,65... | collective-permute-start | bytes 56 | tf_op jit(solution)/shard_map/ppermute | solution.py:33
  16.0 4.1 %collective-permute-start.2 = (s32[4]{0:T(128)S(1)}, s32[4]{0:T(128)S(1)}, u32[]{:S(2)}, u32[]{:S(2)}) collective-permute-start(s32[4]{0:T(128)S(1)} %get-tuple-element.17.idx0.idx), channel_id=1, source_target_pairs={{0,192},{64,0},{128,64},{192,128},{1,193},{65,1},{129,65},{193,129... | collective-permute-start | bytes 56 | tf_op jit(solution)/shard_map/ppermute | solution.py:33
  17.1 14.2 %collective-permute-start.6 = (bf16[256,1024]{1,0:T(8,128)(2,1)S(1)}, bf16[256,1024]{1,0:T(8,128)(2,1)S(1)}, u32[]{:S(2)}, u32[]{:S(2)}) collective-permute-start(bf16[256,1024]{1,0:T(8,128)(2,1)S(1)} %copy-done.9), channel_id=1, source_target_pairs={{0,1},{1,2},{2,3},{3,0},{4,7},{5,4},{6,5},{7,6},{8,9},{9,10},{10,1... | collective-permute-start | bytes 1572872 | tf_op jit(solution)/shard_map/ppermute | solution.py:43
  19.5 10.0 %collective-permute-start.7 = (bf16[128,1024]{1,0:T(8,128)(2,1)S(1)}, bf16[128,1024]{1,0:T(8,128)(2,1)S(1)}, u32[]{:S(2)}, u32[]{:S(2)}) collective-permute-start(bf16[128,1024]{1,0:T(8,128)(2,1)S(1)} %get-tuple-element.22), channel_id=1, source_target_pairs={{0,2},{1,3},{2,0},{3,1},{4,6},{5,7},{6,4},{7,5},{8,10},{9,11},{10,... | collective-permute-start | bytes 786440 | tf_op jit(solution)/shard_map/ppermute | solution.py:33
  21.8 4.2 %collective-permute-start.3 = (bf16[256,256]{1,0:T(8,128)(2,1)S(1)}, bf16[256,256]{1,0:T(8,128)(2,1)S(1)}, u32[]{:S(2)}, u32[]{:S(2)}) collective-permute-start(bf16[256,256]{1,0:T(8,128)(2,1)S(1)} %get-tuple-element.19), channel_id=1, source_target_pairs={{0,192},{64,0},{128,64},{192,128},{1,193},{65,1},{129,65},{193,129... | collective-permute-start | bytes 393224 | tf_op jit(solution)/shard_map/ppermute | solution.py:33
  22.5 5.5 %collective-permute-start.4 = (bf16[256,256]{1,0:T(8,128)(2,1)S(1)}, bf16[256,256]{1,0:T(8,128)(2,1)S(1)}, u32[]{:S(2)}, u32[]{:S(2)}) collective-permute-start(bf16[256,256]{1,0:T(8,128)(2,1)S(1)} %get-tuple-element.20), channel_id=1, source_target_pairs={{0,128},{64,192},{128,0},{192,64},{1,129},{65,193},{129,1},{193,65... | collective-permute-start | bytes 393224 | tf_op jit(solution)/shard_map/ppermute | solution.py:33
  24.1 5.4 %collective-permute-start.5 = (bf16[256,256]{1,0:T(8,128)(2,1)S(1)}, bf16[256,256]{1,0:T(8,128)(2,1)S(1)}, u32[]{:S(2)}, u32[]{:S(2)}) collective-permute-start(bf16[256,256]{1,0:T(8,128)(2,1)S(1)} %get-tuple-element.21), channel_id=1, source_target_pairs={{0,64},{64,128},{128,192},{192,0},{1,65},{65,129},{129,193},{193,1... | collective-permute-start | bytes 393224 | tf_op jit(solution)/shard_map/ppermute | solution.py:33
  29.5 7.2 %copy-start.7 = (bf16[128,1024]{1,0:T(8,128)(2,1)}, bf16[128,1024]{1,0:T(8,128)(2,1)S(1)}, u32[]{:S(2)}) copy-start(bf16[128,1024]{1,0:T(8,128)(2,1)S(1)} %collective-permute-done.7.w2.w_half) | copy-start | bytes 786436
  31.3 7.5 %copy-start.5 = (bf16[256,1024]{1,0:T(8,128)(2,1)}, bf16[256,1024]{1,0:T(8,128)(2,1)S(1)}, u32[]{:S(2)}) copy-start(bf16[256,1024]{1,0:T(8,128)(2,1)S(1)} %collective-permute-done.6.w1.w_near) | copy-start | bytes 1572868
  32.4 17.8 %copy-start.2 = (bf16[1024,256]{1,0:T(8,128)(2,1)S(1)}, bf16[1024,256]{1,0:T(8,128)(2,1)}, u32[]{:S(2)}) copy-start(bf16[1024,256]{1,0:T(8,128)(2,1)} %wq.2) | copy-start | bytes 1572868
  32.4 17.8 %copy-start.3 = (bf16[1024,256]{1,0:T(8,128)(2,1)S(1)}, bf16[1024,256]{1,0:T(8,128)(2,1)}, u32[]{:S(2)}) copy-start(bf16[1024,256]{1,0:T(8,128)(2,1)} %wk.1) | copy-start | bytes 1572868
  32.5 17.8 %copy-start.4 = (bf16[1024,256]{1,0:T(8,128)(2,1)S(1)}, bf16[1024,256]{1,0:T(8,128)(2,1)}, u32[]{:S(2)}) copy-start(bf16[1024,256]{1,0:T(8,128)(2,1)} %wv.1) | copy-start | bytes 1572868
  32.5 6.3 %collective-permute-start.16 = (bf16[8,384,128]{2,1,0:T(8,128)(2,1)S(1)}, bf16[8,384,128]{2,1,0:T(8,128)(2,1)S(1)}, u32[]{:S(2)}, u32[]{:S(2)}) collective-permute-start(bf16[8,384,128]{2,1,0:T(8,128)(2,1)S(1)} %after.2.own), channel_id=1, source_target_pairs={{0,4},{4,0},{8,12},{12,8},{16,20},{20,16},{24,28},{28,24},{32,36},... | collective-permute-start | bytes 2359304 | tf_op jit(solution)/shard_map/ppermute | solution.py:48
  36.7 20.9 %collective-permute-start.15 = (bf16[128,1024]{1,0:T(8,128)(2,1)S(1)}, bf16[128,1024]{1,0:T(8,128)(2,1)}, u32[]{:S(2)}, u32[]{:S(2)}) collective-permute-start(bf16[128,1024]{1,0:T(8,128)(2,1)S(1)} %collective-permute-done.7.w2.w_half), channel_id=1, source_target_pairs={{0,4},{4,0},{8,12},{12,8},{16,20},{20,16},{24,28},{28,24},{32,36},... | collective-permute-start | bytes 786440 | tf_op jit(solution)/shard_map/ppermute | solution.py:48
  36.8 12.7 %collective-permute-start.10 = (bf16[512,256]{1,0:T(8,128)(2,1)S(1)}, bf16[512,256]{1,0:T(8,128)(2,1)}, u32[]{:S(2)}, u32[]{:S(2)}) collective-permute-start(bf16[512,256]{1,0:T(8,128)(2,1)S(1)} %compact.1.x0.refs_1_), channel_id=1, source_target_pairs={{0,3},{1,0},{2,1},{3,2},{4,7},{5,4},{6,5},{7,6},{8,11},{9,8},{10,9... | collective-permute-start | bytes 786440 | tf_op jit(solution)/shard_map/ppermute | solution.py:33
  37.2 12.3 %collective-permute-start.8 = (bf16[512,256]{1,0:T(8,128)(2,1)S(1)}, bf16[512,256]{1,0:T(8,128)(2,1)}, u32[]{:S(2)}, u32[]{:S(2)}) collective-permute-start(bf16[512,256]{1,0:T(8,128)(2,1)S(1)} %compact.1.x0.refs_1_), channel_id=1, source_target_pairs={{0,1},{1,2},{2,3},{3,0},{4,5},{5,6},{6,7},{7,4},{8,9},{9,10},{10,1... | collective-permute-start | bytes 786440 | tf_op jit(solution)/shard_map/ppermute | solution.py:33
  38.2 12.0 %collective-permute-start.9 = (bf16[512,256]{1,0:T(8,128)(2,1)S(1)}, bf16[512,256]{1,0:T(8,128)(2,1)}, u32[]{:S(2)}, u32[]{:S(2)}) collective-permute-start(bf16[512,256]{1,0:T(8,128)(2,1)S(1)} %compact.1.x0.refs_1_), channel_id=1, source_target_pairs={{0,2},{1,3},{2,0},{3,1},{4,6},{5,7},{6,4},{7,5},{8,10},{9,11},{10,... | collective-permute-start | bytes 786440 | tf_op jit(solution)/shard_map/ppermute | solution.py:33
  38.8 18.8 %collective-permute-start.14 = (bf16[256,1024]{1,0:T(8,128)(2,1)S(1)}, bf16[256,1024]{1,0:T(8,128)(2,1)}, u32[]{:S(2)}, u32[]{:S(2)}) collective-permute-start(bf16[256,1024]{1,0:T(8,128)(2,1)S(1)} %collective-permute-done.6.w1.w_near), channel_id=1, source_target_pairs={{0,4},{4,0},{8,12},{12,8},{16,20},{20,16},{24,28},{28,24},{32,36},... | collective-permute-start | bytes 1572872 | tf_op jit(solution)/shard_map/ppermute | solution.py:48
  42.8 14.6 %all-to-all-start.1 = ((bf16[8,128,128]{2,1,0:T(8,128)(2,1)}), bf16[8,128,128]{2,1,0:T(8,128)(2,1)S(1)}, u32[]{:S(2)}, u32[]{:S(2)}) async-start(bf16[8,128,128]{2,1,0:T(8,128)(2,1)} %attend.1), calls=%async_computation.1 | async-start | bytes 524288 | tf_op jit(solution)/shard_map/all_to_all | solution.py:57
  49.5 7.9 %copy-start.6 = (bf16[8,128,128]{2,1,0:T(8,128)(2,1)S(1)}, bf16[8,128,128]{2,1,0:T(8,128)(2,1)}, u32[]{:S(2)}) copy-start(bf16[8,128,128]{2,1,0:T(8,128)(2,1)} %wq.3) | copy-start | bytes 786436
  52.8 8.2 %collective-permute-start.11 = (bf16[256,256]{1,0:T(8,128)(2,1)S(1)}, bf16[256,256]{1,0:T(8,128)(2,1)S(1)}, u32[]{:S(2)}, u32[]{:S(2)}) collective-permute-start(bf16[256,256]{1,0:T(8,128)(2,1)S(1)} %get-tuple-element.24.refs_2_), channel_id=1, source_target_pairs={{0,1},{1,2},{2,3},{3,0},{4,5},{5,6},{6,7},{7,4},{8,9},{9,10},{10,1... | collective-permute-start | bytes 393224 | tf_op jit(solution)/shard_map/ppermute | solution.py:33
  53.8 8.9 %collective-permute-start.12 = (bf16[256,256]{1,0:T(8,128)(2,1)S(1)}, bf16[256,256]{1,0:T(8,128)(2,1)S(1)}, u32[]{:S(2)}, u32[]{:S(2)}) collective-permute-start(bf16[256,256]{1,0:T(8,128)(2,1)S(1)} %get-tuple-element.24.refs_2_), channel_id=1, source_target_pairs={{0,2},{1,3},{2,0},{3,1},{4,6},{5,7},{6,4},{7,5},{8,10},{9,11},{10,... | collective-permute-start | bytes 393224 | tf_op jit(solution)/shard_map/ppermute | solution.py:33
  56.2 6.5 %collective-permute-start.13 = (bf16[256,256]{1,0:T(8,128)(2,1)S(1)}, bf16[256,256]{1,0:T(8,128)(2,1)S(1)}, u32[]{:S(2)}, u32[]{:S(2)}) collective-permute-start(bf16[256,256]{1,0:T(8,128)(2,1)S(1)} %get-tuple-element.24.refs_2_), channel_id=1, source_target_pairs={{0,3},{1,0},{2,1},{3,2},{4,7},{5,4},{6,5},{7,6},{8,11},{9,8},{10,9... | collective-permute-start | bytes 393224 | tf_op jit(solution)/shard_map/ppermute | solution.py:33
  57.6 5.1 %copy-start.1 = (bf16[1024,1024]{1,0:T(8,128)(2,1)S(1)}, bf16[1024,1024]{1,0:T(8,128)(2,1)}, u32[]{:S(2)}) copy-start(bf16[1024,1024]{1,0:T(8,128)(2,1)} %refs_8_.3) | copy-start | bytes 6291460
  59.3 3.4 %copy-start = (bf16[1024,1024]{1,0:T(8,128)(2,1)S(1)}, bf16[1024,1024]{1,0:T(8,128)(2,1)}, u32[]{:S(2)}) copy-start(bf16[1024,1024]{1,0:T(8,128)(2,1)} %refs_7_.3) | copy-start | bytes 6291460
  59.4 11.5 %collective-permute-start.18 = (bf16[256,256]{1,0:T(8,128)(2,1)S(1)}, bf16[256,256]{1,0:T(8,128)(2,1)S(1)}, u32[]{:S(2)}, u32[]{:S(2)}) collective-permute-start(bf16[256,256]{1,0:T(8,128)(2,1)S(1)} %after.3.refs_2_), channel_id=1, source_target_pairs={{0,1},{1,2},{2,3},{3,0},{4,5},{5,6},{6,7},{7,4},{8,9},{9,10},{10,1... | collective-permute-start | bytes 393224 | tf_op jit(solution)/shard_map/ppermute | solution.py:33
  59.9 11.0 %collective-permute-start.19 = (bf16[256,256]{1,0:T(8,128)(2,1)S(1)}, bf16[256,256]{1,0:T(8,128)(2,1)S(1)}, u32[]{:S(2)}, u32[]{:S(2)}) collective-permute-start(bf16[256,256]{1,0:T(8,128)(2,1)S(1)} %after.3.refs_2_), channel_id=1, source_target_pairs={{0,2},{1,3},{2,0},{3,1},{4,6},{5,7},{6,4},{7,5},{8,10},{9,11},{10,... | collective-permute-start | bytes 393224 | tf_op jit(solution)/shard_map/ppermute | solution.py:33
  61.0 9.9 %collective-permute-start.20 = (bf16[256,256]{1,0:T(8,128)(2,1)S(1)}, bf16[256,256]{1,0:T(8,128)(2,1)S(1)}, u32[]{:S(2)}, u32[]{:S(2)}) collective-permute-start(bf16[256,256]{1,0:T(8,128)(2,1)S(1)} %after.3.refs_2_), channel_id=1, source_target_pairs={{0,3},{1,0},{2,1},{3,2},{4,7},{5,4},{6,5},{7,6},{8,11},{9,8},{10,9... | collective-permute-start | bytes 393224 | tf_op jit(solution)/shard_map/ppermute | solution.py:33
  66.2 8.1 %collective-permute-start.17 = (bf16[64,1024]{1,0:T(8,128)(2,1)S(1)}, bf16[64,1024]{1,0:T(8,128)(2,1)S(1)}, u32[]{:S(2)}, u32[]{:S(2)}) collective-permute-start(bf16[64,1024]{1,0:T(8,128)(2,1)S(1)} %cross.2.second), channel_id=1, source_target_pairs={{0,4},{4,8},{8,12},{12,16},{16,20},{20,24},{24,28},{28,32},{32,36}... | collective-permute-start | bytes 393224 | tf_op jit(solution)/shard_map/ppermute | solution.py:33
  (1 other events, 3.4 us)

commit v4 on v3

--- a/solution.py
+++ b/solution.py
@@ -132,27 +132,17 @@
     )(*idx, in_hbm(memory))
 
 
-def compact_kernel(idx, r0, r1, r2, r3, w1, w2, out, sems):
+def compact_kernel(idx, r0, r1, r2, r3, w1, w2, out):
     me = lax.axis_index("enc")
-
-    def each(act):
-        for span in range(2):
-            for j in range(K_NB):
-                at = (idx[span * K_NB + j] // DB - me + N_ENC) % N_ENC
-                for k, r in enumerate((r0, r1, r2, r3)):
-
-                    @pl.when(at == k)
-                    def _():
-                        act(
-                            pltpu.make_async_copy(
-                                r.at[pl.ds(span * NT, NT)],
-                                out.at[pl.ds((span * K_NB + j) * NT, NT)],
-                                sems.at[span * K_NB + j],
-                            )
-                        )
-
-    each(lambda c: c.start())
-    each(lambda c: c.wait())
+    for span in range(2):
+        for j in range(K_NB):
+            at = (idx[span * K_NB + j] // DB - me + N_ENC) % N_ENC
+            for k, r in enumerate((r0, r1, r2, r3)):
+
+                @pl.when(at == k)
+                def _():
+                    begin = (span * K_NB + j) * NT
+                    out[begin : begin + NT] = r[span * NT : (span + 1) * NT]
 
 
 def compact(idx, received, others):
@@ -160,10 +150,9 @@
     return pl.pallas_call(
         compact_kernel,
         out_shape=sds((K_NB * rows, cols)),
-        in_specs=[SMEM] + [ANY] * 6,
-        out_specs=ANY,
-        scratch_shapes=[pltpu.SemaphoreType.DMA((4,))],
-        compiler_params=params(1),
+        in_specs=[SMEM] + [VMEM] * 4 + [ANY] * 2,
+        out_specs=VMEM,
+        compiler_params=params(4),
         cost_estimate=cost(1 * 10**9, 1024),
         name="compact",
     )(idx, *received, *others)
@@ -220,7 +209,7 @@
     )(*pieces, wq, wk, wv)
 
 
-def load_kernel(w0, w_near, w_half, s_near, s_half, tie, wo_out, sems):
+def load_kernel(w0, w_near, w_half, s_near, s_half, heads, wq, wo_out, so, cq, sems):
     width = w0.shape[0]
     half = width // 2
     core = lax.axis_index("seq") % 2
@@ -230,22 +219,29 @@
     for w, begin in begins:
         rows = w.shape[0]
         pairs.append((w, wo_out.at[pl.ds(pl.multiple_of(begin, half), rows)]))
-    for c in run_copies(pairs, sems):
-        c.wait()
-
-
-def load(wo, tie):
+    copies = run_copies(pairs, sems)
+    for h in range(N_Z):
+        cols = slice(h * HEAD_DIM, (h + 1) * HEAD_DIM)
+        value = heads[turned(h)]
+        so[:, cols] = value
+        cq[:, cols] = dot(value, wq[h]).astype(BF)
+    for c in copies:
+        c.wait()
+
+
+def load(wo, heads, wq):
     depth = wo[0].shape[1]
+    tok, cols = heads.shape[1], N_Z * HEAD_DIM
     return pl.pallas_call(
         load_kernel,
-        out_shape=pltpu.VMEM((depth, depth), BF),
-        in_specs=[ANY] * 6,
-        out_specs=ANY,
+        out_shape=[pltpu.VMEM((depth, depth), BF), sds((tok, cols)), sds((tok, cols))],
+        in_specs=[ANY] * 5 + [VMEM] * 2,
+        out_specs=[ANY, VMEM, VMEM],
         scratch_shapes=[pltpu.SemaphoreType.DMA((5,))],
-        compiler_params=params(1),
+        compiler_params=params(4),
         cost_estimate=cost(3 * 10**9, 1024),
         name="load",
-    )(*map(in_hbm, wo[:3]), *wo[3:], tie)
+    )(*map(in_hbm, wo[:3]), *wo[3:], heads, wq)
 
 
 def cross_kernel(which, counts, src, a0, a1, a2, a3, wo, wk, wv, cq, so, out, src_s, attn, sems):
@@ -402,28 +398,6 @@
     )(own, other)
 
 
-def query_kernel(heads, wq, so, cq):
-    for h in range(N_Z):
-        cols = slice(h * HEAD_DIM, (h + 1) * HEAD_DIM)
-        value = heads[turned(h)]
-        so[:, cols] = value
-        cq[:, cols] = dot(value, wq[h]).astype(BF)
-
-
-def cross_queries(heads, wq):
-    tok = heads.shape[1]
-    cols = N_Z * HEAD_DIM
-    return pl.pallas_call(
-        query_kernel,
-        out_shape=[sds((tok, cols))] * 2,
-        in_specs=[VMEM] * 2,
-        out_specs=[VMEM] * 2,
-        compiler_params=params(4),
-        cost_estimate=cost(1 * 10**9, 1024),
-        name="cross_queries",
-    )(heads, wq)
-
-
 def place_kernel(received, first, second, out):
     rows = jnp.concatenate([received[...], first[...], second[...]], axis=0).astype(F32)
     out[0] = pltpu.roll(rows, rows.shape[0] - 1, 0)[: out.shape[1]].astype(BF)
@@ -458,11 +432,10 @@
 
     packed = after(packed, mine)
     heads = over_z(attend(packed, core_swap(packed)))
-    so, cq = cross_queries(heads, cross_wq)
 
     early, late, source = encode(pieces, enc_wq, enc_wk, enc_wv)
     late = [late] + [shifted(late, "mp", k) for k in range(1, N_MP)]
-    wo = load((enc_wo, near, far, core_swap(near), core_swap(far)), cq)
+    wo, so, cq = load((enc_wo, near, far, core_swap(near), core_swap(far)), heads, cross_wq)
     early = after(early, wo)
     early = [early] + [shifted(early, "mp", k) for k in range(1, N_MP)]
     second = cross(1, nbr_count, source, late, wo, cross_wk, cross_wv, cq, so)

time: 75.5 us -> 74.9 us (level)
    pallas_call x2 -> x1, Pallas kernels: 1.91 us -> 1.76 us  [load(): pl.pallas_call(load_kernel, out_shape=[pltpu.VMEM((depth, depth), BF), sd...]
where the time goes in v4:
time: 74.9 us; the launch traced here: 74.4 us
  starting transfers between devices  47 us (63%)
  Pallas kernels  19.2 us (26%)
  waiting for transfers between devices  8.02 us (11%)
    ppermute x17, starting transfers between devices, shifted(): lax.ppermute(block, axis, [(i, (i + distance) % size) for i in range(size)])  22.4 us
    all_to_all x2, starting transfers between devices, over_z(): lax.all_to_all(blocks, 'seq', 0, 0, axis_index_groups=groups, tiled=True)  16.5 us
    pallas_call x2, Pallas kernels, cross(): pl.pallas_call(body, out_shape=sds((SPAN, cols)), in_specs=[SMEM] + [ANY]...  6.72 us
    ppermute x17, waiting for transfers between devices, shifted(): lax.ppermute(block, axis, [(i, (i + distance) % size) for i in range(size)])  6.31 us
    ppermute x3, starting transfers between devices, core_swap(): return lax.ppermute(block, 'seq', [(i, i ^ 1) for i in range(size)])  5.54 us
    pallas_call x1, Pallas kernels, attend(): pl.pallas_call(attend_kernel, out_shape=sds((N_Z, tok, HEAD_DIM)), in_spe...  2.76 us
    pallas_call x1, Pallas kernels, encode(): pl.pallas_call(encode_kernel, out_shape=[sds((rows // 2, width))] * 2 + [...  2.57 us
    ppermute x1, starting transfers between devices, to_sides(): return lax.ppermute(block, ('seq', 'mp'), route)  2.48 us
  transfers between devices with their start and end apart: 23, of which 5 were waited for; matrix products, arithmetic and copies ran while one was open for 0% of the time, Pallas kernels for 22%

profile of v4, /device:TPU:1, one launch (start us, length us, event | category | flops | bytes accessed | tf_op | source)
XLA Modules:
  0.0 74.4 jit_solution(2316724039377145586)
XLA Ops:
  0.0 2.2 %pack.1 = (bf16[8,384,128]{2,1,0:T(8,128)(2,1)}, s32[4]{0:T(128)S(1)}, bf16[128,1024]{1,0:T(8,128)(2,1)S(1)}) custom-call(bf16[1,128,1024]{2,1,0:T(8,128)(2,1)} %q.1, bf16[1,128,1024]{2,1,0:T(8,128)(2,1)} %k.1, bf16[1,128,1024]{2,1,0:T(8,128)(2,1)} %v.1, bf16[256,1024]{1,0:T(8,128)(2,1)} %w0.1, s32[1,2,2]{2,1,0:T(2,128)} %nbr_rows.1, s32[1,2,2]{2,1,0:T(2,128)} %nbr_owner.1), custom_call_target="tpu_custom_call" | custom-call | flops 1000000000 | bytes 1024 | tf_op jit(solution)/shard_map/pack/pallas_call | solution.py:323
  2.2 9.9 %all-to-all-start = ((bf16[8,384,128]{2,1,0:T(8,128)(2,1)}), bf16[8,384,128]{2,1,0:T(8,128)(2,1)S(1)}, u32[]{:S(2)}, u32[]{:S(2)}) async-start(bf16[8,384,128]{2,1,0:T(8,128)(2,1)} %get-tuple-element.26), calls=%async_computation | async-start | bytes 1572864 | tf_op jit(solution)/shard_map/all_to_all | solution.py:57
  12.1 1.3 %collective-permute-start = (s32[4]{0:T(128)S(1)}, s32[4]{0:T(128)S(1)}, u32[]{:S(2)}, u32[]{:S(2)}) collective-permute-start(s32[4]{0:T(128)S(1)} %get-tuple-element.18.idx0.idx), channel_id=1, source_target_pairs={{0,64},{64,128},{128,192},{192,0},{1,65},{65,129},{129,193},{193,1... | collective-permute-start | bytes 56 | tf_op jit(solution)/shard_map/ppermute | solution.py:33
  13.4 2.6 %collective-permute-start.1 = (s32[4]{0:T(128)S(1)}, s32[4]{0:T(128)S(1)}, u32[]{:S(2)}, u32[]{:S(2)}) collective-permute-start(s32[4]{0:T(128)S(1)} %get-tuple-element.18.idx0.idx), channel_id=1, source_target_pairs={{0,128},{64,192},{128,0},{192,64},{1,129},{65,193},{129,1},{193,65... | collective-permute-start | bytes 56 | tf_op jit(solution)/shard_map/ppermute | solution.py:33
  16.0 1.1 %collective-permute-start.2 = (s32[4]{0:T(128)S(1)}, s32[4]{0:T(128)S(1)}, u32[]{:S(2)}, u32[]{:S(2)}) collective-permute-start(s32[4]{0:T(128)S(1)} %get-tuple-element.18.idx0.idx), channel_id=1, source_target_pairs={{0,192},{64,0},{128,64},{192,128},{1,193},{65,1},{129,65},{193,129... | collective-permute-start | bytes 56 | tf_op jit(solution)/shard_map/ppermute | solution.py:33
  17.1 2.5 %collective-permute-start.6 = (bf16[256,1024]{1,0:T(8,128)(2,1)S(1)}, bf16[256,1024]{1,0:T(8,128)(2,1)S(1)}, u32[]{:S(2)}, u32[]{:S(2)}) collective-permute-start(bf16[256,1024]{1,0:T(8,128)(2,1)S(1)} %copy-done.9), channel_id=1, source_target_pairs={{0,1},{1,2},{2,3},{3,0},{4,7},{5,4},{6,5},{7,6},{8,9},{9,10},{10,1... | collective-permute-start | bytes 1572872 | tf_op jit(solution)/shard_map/ppermute | solution.py:43
  20.1 1.7 %fetch.1 = (bf16[256,256]{1,0:T(8,128)(2,1)S(1)}, bf16[256,256]{1,0:T(8,128)(2,1)S(1)}, bf16[256,256]{1,0:T(8,128)(2,1)S(1)}, bf16[256,256]{1,0:T(8,128)(2,1)S(1)}) custom-call(s32[4]{0:T(128)S(1)} %get-tuple-element.18.idx0.idx, s32[4]{0:T(128)S(1)} %collective-permute-done.idx1, s32[4]{0:T(128)S(1)} %collective-permute-done.1.idx2, ...), custom_call_target="tpu_custom_call" | custom-call | flops 5000000000 | bytes 1024 | tf_op jit(solution)/shard_map/fetch/pallas_call | solution.py:123
  21.8 0.7 collective-permute-start.3
  22.6 1.5 %collective-permute-start.4 = (bf16[256,256]{1,0:T(8,128)(2,1)S(1)}, bf16[256,256]{1,0:T(8,128)(2,1)S(1)}, u32[]{:S(2)}, u32[]{:S(2)}) collective-permute-start(bf16[256,256]{1,0:T(8,128)(2,1)S(1)} %get-tuple-element.21), channel_id=1, source_target_pairs={{0,128},{64,192},{128,0},{192,64},{1,129},{65,193},{129,1},{193,65... | collective-permute-start | bytes 393224 | tf_op jit(solution)/shard_map/ppermute | solution.py:33
  24.1 1.9 %collective-permute-done.3.r1 = bf16[256,256]{1,0:T(8,128)(2,1)S(1)} collective-permute-done((bf16[256,256]{1,0:T(8,128)(2,1)S(1)}, bf16[256,256]{1,0:T(8,128)(2,1)S(1)}, u32[]{:S(2)}, u32[]{:S(2)}) %collective-permute-start.3) | collective-permute-done | bytes 131104 | tf_op jit(solution)/shard_map/ppermute | solution.py:33
  26.0 2.0 %collective-permute-done.4.r2 = bf16[256,256]{1,0:T(8,128)(2,1)S(1)} collective-permute-done((bf16[256,256]{1,0:T(8,128)(2,1)S(1)}, bf16[256,256]{1,0:T(8,128)(2,1)S(1)}, u32[]{:S(2)}, u32[]{:S(2)}) %collective-permute-start.4) | collective-permute-done | bytes 131104 | tf_op jit(solution)/shard_map/ppermute | solution.py:33
  28.0 1.6 %collective-permute-done.5.r3 = bf16[256,256]{1,0:T(8,128)(2,1)S(1)} collective-permute-done((bf16[256,256]{1,0:T(8,128)(2,1)S(1)}, bf16[256,256]{1,0:T(8,128)(2,1)S(1)}, u32[]{:S(2)}, u32[]{:S(2)}) %collective-permute-start.5) | collective-permute-done | bytes 131104 | tf_op jit(solution)/shard_map/ppermute | solution.py:33
  29.6 1.7 %collective-permute-done.6.w1.w_near = bf16[256,1024]{1,0:T(8,128)(2,1)S(1)} collective-permute-done((bf16[256,1024]{1,0:T(8,128)(2,1)S(1)}, bf16[256,1024]{1,0:T(8,128)(2,1)S(1)}, u32[]{:S(2)}, u32[]{:S(2)}) %collective-permute-start.6) | collective-permute-done | bytes 524320 | tf_op jit(solution)/shard_map/ppermute | solution.py:43
  31.3 0.7 compact.1.x0.refs_1_
  32.0 4.2 %collective-permute-start.16 = (bf16[8,384,128]{2,1,0:T(8,128)(2,1)S(1)}, bf16[8,384,128]{2,1,0:T(8,128)(2,1)S(1)}, u32[]{:S(2)}, u32[]{:S(2)}) collective-permute-start(bf16[8,384,128]{2,1,0:T(8,128)(2,1)S(1)} %after.2.own), channel_id=1, source_target_pairs={{0,4},{4,0},{8,12},{12,8},{16,20},{20,16},{24,28},{28,24},{32,36},... | collective-permute-start | bytes 2359304 | tf_op jit(solution)/shard_map/ppermute | solution.py:48
  36.7 1.1 %collective-permute-start.8 = (bf16[512,256]{1,0:T(8,128)(2,1)S(1)}, bf16[512,256]{1,0:T(8,128)(2,1)}, u32[]{:S(2)}, u32[]{:S(2)}) collective-permute-start(bf16[512,256]{1,0:T(8,128)(2,1)S(1)} %compact.1.x0.refs_1_), channel_id=1, source_target_pairs={{0,1},{1,2},{2,3},{3,0},{4,5},{5,6},{6,7},{7,4},{8,9},{9,10},{10,1... | collective-permute-start | bytes 786440 | tf_op jit(solution)/shard_map/ppermute | solution.py:33
  37.8 0.5 collective-permute-start.9
  38.3 1.2 %collective-permute-start.14 = (bf16[256,1024]{1,0:T(8,128)(2,1)S(1)}, bf16[256,1024]{1,0:T(8,128)(2,1)}, u32[]{:S(2)}, u32[]{:S(2)}) collective-permute-start(bf16[256,1024]{1,0:T(8,128)(2,1)S(1)} %collective-permute-done.6.w1.w_near), channel_id=1, source_target_pairs={{0,4},{4,0},{8,12},{12,8},{16,20},{20,16},{24,28},{28,24},{32,36},... | collective-permute-start | bytes 1572872 | tf_op jit(solution)/shard_map/ppermute | solution.py:48
  39.6 2.8 %attend.1 = bf16[8,128,128]{2,1,0:T(8,128)(2,1)} custom-call(bf16[8,384,128]{2,1,0:T(8,128)(2,1)S(1)} %after.2.own, bf16[8,384,128]{2,1,0:T(8,128)(2,1)S(1)} %collective-permute-done.16.other), custom_call_target="tpu_custom_call" | custom-call | flops 10000000000 | bytes 1024 | tf_op jit(solution)/shard_map/attend/pallas_call | solution.py:390
  42.4 6.7 %all-to-all-start.1 = ((bf16[8,128,128]{2,1,0:T(8,128)(2,1)}), bf16[8,128,128]{2,1,0:T(8,128)(2,1)S(1)}, u32[]{:S(2)}, u32[]{:S(2)}) async-start(bf16[8,128,128]{2,1,0:T(8,128)(2,1)} %attend.1), calls=%async_computation.1 | async-start | bytes 524288 | tf_op jit(solution)/shard_map/all_to_all | solution.py:57
  49.0 0.8 %collective-permute-done.9.x2 = bf16[512,256]{1,0:T(8,128)(2,1)} collective-permute-done((bf16[512,256]{1,0:T(8,128)(2,1)S(1)}, bf16[512,256]{1,0:T(8,128)(2,1)}, u32[]{:S(2)}, u32[]{:S(2)}) %collective-permute-start.9) | collective-permute-done | bytes 262176 | tf_op jit(solution)/shard_map/ppermute | solution.py:33
  49.8 2.6 %encode.1 = (bf16[256,256]{1,0:T(8,128)(2,1)S(1)}, bf16[256,256]{1,0:T(8,128)(2,1)S(1)}, bf16[512,1024]{1,0:T(8,128)(2,1)}) custom-call(bf16[512,256]{1,0:T(8,128)(2,1)S(1)} %compact.1.x0.refs_1_, bf16[512,256]{1,0:T(8,128)(2,1)} %collective-permute-done.8.x1, bf16[512,256]{1,0:T(8,128)(2,1)} %collective-permute-done.9.x2, ...), custom_call_target="tpu_custom_call" | custom-call | flops 30000001024 | bytes 1024 | tf_op jit(solution)/shard_map/encode/pallas_call | solution.py:200
  52.4 1.0 %collective-permute-start.11 = (bf16[256,256]{1,0:T(8,128)(2,1)S(1)}, bf16[256,256]{1,0:T(8,128)(2,1)S(1)}, u32[]{:S(2)}, u32[]{:S(2)}) collective-permute-start(bf16[256,256]{1,0:T(8,128)(2,1)S(1)} %get-tuple-element.25.refs_2_), channel_id=1, source_target_pairs={{0,1},{1,2},{2,3},{3,0},{4,5},{5,6},{6,7},{7,4},{8,9},{9,10},{10,1... | collective-permute-start | bytes 393224 | tf_op jit(solution)/shard_map/ppermute | solution.py:33
  53.4 2.4 %collective-permute-start.12 = (bf16[256,256]{1,0:T(8,128)(2,1)S(1)}, bf16[256,256]{1,0:T(8,128)(2,1)S(1)}, u32[]{:S(2)}, u32[]{:S(2)}) collective-permute-start(bf16[256,256]{1,0:T(8,128)(2,1)S(1)} %get-tuple-element.25.refs_2_), channel_id=1, source_target_pairs={{0,2},{1,3},{2,0},{3,1},{4,6},{5,7},{6,4},{7,5},{8,10},{9,11},{10,... | collective-permute-start | bytes 393224 | tf_op jit(solution)/shard_map/ppermute | solution.py:33
  55.8 1.1 %collective-permute-start.13 = (bf16[256,256]{1,0:T(8,128)(2,1)S(1)}, bf16[256,256]{1,0:T(8,128)(2,1)S(1)}, u32[]{:S(2)}, u32[]{:S(2)}) collective-permute-start(bf16[256,256]{1,0:T(8,128)(2,1)S(1)} %get-tuple-element.25.refs_2_), channel_id=1, source_target_pairs={{0,3},{1,0},{2,1},{3,2},{4,7},{5,4},{6,5},{7,6},{8,11},{9,8},{10,9... | collective-permute-start | bytes 393224 | tf_op jit(solution)/shard_map/ppermute | solution.py:33
  57.0 1.8 %load.1 = (bf16[1024,1024]{1,0:T(8,128)(2,1)S(1)}, bf16[128,1024]{1,0:T(8,128)(2,1)S(1)}, bf16[128,1024]{1,0:T(8,128)(2,1)S(1)}) custom-call(bf16[256,1024]{1,0:T(8,128)(2,1)} %w0.1, bf16[256,1024]{1,0:T(8,128)(2,1)} %copy-done.5, bf16[128,1024]{1,0:T(8,128)(2,1)} %copy-done.7, bf16[256,1024]{1,0:T(8,128)(2,1)} %collective-permute-done.14.s_near, ...), custom_call_target="tpu_custom_call" | custom-call | flops 3000000000 | bytes 1024 | tf_op jit(solution)/shard_map/load/pallas_call | solution.py:235
  59.3 1.1 %collective-permute-start.19 = (bf16[256,256]{1,0:T(8,128)(2,1)S(1)}, bf16[256,256]{1,0:T(8,128)(2,1)S(1)}, u32[]{:S(2)}, u32[]{:S(2)}) collective-permute-start(bf16[256,256]{1,0:T(8,128)(2,1)S(1)} %after.3.refs_2_), channel_id=1, source_target_pairs={{0,2},{1,3},{2,0},{3,1},{4,6},{5,7},{6,4},{7,5},{8,10},{9,11},{10,... | collective-permute-start | bytes 393224 | tf_op jit(solution)/shard_map/ppermute | solution.py:33
  60.4 1.7 %collective-permute-start.20 = (bf16[256,256]{1,0:T(8,128)(2,1)S(1)}, bf16[256,256]{1,0:T(8,128)(2,1)S(1)}, u32[]{:S(2)}, u32[]{:S(2)}) collective-permute-start(bf16[256,256]{1,0:T(8,128)(2,1)S(1)} %after.3.refs_2_), channel_id=1, source_target_pairs={{0,3},{1,0},{2,1},{3,2},{4,7},{5,4},{6,5},{7,6},{8,11},{9,8},{10,9... | collective-permute-start | bytes 393224 | tf_op jit(solution)/shard_map/ppermute | solution.py:33
  62.2 3.4 %cross.2.second = bf16[64,1024]{1,0:T(8,128)(2,1)S(1)} custom-call(s32[1,32]{1,0:T(1,128)S(1)} %copy-done.8, bf16[512,1024]{1,0:T(8,128)(2,1)} %get-tuple-element.24.refs_1_, bf16[256,256]{1,0:T(8,128)(2,1)S(1)} %get-tuple-element.25.refs_2_, bf16[256,256]{1,0:T(8,128)(2,1)S(1)} %collective-permute-done.11.refs_3_, ...), custom_call_target="tpu_custom_call" | custom-call | flops 5000000000 | bytes 1024 | tf_op jit(solution)/shard_map/cross/pallas_call | solution.py:284
  65.5 4.7 %collective-permute-start.17 = (bf16[64,1024]{1,0:T(8,128)(2,1)S(1)}, bf16[64,1024]{1,0:T(8,128)(2,1)S(1)}, u32[]{:S(2)}, u32[]{:S(2)}) collective-permute-start(bf16[64,1024]{1,0:T(8,128)(2,1)S(1)} %cross.2.second), channel_id=1, source_target_pairs={{0,4},{4,8},{8,12},{12,16},{16,20},{20,24},{24,28},{28,32},{32,36}... | collective-permute-start | bytes 393224 | tf_op jit(solution)/shard_map/ppermute | solution.py:33
  70.3 3.4 %cross.3.first = bf16[64,1024]{1,0:T(8,128)(2,1)S(1)} custom-call(s32[1,32]{1,0:T(1,128)S(1)} %copy-done.8, bf16[512,1024]{1,0:T(8,128)(2,1)} %get-tuple-element.24.refs_1_, bf16[256,256]{1,0:T(8,128)(2,1)S(1)} %after.3.refs_2_, bf16[256,256]{1,0:T(8,128)(2,1)S(1)} %collective-permute-done.18.refs_3_, bf16[256,256]{1,0:T(8,128)(2,1)S(1)} %collective-permute-done.19.refs_4_, ...), custom_call_target="tpu_custom_call" | custom-call | flops 5000000000 | bytes 1024 | tf_op jit(solution)/shard_map/cross/pallas_call | solution.py:284
  73.7 0.8 %place.1 = bf16[1,128,1024]{2,1,0:T(8,128)(2,1)} custom-call(bf16[64,1024]{1,0:T(8,128)(2,1)S(1)} %collective-permute-done.17.received, bf16[64,1024]{1,0:T(8,128)(2,1)S(1)} %cross.3.first, bf16[64,1024]{1,0:T(8,128)(2,1)S(1)} %cross.2.second), custom_call_target="tpu_custom_call" | custom-call | flops 1000000000 | bytes 1024 | tf_op jit(solution)/shard_map/place/pallas_call | solution.py:408
  (45 shorter events, 1.7 us)
Async XLA Ops:
  0.0 17.1 %copy-start.9 = (bf16[256,1024]{1,0:T(8,128)(2,1)S(1)}, bf16[256,1024]{1,0:T(8,128)(2,1)}, u32[]{:S(2)}) copy-start(bf16[256,1024]{1,0:T(8,128)(2,1)} %w0.1) | copy-start | bytes 1572868
  2.2 29.8 %all-to-all-start = ((bf16[8,384,128]{2,1,0:T(8,128)(2,1)}), bf16[8,384,128]{2,1,0:T(8,128)(2,1)S(1)}, u32[]{:S(2)}, u32[]{:S(2)}) async-start(bf16[8,384,128]{2,1,0:T(8,128)(2,1)} %get-tuple-element.26), calls=%async_computation | async-start | bytes 1572864 | tf_op jit(solution)/shard_map/all_to_all | solution.py:57
  12.1 8.0 %collective-permute-start = (s32[4]{0:T(128)S(1)}, s32[4]{0:T(128)S(1)}, u32[]{:S(2)}, u32[]{:S(2)}) collective-permute-start(s32[4]{0:T(128)S(1)} %get-tuple-element.18.idx0.idx), channel_id=1, source_target_pairs={{0,64},{64,128},{128,192},{192,0},{1,65},{65,129},{129,193},{193,1... | collective-permute-start | bytes 56 | tf_op jit(solution)/shard_map/ppermute | solution.py:33
  13.4 6.7 %collective-permute-start.1 = (s32[4]{0:T(128)S(1)}, s32[4]{0:T(128)S(1)}, u32[]{:S(2)}, u32[]{:S(2)}) collective-permute-start(s32[4]{0:T(128)S(1)} %get-tuple-element.18.idx0.idx), channel_id=1, source_target_pairs={{0,128},{64,192},{128,0},{192,64},{1,129},{65,193},{129,1},{193,65... | collective-permute-start | bytes 56 | tf_op jit(solution)/shard_map/ppermute | solution.py:33
  16.0 4.1 %collective-permute-start.2 = (s32[4]{0:T(128)S(1)}, s32[4]{0:T(128)S(1)}, u32[]{:S(2)}, u32[]{:S(2)}) collective-permute-start(s32[4]{0:T(128)S(1)} %get-tuple-element.18.idx0.idx), channel_id=1, source_target_pairs={{0,192},{64,0},{128,64},{192,128},{1,193},{65,1},{129,65},{193,129... | collective-permute-start | bytes 56 | tf_op jit(solution)/shard_map/ppermute | solution.py:33
  17.1 14.2 %collective-permute-start.6 = (bf16[256,1024]{1,0:T(8,128)(2,1)S(1)}, bf16[256,1024]{1,0:T(8,128)(2,1)S(1)}, u32[]{:S(2)}, u32[]{:S(2)}) collective-permute-start(bf16[256,1024]{1,0:T(8,128)(2,1)S(1)} %copy-done.9), channel_id=1, source_target_pairs={{0,1},{1,2},{2,3},{3,0},{4,7},{5,4},{6,5},{7,6},{8,9},{9,10},{10,1... | collective-permute-start | bytes 1572872 | tf_op jit(solution)/shard_map/ppermute | solution.py:43
  19.5 10.0 %collective-permute-start.7 = (bf16[128,1024]{1,0:T(8,128)(2,1)S(1)}, bf16[128,1024]{1,0:T(8,128)(2,1)S(1)}, u32[]{:S(2)}, u32[]{:S(2)}) collective-permute-start(bf16[128,1024]{1,0:T(8,128)(2,1)S(1)} %get-tuple-element.23), channel_id=1, source_target_pairs={{0,2},{1,3},{2,0},{3,1},{4,6},{5,7},{6,4},{7,5},{8,10},{9,11},{10,... | collective-permute-start | bytes 786440 | tf_op jit(solution)/shard_map/ppermute | solution.py:33
  21.8 4.2 %collective-permute-start.3 = (bf16[256,256]{1,0:T(8,128)(2,1)S(1)}, bf16[256,256]{1,0:T(8,128)(2,1)S(1)}, u32[]{:S(2)}, u32[]{:S(2)}) collective-permute-start(bf16[256,256]{1,0:T(8,128)(2,1)S(1)} %get-tuple-element.20), channel_id=1, source_target_pairs={{0,192},{64,0},{128,64},{192,128},{1,193},{65,1},{129,65},{193,129... | collective-permute-start | bytes 393224 | tf_op jit(solution)/shard_map/ppermute | solution.py:33
  22.6 5.5 %collective-permute-start.4 = (bf16[256,256]{1,0:T(8,128)(2,1)S(1)}, bf16[256,256]{1,0:T(8,128)(2,1)S(1)}, u32[]{:S(2)}, u32[]{:S(2)}) collective-permute-start(bf16[256,256]{1,0:T(8,128)(2,1)S(1)} %get-tuple-element.21), channel_id=1, source_target_pairs={{0,128},{64,192},{128,0},{192,64},{1,129},{65,193},{129,1},{193,65... | collective-permute-start | bytes 393224 | tf_op jit(solution)/shard_map/ppermute | solution.py:33
  24.1 5.5 %collective-permute-start.5 = (bf16[256,256]{1,0:T(8,128)(2,1)S(1)}, bf16[256,256]{1,0:T(8,128)(2,1)S(1)}, u32[]{:S(2)}, u32[]{:S(2)}) collective-permute-start(bf16[256,256]{1,0:T(8,128)(2,1)S(1)} %get-tuple-element.22), channel_id=1, source_target_pairs={{0,64},{64,128},{128,192},{192,0},{1,65},{65,129},{129,193},{193,1... | collective-permute-start | bytes 393224 | tf_op jit(solution)/shard_map/ppermute | solution.py:33
  29.6 6.6 %copy-start.7 = (bf16[128,1024]{1,0:T(8,128)(2,1)}, bf16[128,1024]{1,0:T(8,128)(2,1)S(1)}, u32[]{:S(2)}) copy-start(bf16[128,1024]{1,0:T(8,128)(2,1)S(1)} %collective-permute-done.7.w2.w_half) | copy-start | bytes 786436
  31.3 7.1 %copy-start.5 = (bf16[256,1024]{1,0:T(8,128)(2,1)}, bf16[256,1024]{1,0:T(8,128)(2,1)S(1)}, u32[]{:S(2)}) copy-start(bf16[256,1024]{1,0:T(8,128)(2,1)S(1)} %collective-permute-done.6.w1.w_near) | copy-start | bytes 1572868
  32.0 17.8 %copy-start.2 = (bf16[1024,256]{1,0:T(8,128)(2,1)S(1)}, bf16[1024,256]{1,0:T(8,128)(2,1)}, u32[]{:S(2)}) copy-start(bf16[1024,256]{1,0:T(8,128)(2,1)} %wq.2) | copy-start | bytes 1572868
  32.0 17.8 %copy-start.3 = (bf16[1024,256]{1,0:T(8,128)(2,1)S(1)}, bf16[1024,256]{1,0:T(8,128)(2,1)}, u32[]{:S(2)}) copy-start(bf16[1024,256]{1,0:T(8,128)(2,1)} %wk.1) | copy-start | bytes 1572868
  32.0 17.8 %copy-start.4 = (bf16[1024,256]{1,0:T(8,128)(2,1)S(1)}, bf16[1024,256]{1,0:T(8,128)(2,1)}, u32[]{:S(2)}) copy-start(bf16[1024,256]{1,0:T(8,128)(2,1)} %wv.1) | copy-start | bytes 1572868
  32.0 6.3 %collective-permute-start.16 = (bf16[8,384,128]{2,1,0:T(8,128)(2,1)S(1)}, bf16[8,384,128]{2,1,0:T(8,128)(2,1)S(1)}, u32[]{:S(2)}, u32[]{:S(2)}) collective-permute-start(bf16[8,384,128]{2,1,0:T(8,128)(2,1)S(1)} %after.2.own), channel_id=1, source_target_pairs={{0,4},{4,0},{8,12},{12,8},{16,20},{20,16},{24,28},{28,24},{32,36},... | collective-permute-start | bytes 2359304 | tf_op jit(solution)/shard_map/ppermute | solution.py:48
  36.2 20.7 %collective-permute-start.15 = (bf16[128,1024]{1,0:T(8,128)(2,1)S(1)}, bf16[128,1024]{1,0:T(8,128)(2,1)}, u32[]{:S(2)}, u32[]{:S(2)}) collective-permute-start(bf16[128,1024]{1,0:T(8,128)(2,1)S(1)} %collective-permute-done.7.w2.w_half), channel_id=1, source_target_pairs={{0,4},{4,0},{8,12},{12,8},{16,20},{20,16},{24,28},{28,24},{32,36},... | collective-permute-start | bytes 786440 | tf_op jit(solution)/shard_map/ppermute | solution.py:48
  36.3 12.7 %collective-permute-start.10 = (bf16[512,256]{1,0:T(8,128)(2,1)S(1)}, bf16[512,256]{1,0:T(8,128)(2,1)}, u32[]{:S(2)}, u32[]{:S(2)}) collective-permute-start(bf16[512,256]{1,0:T(8,128)(2,1)S(1)} %compact.1.x0.refs_1_), channel_id=1, source_target_pairs={{0,3},{1,0},{2,1},{3,2},{4,7},{5,4},{6,5},{7,6},{8,11},{9,8},{10,9... | collective-permute-start | bytes 786440 | tf_op jit(solution)/shard_map/ppermute | solution.py:33
  36.7 12.3 %collective-permute-start.8 = (bf16[512,256]{1,0:T(8,128)(2,1)S(1)}, bf16[512,256]{1,0:T(8,128)(2,1)}, u32[]{:S(2)}, u32[]{:S(2)}) collective-permute-start(bf16[512,256]{1,0:T(8,128)(2,1)S(1)} %compact.1.x0.refs_1_), channel_id=1, source_target_pairs={{0,1},{1,2},{2,3},{3,0},{4,5},{5,6},{6,7},{7,4},{8,9},{9,10},{10,1... | collective-permute-start | bytes 786440 | tf_op jit(solution)/shard_map/ppermute | solution.py:33
  37.8 12.0 %collective-permute-start.9 = (bf16[512,256]{1,0:T(8,128)(2,1)S(1)}, bf16[512,256]{1,0:T(8,128)(2,1)}, u32[]{:S(2)}, u32[]{:S(2)}) collective-permute-start(bf16[512,256]{1,0:T(8,128)(2,1)S(1)} %compact.1.x0.refs_1_), channel_id=1, source_target_pairs={{0,2},{1,3},{2,0},{3,1},{4,6},{5,7},{6,4},{7,5},{8,10},{9,11},{10,... | collective-permute-start | bytes 786440 | tf_op jit(solution)/shard_map/ppermute | solution.py:33
  38.3 18.6 %collective-permute-start.14 = (bf16[256,1024]{1,0:T(8,128)(2,1)S(1)}, bf16[256,1024]{1,0:T(8,128)(2,1)}, u32[]{:S(2)}, u32[]{:S(2)}) collective-permute-start(bf16[256,1024]{1,0:T(8,128)(2,1)S(1)} %collective-permute-done.6.w1.w_near), channel_id=1, source_target_pairs={{0,4},{4,0},{8,12},{12,8},{16,20},{20,16},{24,28},{28,24},{32,36},... | collective-permute-start | bytes 1572872 | tf_op jit(solution)/shard_map/ppermute | solution.py:48
  42.4 14.6 %all-to-all-start.1 = ((bf16[8,128,128]{2,1,0:T(8,128)(2,1)}), bf16[8,128,128]{2,1,0:T(8,128)(2,1)S(1)}, u32[]{:S(2)}, u32[]{:S(2)}) async-start(bf16[8,128,128]{2,1,0:T(8,128)(2,1)} %attend.1), calls=%async_computation.1 | async-start | bytes 524288 | tf_op jit(solution)/shard_map/all_to_all | solution.py:57
  49.0 7.9 %copy-start.6 = (bf16[8,128,128]{2,1,0:T(8,128)(2,1)S(1)}, bf16[8,128,128]{2,1,0:T(8,128)(2,1)}, u32[]{:S(2)}) copy-start(bf16[8,128,128]{2,1,0:T(8,128)(2,1)} %wq.3) | copy-start | bytes 786436
  52.4 8.0 %collective-permute-start.11 = (bf16[256,256]{1,0:T(8,128)(2,1)S(1)}, bf16[256,256]{1,0:T(8,128)(2,1)S(1)}, u32[]{:S(2)}, u32[]{:S(2)}) collective-permute-start(bf16[256,256]{1,0:T(8,128)(2,1)S(1)} %get-tuple-element.25.refs_2_), channel_id=1, source_target_pairs={{0,1},{1,2},{2,3},{3,0},{4,5},{5,6},{6,7},{7,4},{8,9},{9,10},{10,1... | collective-permute-start | bytes 393224 | tf_op jit(solution)/shard_map/ppermute | solution.py:33
  53.4 8.7 %collective-permute-start.12 = (bf16[256,256]{1,0:T(8,128)(2,1)S(1)}, bf16[256,256]{1,0:T(8,128)(2,1)S(1)}, u32[]{:S(2)}, u32[]{:S(2)}) collective-permute-start(bf16[256,256]{1,0:T(8,128)(2,1)S(1)} %get-tuple-element.25.refs_2_), channel_id=1, source_target_pairs={{0,2},{1,3},{2,0},{3,1},{4,6},{5,7},{6,4},{7,5},{8,10},{9,11},{10,... | collective-permute-start | bytes 393224 | tf_op jit(solution)/shard_map/ppermute | solution.py:33
  55.8 6.4 %collective-permute-start.13 = (bf16[256,256]{1,0:T(8,128)(2,1)S(1)}, bf16[256,256]{1,0:T(8,128)(2,1)S(1)}, u32[]{:S(2)}, u32[]{:S(2)}) collective-permute-start(bf16[256,256]{1,0:T(8,128)(2,1)S(1)} %get-tuple-element.25.refs_2_), channel_id=1, source_target_pairs={{0,3},{1,0},{2,1},{3,2},{4,7},{5,4},{6,5},{7,6},{8,11},{9,8},{10,9... | collective-permute-start | bytes 393224 | tf_op jit(solution)/shard_map/ppermute | solution.py:33
  57.0 5.2 %copy-start.1 = (bf16[1024,1024]{1,0:T(8,128)(2,1)S(1)}, bf16[1024,1024]{1,0:T(8,128)(2,1)}, u32[]{:S(2)}) copy-start(bf16[1024,1024]{1,0:T(8,128)(2,1)} %refs_8_.3) | copy-start | bytes 6291460
  58.7 3.4 %copy-start = (bf16[1024,1024]{1,0:T(8,128)(2,1)S(1)}, bf16[1024,1024]{1,0:T(8,128)(2,1)}, u32[]{:S(2)}) copy-start(bf16[1024,1024]{1,0:T(8,128)(2,1)} %refs_7_.3) | copy-start | bytes 6291460
  58.8 11.5 %collective-permute-start.18 = (bf16[256,256]{1,0:T(8,128)(2,1)S(1)}, bf16[256,256]{1,0:T(8,128)(2,1)S(1)}, u32[]{:S(2)}, u32[]{:S(2)}) collective-permute-start(bf16[256,256]{1,0:T(8,128)(2,1)S(1)} %after.3.refs_2_), channel_id=1, source_target_pairs={{0,1},{1,2},{2,3},{3,0},{4,5},{5,6},{6,7},{7,4},{8,9},{9,10},{10,1... | collective-permute-start | bytes 393224 | tf_op jit(solution)/shard_map/ppermute | solution.py:33
  59.3 11.0 %collective-permute-start.19 = (bf16[256,256]{1,0:T(8,128)(2,1)S(1)}, bf16[256,256]{1,0:T(8,128)(2,1)S(1)}, u32[]{:S(2)}, u32[]{:S(2)}) collective-permute-start(bf16[256,256]{1,0:T(8,128)(2,1)S(1)} %after.3.refs_2_), channel_id=1, source_target_pairs={{0,2},{1,3},{2,0},{3,1},{4,6},{5,7},{6,4},{7,5},{8,10},{9,11},{10,... | collective-permute-start | bytes 393224 | tf_op jit(solution)/shard_map/ppermute | solution.py:33
  60.4 9.9 %collective-permute-start.20 = (bf16[256,256]{1,0:T(8,128)(2,1)S(1)}, bf16[256,256]{1,0:T(8,128)(2,1)S(1)}, u32[]{:S(2)}, u32[]{:S(2)}) collective-permute-start(bf16[256,256]{1,0:T(8,128)(2,1)S(1)} %after.3.refs_2_), channel_id=1, source_target_pairs={{0,3},{1,0},{2,1},{3,2},{4,7},{5,4},{6,5},{7,6},{8,11},{9,8},{10,9... | collective-permute-start | bytes 393224 | tf_op jit(solution)/shard_map/ppermute | solution.py:33
  65.5 8.1 %collective-permute-start.17 = (bf16[64,1024]{1,0:T(8,128)(2,1)S(1)}, bf16[64,1024]{1,0:T(8,128)(2,1)S(1)}, u32[]{:S(2)}, u32[]{:S(2)}) collective-permute-start(bf16[64,1024]{1,0:T(8,128)(2,1)S(1)} %cross.2.second), channel_id=1, source_target_pairs={{0,4},{4,8},{8,12},{12,16},{16,20},{20,24},{24,28},{28,32},{32,36}... | collective-permute-start | bytes 393224 | tf_op jit(solution)/shard_map/ppermute | solution.py:33
  (1 other events, 3.4 us)

commit v5 on v4

--- a/solution.py
+++ b/solution.py
@@ -132,7 +132,7 @@
     )(*idx, in_hbm(memory))
 
 
-def compact_kernel(idx, r0, r1, r2, r3, w1, w2, out):
+def compact_kernel(idx, r0, r1, r2, r3, out):
     me = lax.axis_index("enc")
     for span in range(2):
         for j in range(K_NB):
@@ -145,17 +145,17 @@
                     out[begin : begin + NT] = r[span * NT : (span + 1) * NT]
 
 
-def compact(idx, received, others):
+def compact(idx, received):
     rows, cols = received[0].shape
     return pl.pallas_call(
         compact_kernel,
         out_shape=sds((K_NB * rows, cols)),
-        in_specs=[SMEM] + [VMEM] * 4 + [ANY] * 2,
+        in_specs=[SMEM] + [VMEM] * 4,
         out_specs=VMEM,
         compiler_params=params(4),
         cost_estimate=cost(1 * 10**9, 1024),
         name="compact",
-    )(idx, *received, *others)
+    )(idx, *received)
 
 
 def source_columns(k, width):
@@ -427,10 +427,10 @@
 
     sent = fetch(asked, memory)
     received = [sent[0]] + [shifted(sent[k], "enc", -k) for k in range(1, N_ENC)]
-    mine = compact(idx, received, (near, far))
+    mine = compact(idx, received)
     pieces = [mine] + [shifted(mine, "mp", k) for k in range(1, N_MP)]
 
-    packed = after(packed, mine)
+    packed = after(packed, mine, near, far)
     heads = over_z(attend(packed, core_swap(packed)))
 
     early, late, source = encode(pieces, enc_wq, enc_wk, enc_wv)

time: 74.9 us -> 74.4 us (level)
  transfers between devices with their start and end apart: 23 -> 23, of which waited for: 5 -> 6; matrix products, arithmetic and copies ran while one was open for 0% -> 0% of each run, Pallas kernels for 22% -> 22%
where the time goes in v5:
time: 74.4 us; the launch traced here: 73.9 us
  starting transfers between devices  46.5 us (62%)
  Pallas kernels  19.2 us (26%)
  waiting for transfers between devices  8.01 us (11%)
    ppermute x17, starting transfers between devices, shifted(): lax.ppermute(block, axis, [(i, (i + distance) % size) for i in range(size)])  22.4 us
    all_to_all x2, starting transfers between devices, over_z(): lax.all_to_all(blocks, 'seq', 0, 0, axis_index_groups=groups, tiled=True)  16.4 us
    ppermute x17, waiting for transfers between devices, shifted(): lax.ppermute(block, axis, [(i, (i + distance) % size) for i in range(size)])  6.92 us
    pallas_call x2, Pallas kernels, cross(): pl.pallas_call(body, out_shape=sds((SPAN, cols)), in_specs=[SMEM] + [ANY]...  6.72 us
    ppermute x3, starting transfers between devices, core_swap(): return lax.ppermute(block, 'seq', [(i, i ^ 1) for i in range(size)])  5.14 us
    pallas_call x1, Pallas kernels, attend(): pl.pallas_call(attend_kernel, out_shape=sds((N_Z, tok, HEAD_DIM)), in_spe...  2.76 us
    pallas_call x1, Pallas kernels, encode(): pl.pallas_call(encode_kernel, out_shape=[sds((rows // 2, width))] * 2 + [...  2.57 us
    ppermute x1, starting transfers between devices, to_sides(): return lax.ppermute(block, ('seq', 'mp'), route)  2.48 us
  transfers between devices with their start and end apart: 23, of which 6 were waited for; matrix products, arithmetic and copies ran while one was open for 0% of the time, Pallas kernels for 22%

profile of v5, /device:TPU:1, one launch (start us, length us, event | category | flops | bytes accessed | tf_op | source)
XLA Modules:
  0.0 73.9 jit_solution(2139331907107611911)
XLA Ops:
  0.0 2.2 %pack.1 = (bf16[8,384,128]{2,1,0:T(8,128)(2,1)}, s32[4]{0:T(128)S(1)}, bf16[128,1024]{1,0:T(8,128)(2,1)S(1)}) custom-call(bf16[1,128,1024]{2,1,0:T(8,128)(2,1)} %q.1, bf16[1,128,1024]{2,1,0:T(8,128)(2,1)} %k.1, bf16[1,128,1024]{2,1,0:T(8,128)(2,1)} %v.1, bf16[256,1024]{1,0:T(8,128)(2,1)} %w0.1, s32[1,2,2]{2,1,0:T(2,128)} %nbr_rows.1, s32[1,2,2]{2,1,0:T(2,128)} %nbr_owner.1), custom_call_target="tpu_custom_call" | custom-call | flops 1000000000 | bytes 1024 | tf_op jit(solution)/shard_map/pack/pallas_call | solution.py:323
  2.2 9.9 %all-to-all-start = ((bf16[8,384,128]{2,1,0:T(8,128)(2,1)}), bf16[8,384,128]{2,1,0:T(8,128)(2,1)S(1)}, u32[]{:S(2)}, u32[]{:S(2)}) async-start(bf16[8,384,128]{2,1,0:T(8,128)(2,1)} %get-tuple-element.26), calls=%async_computation | async-start | bytes 1572864 | tf_op jit(solution)/shard_map/all_to_all | solution.py:57
  12.1 1.3 %collective-permute-start = (s32[4]{0:T(128)S(1)}, s32[4]{0:T(128)S(1)}, u32[]{:S(2)}, u32[]{:S(2)}) collective-permute-start(s32[4]{0:T(128)S(1)} %get-tuple-element.18.idx0.idx), channel_id=1, source_target_pairs={{0,64},{64,128},{128,192},{192,0},{1,65},{65,129},{129,193},{193,1... | collective-permute-start | bytes 56 | tf_op jit(solution)/shard_map/ppermute | solution.py:33
  13.4 2.6 %collective-permute-start.1 = (s32[4]{0:T(128)S(1)}, s32[4]{0:T(128)S(1)}, u32[]{:S(2)}, u32[]{:S(2)}) collective-permute-start(s32[4]{0:T(128)S(1)} %get-tuple-element.18.idx0.idx), channel_id=1, source_target_pairs={{0,128},{64,192},{128,0},{192,64},{1,129},{65,193},{129,1},{193,65... | collective-permute-start | bytes 56 | tf_op jit(solution)/shard_map/ppermute | solution.py:33
  16.0 1.1 %collective-permute-start.2 = (s32[4]{0:T(128)S(1)}, s32[4]{0:T(128)S(1)}, u32[]{:S(2)}, u32[]{:S(2)}) collective-permute-start(s32[4]{0:T(128)S(1)} %get-tuple-element.18.idx0.idx), channel_id=1, source_target_pairs={{0,192},{64,0},{128,64},{192,128},{1,193},{65,1},{129,65},{193,129... | collective-permute-start | bytes 56 | tf_op jit(solution)/shard_map/ppermute | solution.py:33
  17.1 2.5 %collective-permute-start.12 = (bf16[256,1024]{1,0:T(8,128)(2,1)S(1)}, bf16[256,1024]{1,0:T(8,128)(2,1)S(1)}, u32[]{:S(2)}, u32[]{:S(2)}) collective-permute-start(bf16[256,1024]{1,0:T(8,128)(2,1)S(1)} %copy-done.9), channel_id=1, source_target_pairs={{0,1},{1,2},{2,3},{3,0},{4,7},{5,4},{6,5},{7,6},{8,9},{9,10},{10,1... | collective-permute-start | bytes 1572872 | tf_op jit(solution)/shard_map/ppermute | solution.py:43
  20.1 1.7 %fetch.1 = (bf16[256,256]{1,0:T(8,128)(2,1)S(1)}, bf16[256,256]{1,0:T(8,128)(2,1)S(1)}, bf16[256,256]{1,0:T(8,128)(2,1)S(1)}, bf16[256,256]{1,0:T(8,128)(2,1)S(1)}) custom-call(s32[4]{0:T(128)S(1)} %get-tuple-element.18.idx0.idx, s32[4]{0:T(128)S(1)} %collective-permute-done.idx1, s32[4]{0:T(128)S(1)} %collective-permute-done.1.idx2, ...), custom_call_target="tpu_custom_call" | custom-call | flops 5000000000 | bytes 1024 | tf_op jit(solution)/shard_map/fetch/pallas_call | solution.py:123
  21.8 0.7 collective-permute-start.3
  22.5 1.7 %collective-permute-start.4 = (bf16[256,256]{1,0:T(8,128)(2,1)S(1)}, bf16[256,256]{1,0:T(8,128)(2,1)S(1)}, u32[]{:S(2)}, u32[]{:S(2)}) collective-permute-start(bf16[256,256]{1,0:T(8,128)(2,1)S(1)} %get-tuple-element.21), channel_id=1, source_target_pairs={{0,128},{64,192},{128,0},{192,64},{1,129},{65,193},{129,1},{193,65... | collective-permute-start | bytes 393224 | tf_op jit(solution)/shard_map/ppermute | solution.py:33
  24.1 1.9 %collective-permute-done.3.r1 = bf16[256,256]{1,0:T(8,128)(2,1)S(1)} collective-permute-done((bf16[256,256]{1,0:T(8,128)(2,1)S(1)}, bf16[256,256]{1,0:T(8,128)(2,1)S(1)}, u32[]{:S(2)}, u32[]{:S(2)}) %collective-permute-start.3) | collective-permute-done | bytes 131104 | tf_op jit(solution)/shard_map/ppermute | solution.py:33
  26.0 1.9 %collective-permute-done.4.r2 = bf16[256,256]{1,0:T(8,128)(2,1)S(1)} collective-permute-done((bf16[256,256]{1,0:T(8,128)(2,1)S(1)}, bf16[256,256]{1,0:T(8,128)(2,1)S(1)}, u32[]{:S(2)}, u32[]{:S(2)}) %collective-permute-start.4) | collective-permute-done | bytes 131104 | tf_op jit(solution)/shard_map/ppermute | solution.py:33
  27.9 1.6 %collective-permute-done.5.r3 = bf16[256,256]{1,0:T(8,128)(2,1)S(1)} collective-permute-done((bf16[256,256]{1,0:T(8,128)(2,1)S(1)}, bf16[256,256]{1,0:T(8,128)(2,1)S(1)}, u32[]{:S(2)}, u32[]{:S(2)}) %collective-permute-start.5) | collective-permute-done | bytes 131104 | tf_op jit(solution)/shard_map/ppermute | solution.py:33
  29.5 0.7 compact.1.x0.refs_1_
  30.2 1.1 %collective-permute-done.12.refs_2_.w_near = bf16[256,1024]{1,0:T(8,128)(2,1)S(1)} collective-permute-done((bf16[256,1024]{1,0:T(8,128)(2,1)S(1)}, bf16[256,1024]{1,0:T(8,128)(2,1)S(1)}, u32[]{:S(2)}, u32[]{:S(2)}) %collective-permute-start.12) | collective-permute-done | bytes 524320 | tf_op jit(solution)/shard_map/ppermute | solution.py:43
  31.3 4.2 %collective-permute-start.16 = (bf16[8,384,128]{2,1,0:T(8,128)(2,1)S(1)}, bf16[8,384,128]{2,1,0:T(8,128)(2,1)S(1)}, u32[]{:S(2)}, u32[]{:S(2)}) collective-permute-start(bf16[8,384,128]{2,1,0:T(8,128)(2,1)S(1)} %after.2.own), channel_id=1, source_target_pairs={{0,4},{4,0},{8,12},{12,8},{16,20},{20,16},{24,28},{28,24},{32,36},... | collective-permute-start | bytes 2359304 | tf_op jit(solution)/shard_map/ppermute | solution.py:48
  35.5 2.3 %collective-permute-start.7 = (bf16[512,256]{1,0:T(8,128)(2,1)S(1)}, bf16[512,256]{1,0:T(8,128)(2,1)}, u32[]{:S(2)}, u32[]{:S(2)}) collective-permute-start(bf16[512,256]{1,0:T(8,128)(2,1)S(1)} %compact.1.x0.refs_1_), channel_id=1, source_target_pairs={{0,2},{1,3},{2,0},{3,1},{4,6},{5,7},{6,4},{7,5},{8,10},{9,11},{10,... | collective-permute-start | bytes 786440 | tf_op jit(solution)/shard_map/ppermute | solution.py:33
  37.8 1.0 %collective-permute-start.8 = (bf16[512,256]{1,0:T(8,128)(2,1)S(1)}, bf16[512,256]{1,0:T(8,128)(2,1)}, u32[]{:S(2)}, u32[]{:S(2)}) collective-permute-start(bf16[512,256]{1,0:T(8,128)(2,1)S(1)} %compact.1.x0.refs_1_), channel_id=1, source_target_pairs={{0,3},{1,0},{2,1},{3,2},{4,7},{5,4},{6,5},{7,6},{8,11},{9,8},{10,9... | collective-permute-start | bytes 786440 | tf_op jit(solution)/shard_map/ppermute | solution.py:33
  38.9 0.9 %collective-permute-start.15 = (bf16[128,1024]{1,0:T(8,128)(2,1)S(1)}, bf16[128,1024]{1,0:T(8,128)(2,1)}, u32[]{:S(2)}, u32[]{:S(2)}) collective-permute-start(bf16[128,1024]{1,0:T(8,128)(2,1)S(1)} %collective-permute-done.13.refs_3_.w_half), channel_id=1, source_target_pairs={{0,4},{4,0},{8,12},{12,8},{16,20},{20,16},{24,28},{28,24},{32,36},... | collective-permute-start | bytes 786440 | tf_op jit(solution)/shard_map/ppermute | solution.py:48
  39.8 2.8 %attend.1 = bf16[8,128,128]{2,1,0:T(8,128)(2,1)} custom-call(bf16[8,384,128]{2,1,0:T(8,128)(2,1)S(1)} %after.2.own, bf16[8,384,128]{2,1,0:T(8,128)(2,1)S(1)} %collective-permute-done.16.other), custom_call_target="tpu_custom_call" | custom-call | flops 10000000000 | bytes 1024 | tf_op jit(solution)/shard_map/attend/pallas_call | solution.py:390
  42.6 6.6 %all-to-all-start.1 = ((bf16[8,128,128]{2,1,0:T(8,128)(2,1)}), bf16[8,128,128]{2,1,0:T(8,128)(2,1)S(1)}, u32[]{:S(2)}, u32[]{:S(2)}) async-start(bf16[8,128,128]{2,1,0:T(8,128)(2,1)} %attend.1), calls=%async_computation.1 | async-start | bytes 524288 | tf_op jit(solution)/shard_map/all_to_all | solution.py:57
  49.1 0.9 %collective-permute-done.7.x2 = bf16[512,256]{1,0:T(8,128)(2,1)} collective-permute-done((bf16[512,256]{1,0:T(8,128)(2,1)S(1)}, bf16[512,256]{1,0:T(8,128)(2,1)}, u32[]{:S(2)}, u32[]{:S(2)}) %collective-permute-start.7) | collective-permute-done | bytes 262176 | tf_op jit(solution)/shard_map/ppermute | solution.py:33
  50.0 0.6 collective-permute-done.8.x3
  50.6 2.6 %encode.1 = (bf16[256,256]{1,0:T(8,128)(2,1)S(1)}, bf16[256,256]{1,0:T(8,128)(2,1)S(1)}, bf16[512,1024]{1,0:T(8,128)(2,1)}) custom-call(bf16[512,256]{1,0:T(8,128)(2,1)S(1)} %compact.1.x0.refs_1_, bf16[512,256]{1,0:T(8,128)(2,1)} %collective-permute-done.6.x1, bf16[512,256]{1,0:T(8,128)(2,1)} %collective-permute-done.7.x2, ...), custom_call_target="tpu_custom_call" | custom-call | flops 30000001024 | bytes 1024 | tf_op jit(solution)/shard_map/encode/pallas_call | solution.py:200
  53.2 1.3 %collective-permute-start.10 = (bf16[256,256]{1,0:T(8,128)(2,1)S(1)}, bf16[256,256]{1,0:T(8,128)(2,1)S(1)}, u32[]{:S(2)}, u32[]{:S(2)}) collective-permute-start(bf16[256,256]{1,0:T(8,128)(2,1)S(1)} %get-tuple-element.24.refs_2_), channel_id=1, source_target_pairs={{0,2},{1,3},{2,0},{3,1},{4,6},{5,7},{6,4},{7,5},{8,10},{9,11},{10,... | collective-permute-start | bytes 393224 | tf_op jit(solution)/shard_map/ppermute | solution.py:33
  54.6 2.4 %collective-permute-start.11 = (bf16[256,256]{1,0:T(8,128)(2,1)S(1)}, bf16[256,256]{1,0:T(8,128)(2,1)S(1)}, u32[]{:S(2)}, u32[]{:S(2)}) collective-permute-start(bf16[256,256]{1,0:T(8,128)(2,1)S(1)} %get-tuple-element.24.refs_2_), channel_id=1, source_target_pairs={{0,3},{1,0},{2,1},{3,2},{4,7},{5,4},{6,5},{7,6},{8,11},{9,8},{10,9... | collective-permute-start | bytes 393224 | tf_op jit(solution)/shard_map/ppermute | solution.py:33
  57.0 1.8 %load.1 = (bf16[1024,1024]{1,0:T(8,128)(2,1)S(1)}, bf16[128,1024]{1,0:T(8,128)(2,1)S(1)}, bf16[128,1024]{1,0:T(8,128)(2,1)S(1)}) custom-call(bf16[256,1024]{1,0:T(8,128)(2,1)} %w0.1, bf16[256,1024]{1,0:T(8,128)(2,1)} %copy-done, bf16[128,1024]{1,0:T(8,128)(2,1)} %copy-done.1, bf16[256,1024]{1,0:T(8,128)(2,1)} %collective-permute-done.14.s_near, ...), custom_call_target="tpu_custom_call" | custom-call | flops 3000000000 | bytes 1024 | tf_op jit(solution)/shard_map/load/pallas_call | solution.py:235
  58.9 1.5 %collective-permute-start.18 = (bf16[256,256]{1,0:T(8,128)(2,1)S(1)}, bf16[256,256]{1,0:T(8,128)(2,1)S(1)}, u32[]{:S(2)}, u32[]{:S(2)}) collective-permute-start(bf16[256,256]{1,0:T(8,128)(2,1)S(1)} %after.3.refs_2_), channel_id=1, source_target_pairs={{0,1},{1,2},{2,3},{3,0},{4,5},{5,6},{6,7},{7,4},{8,9},{9,10},{10,1... | collective-permute-start | bytes 393224 | tf_op jit(solution)/shard_map/ppermute | solution.py:33
  60.3 2.5 %collective-permute-start.19 = (bf16[256,256]{1,0:T(8,128)(2,1)S(1)}, bf16[256,256]{1,0:T(8,128)(2,1)S(1)}, u32[]{:S(2)}, u32[]{:S(2)}) collective-permute-start(bf16[256,256]{1,0:T(8,128)(2,1)S(1)} %after.3.refs_2_), channel_id=1, source_target_pairs={{0,2},{1,3},{2,0},{3,1},{4,6},{5,7},{6,4},{7,5},{8,10},{9,11},{10,... | collective-permute-start | bytes 393224 | tf_op jit(solution)/shard_map/ppermute | solution.py:33
  62.9 3.4 %cross.2.second = bf16[64,1024]{1,0:T(8,128)(2,1)S(1)} custom-call(s32[1,32]{1,0:T(1,128)S(1)} %copy-done.8, bf16[512,1024]{1,0:T(8,128)(2,1)} %get-tuple-element.23.refs_1_, bf16[256,256]{1,0:T(8,128)(2,1)S(1)} %get-tuple-element.24.refs_2_, bf16[256,256]{1,0:T(8,128)(2,1)S(1)} %collective-permute-done.9.refs_3_, ...), custom_call_target="tpu_custom_call" | custom-call | flops 5000000000 | bytes 1024 | tf_op jit(solution)/shard_map/cross/pallas_call | solution.py:284
  66.2 3.5 %collective-permute-start.17 = (bf16[64,1024]{1,0:T(8,128)(2,1)S(1)}, bf16[64,1024]{1,0:T(8,128)(2,1)S(1)}, u32[]{:S(2)}, u32[]{:S(2)}) collective-permute-start(bf16[64,1024]{1,0:T(8,128)(2,1)S(1)} %cross.2.second), channel_id=1, source_target_pairs={{0,4},{4,8},{8,12},{12,16},{16,20},{20,24},{24,28},{28,32},{32,36}... | collective-permute-start | bytes 393224 | tf_op jit(solution)/shard_map/ppermute | solution.py:33
  69.8 3.4 %cross.3.first = bf16[64,1024]{1,0:T(8,128)(2,1)S(1)} custom-call(s32[1,32]{1,0:T(1,128)S(1)} %copy-done.8, bf16[512,1024]{1,0:T(8,128)(2,1)} %get-tuple-element.23.refs_1_, bf16[256,256]{1,0:T(8,128)(2,1)S(1)} %after.3.refs_2_, bf16[256,256]{1,0:T(8,128)(2,1)S(1)} %collective-permute-done.18.refs_3_, bf16[256,256]{1,0:T(8,128)(2,1)S(1)} %collective-permute-done.19.refs_4_, ...), custom_call_target="tpu_custom_call" | custom-call | flops 5000000000 | bytes 1024 | tf_op jit(solution)/shard_map/cross/pallas_call | solution.py:284
  73.2 0.8 %place.1 = bf16[1,128,1024]{2,1,0:T(8,128)(2,1)} custom-call(bf16[64,1024]{1,0:T(8,128)(2,1)S(1)} %collective-permute-done.17.received, bf16[64,1024]{1,0:T(8,128)(2,1)S(1)} %cross.3.first, bf16[64,1024]{1,0:T(8,128)(2,1)S(1)} %cross.2.second), custom_call_target="tpu_custom_call" | custom-call | flops 1000000000 | bytes 1024 | tf_op jit(solution)/shard_map/place/pallas_call | solution.py:408
  (45 shorter events, 0.7 us)
Async XLA Ops:
  0.0 17.1 %copy-start.9 = (bf16[256,1024]{1,0:T(8,128)(2,1)S(1)}, bf16[256,1024]{1,0:T(8,128)(2,1)}, u32[]{:S(2)}) copy-start(bf16[256,1024]{1,0:T(8,128)(2,1)} %w0.1) | copy-start | bytes 1572868
  2.2 29.1 %all-to-all-start = ((bf16[8,384,128]{2,1,0:T(8,128)(2,1)}), bf16[8,384,128]{2,1,0:T(8,128)(2,1)S(1)}, u32[]{:S(2)}, u32[]{:S(2)}) async-start(bf16[8,384,128]{2,1,0:T(8,128)(2,1)} %get-tuple-element.26), calls=%async_computation | async-start | bytes 1572864 | tf_op jit(solution)/shard_map/all_to_all | solution.py:57
  12.1 8.0 %collective-permute-start = (s32[4]{0:T(128)S(1)}, s32[4]{0:T(128)S(1)}, u32[]{:S(2)}, u32[]{:S(2)}) collective-permute-start(s32[4]{0:T(128)S(1)} %get-tuple-element.18.idx0.idx), channel_id=1, source_target_pairs={{0,64},{64,128},{128,192},{192,0},{1,65},{65,129},{129,193},{193,1... | collective-permute-start | bytes 56 | tf_op jit(solution)/shard_map/ppermute | solution.py:33
  13.4 6.7 %collective-permute-start.1 = (s32[4]{0:T(128)S(1)}, s32[4]{0:T(128)S(1)}, u32[]{:S(2)}, u32[]{:S(2)}) collective-permute-start(s32[4]{0:T(128)S(1)} %get-tuple-element.18.idx0.idx), channel_id=1, source_target_pairs={{0,128},{64,192},{128,0},{192,64},{1,129},{65,193},{129,1},{193,65... | collective-permute-start | bytes 56 | tf_op jit(solution)/shard_map/ppermute | solution.py:33
  16.0 4.1 %collective-permute-start.2 = (s32[4]{0:T(128)S(1)}, s32[4]{0:T(128)S(1)}, u32[]{:S(2)}, u32[]{:S(2)}) collective-permute-start(s32[4]{0:T(128)S(1)} %get-tuple-element.18.idx0.idx), channel_id=1, source_target_pairs={{0,192},{64,0},{128,64},{192,128},{1,193},{65,1},{129,65},{193,129... | collective-permute-start | bytes 56 | tf_op jit(solution)/shard_map/ppermute | solution.py:33
  17.1 14.2 %collective-permute-start.12 = (bf16[256,1024]{1,0:T(8,128)(2,1)S(1)}, bf16[256,1024]{1,0:T(8,128)(2,1)S(1)}, u32[]{:S(2)}, u32[]{:S(2)}) collective-permute-start(bf16[256,1024]{1,0:T(8,128)(2,1)S(1)} %copy-done.9), channel_id=1, source_target_pairs={{0,1},{1,2},{2,3},{3,0},{4,7},{5,4},{6,5},{7,6},{8,9},{9,10},{10,1... | collective-permute-start | bytes 1572872 | tf_op jit(solution)/shard_map/ppermute | solution.py:43
  19.5 10.6 %collective-permute-start.13 = (bf16[128,1024]{1,0:T(8,128)(2,1)S(1)}, bf16[128,1024]{1,0:T(8,128)(2,1)S(1)}, u32[]{:S(2)}, u32[]{:S(2)}) collective-permute-start(bf16[128,1024]{1,0:T(8,128)(2,1)S(1)} %get-tuple-element.25), channel_id=1, source_target_pairs={{0,2},{1,3},{2,0},{3,1},{4,6},{5,7},{6,4},{7,5},{8,10},{9,11},{10,... | collective-permute-start | bytes 786440 | tf_op jit(solution)/shard_map/ppermute | solution.py:33
  21.8 4.2 %collective-permute-start.3 = (bf16[256,256]{1,0:T(8,128)(2,1)S(1)}, bf16[256,256]{1,0:T(8,128)(2,1)S(1)}, u32[]{:S(2)}, u32[]{:S(2)}) collective-permute-start(bf16[256,256]{1,0:T(8,128)(2,1)S(1)} %get-tuple-element.20), channel_id=1, source_target_pairs={{0,192},{64,0},{128,64},{192,128},{1,193},{65,1},{129,65},{193,129... | collective-permute-start | bytes 393224 | tf_op jit(solution)/shard_map/ppermute | solution.py:33
  22.5 5.5 %collective-permute-start.4 = (bf16[256,256]{1,0:T(8,128)(2,1)S(1)}, bf16[256,256]{1,0:T(8,128)(2,1)S(1)}, u32[]{:S(2)}, u32[]{:S(2)}) collective-permute-start(bf16[256,256]{1,0:T(8,128)(2,1)S(1)} %get-tuple-element.21), channel_id=1, source_target_pairs={{0,128},{64,192},{128,0},{192,64},{1,129},{65,193},{129,1},{193,65... | collective-permute-start | bytes 393224 | tf_op jit(solution)/shard_map/ppermute | solution.py:33
  24.1 5.4 %collective-permute-start.5 = (bf16[256,256]{1,0:T(8,128)(2,1)S(1)}, bf16[256,256]{1,0:T(8,128)(2,1)S(1)}, u32[]{:S(2)}, u32[]{:S(2)}) collective-permute-start(bf16[256,256]{1,0:T(8,128)(2,1)S(1)} %get-tuple-element.22), channel_id=1, source_target_pairs={{0,64},{64,128},{128,192},{192,0},{1,65},{65,129},{129,193},{193,1... | collective-permute-start | bytes 393224 | tf_op jit(solution)/shard_map/ppermute | solution.py:33
  30.2 12.4 %copy-start.1 = (bf16[128,1024]{1,0:T(8,128)(2,1)}, bf16[128,1024]{1,0:T(8,128)(2,1)S(1)}, u32[]{:S(2)}) copy-start(bf16[128,1024]{1,0:T(8,128)(2,1)S(1)} %collective-permute-done.13.refs_3_.w_half) | copy-start | bytes 786436
  31.3 11.3 %copy-start = (bf16[256,1024]{1,0:T(8,128)(2,1)}, bf16[256,1024]{1,0:T(8,128)(2,1)S(1)}, u32[]{:S(2)}) copy-start(bf16[256,1024]{1,0:T(8,128)(2,1)S(1)} %collective-permute-done.12.refs_2_.w_near) | copy-start | bytes 1572868
  31.3 19.3 %copy-start.4 = (bf16[1024,256]{1,0:T(8,128)(2,1)S(1)}, bf16[1024,256]{1,0:T(8,128)(2,1)}, u32[]{:S(2)}) copy-start(bf16[1024,256]{1,0:T(8,128)(2,1)} %wq.2) | copy-start | bytes 1572868
  31.3 19.3 %copy-start.5 = (bf16[1024,256]{1,0:T(8,128)(2,1)S(1)}, bf16[1024,256]{1,0:T(8,128)(2,1)}, u32[]{:S(2)}) copy-start(bf16[1024,256]{1,0:T(8,128)(2,1)} %wk.1) | copy-start | bytes 1572868
  31.3 19.3 %copy-start.6 = (bf16[1024,256]{1,0:T(8,128)(2,1)S(1)}, bf16[1024,256]{1,0:T(8,128)(2,1)}, u32[]{:S(2)}) copy-start(bf16[1024,256]{1,0:T(8,128)(2,1)} %wv.1) | copy-start | bytes 1572868
  31.3 8.5 %collective-permute-start.16 = (bf16[8,384,128]{2,1,0:T(8,128)(2,1)S(1)}, bf16[8,384,128]{2,1,0:T(8,128)(2,1)S(1)}, u32[]{:S(2)}, u32[]{:S(2)}) collective-permute-start(bf16[8,384,128]{2,1,0:T(8,128)(2,1)S(1)} %after.2.own), channel_id=1, source_target_pairs={{0,4},{4,0},{8,12},{12,8},{16,20},{20,16},{24,28},{28,24},{32,36},... | collective-permute-start | bytes 2359304 | tf_op jit(solution)/shard_map/ppermute | solution.py:48
  35.5 13.6 %collective-permute-start.6 = (bf16[512,256]{1,0:T(8,128)(2,1)S(1)}, bf16[512,256]{1,0:T(8,128)(2,1)}, u32[]{:S(2)}, u32[]{:S(2)}) collective-permute-start(bf16[512,256]{1,0:T(8,128)(2,1)S(1)} %compact.1.x0.refs_1_), channel_id=1, source_target_pairs={{0,1},{1,2},{2,3},{3,0},{4,5},{5,6},{6,7},{7,4},{8,9},{9,10},{10,1... | collective-permute-start | bytes 786440 | tf_op jit(solution)/shard_map/ppermute | solution.py:33
  35.5 14.5 %collective-permute-start.7 = (bf16[512,256]{1,0:T(8,128)(2,1)S(1)}, bf16[512,256]{1,0:T(8,128)(2,1)}, u32[]{:S(2)}, u32[]{:S(2)}) collective-permute-start(bf16[512,256]{1,0:T(8,128)(2,1)S(1)} %compact.1.x0.refs_1_), channel_id=1, source_target_pairs={{0,2},{1,3},{2,0},{3,1},{4,6},{5,7},{6,4},{7,5},{8,10},{9,11},{10,... | collective-permute-start | bytes 786440 | tf_op jit(solution)/shard_map/ppermute | solution.py:33
  37.8 12.8 %collective-permute-start.8 = (bf16[512,256]{1,0:T(8,128)(2,1)S(1)}, bf16[512,256]{1,0:T(8,128)(2,1)}, u32[]{:S(2)}, u32[]{:S(2)}) collective-permute-start(bf16[512,256]{1,0:T(8,128)(2,1)S(1)} %compact.1.x0.refs_1_), channel_id=1, source_target_pairs={{0,3},{1,0},{2,1},{3,2},{4,7},{5,4},{6,5},{7,6},{8,11},{9,8},{10,9... | collective-permute-start | bytes 786440 | tf_op jit(solution)/shard_map/ppermute | solution.py:33
  38.9 18.1 %collective-permute-start.15 = (bf16[128,1024]{1,0:T(8,128)(2,1)S(1)}, bf16[128,1024]{1,0:T(8,128)(2,1)}, u32[]{:S(2)}, u32[]{:S(2)}) collective-permute-start(bf16[128,1024]{1,0:T(8,128)(2,1)S(1)} %collective-permute-done.13.refs_3_.w_half), channel_id=1, source_target_pairs={{0,4},{4,0},{8,12},{12,8},{16,20},{20,16},{24,28},{28,24},{32,36},... | collective-permute-start | bytes 786440 | tf_op jit(solution)/shard_map/ppermute | solution.py:48
  39.8 17.2 %collective-permute-start.14 = (bf16[256,1024]{1,0:T(8,128)(2,1)S(1)}, bf16[256,1024]{1,0:T(8,128)(2,1)}, u32[]{:S(2)}, u32[]{:S(2)}) collective-permute-start(bf16[256,1024]{1,0:T(8,128)(2,1)S(1)} %collective-permute-done.12.refs_2_.w_near), channel_id=1, source_target_pairs={{0,4},{4,0},{8,12},{12,8},{16,20},{20,16},{24,28},{28,24},{32,36},... | collective-permute-start | bytes 1572872 | tf_op jit(solution)/shard_map/ppermute | solution.py:48
  42.6 14.5 %all-to-all-start.1 = ((bf16[8,128,128]{2,1,0:T(8,128)(2,1)}), bf16[8,128,128]{2,1,0:T(8,128)(2,1)S(1)}, u32[]{:S(2)}, u32[]{:S(2)}) async-start(bf16[8,128,128]{2,1,0:T(8,128)(2,1)} %attend.1), calls=%async_computation.1 | async-start | bytes 524288 | tf_op jit(solution)/shard_map/all_to_all | solution.py:57
  49.1 7.9 %copy-start.7 = (bf16[8,128,128]{2,1,0:T(8,128)(2,1)S(1)}, bf16[8,128,128]{2,1,0:T(8,128)(2,1)}, u32[]{:S(2)}) copy-start(bf16[8,128,128]{2,1,0:T(8,128)(2,1)} %wq.3) | copy-start | bytes 786436
  53.2 9.6 %collective-permute-start.10 = (bf16[256,256]{1,0:T(8,128)(2,1)S(1)}, bf16[256,256]{1,0:T(8,128)(2,1)S(1)}, u32[]{:S(2)}, u32[]{:S(2)}) collective-permute-start(bf16[256,256]{1,0:T(8,128)(2,1)S(1)} %get-tuple-element.24.refs_2_), channel_id=1, source_target_pairs={{0,2},{1,3},{2,0},{3,1},{4,6},{5,7},{6,4},{7,5},{8,10},{9,11},{10,... | collective-permute-start | bytes 393224 | tf_op jit(solution)/shard_map/ppermute | solution.py:33
  54.6 8.3 %collective-permute-start.11 = (bf16[256,256]{1,0:T(8,128)(2,1)S(1)}, bf16[256,256]{1,0:T(8,128)(2,1)S(1)}, u32[]{:S(2)}, u32[]{:S(2)}) collective-permute-start(bf16[256,256]{1,0:T(8,128)(2,1)S(1)} %get-tuple-element.24.refs_2_), channel_id=1, source_target_pairs={{0,3},{1,0},{2,1},{3,2},{4,7},{5,4},{6,5},{7,6},{8,11},{9,8},{10,9... | collective-permute-start | bytes 393224 | tf_op jit(solution)/shard_map/ppermute | solution.py:33
  57.0 5.8 %collective-permute-start.9 = (bf16[256,256]{1,0:T(8,128)(2,1)S(1)}, bf16[256,256]{1,0:T(8,128)(2,1)S(1)}, u32[]{:S(2)}, u32[]{:S(2)}) collective-permute-start(bf16[256,256]{1,0:T(8,128)(2,1)S(1)} %get-tuple-element.24.refs_2_), channel_id=1, source_target_pairs={{0,1},{1,2},{2,3},{3,0},{4,5},{5,6},{6,7},{7,4},{8,9},{9,10},{10,1... | collective-permute-start | bytes 393224 | tf_op jit(solution)/shard_map/ppermute | solution.py:33
  57.0 5.8 %copy-start.3 = (bf16[1024,1024]{1,0:T(8,128)(2,1)S(1)}, bf16[1024,1024]{1,0:T(8,128)(2,1)}, u32[]{:S(2)}) copy-start(bf16[1024,1024]{1,0:T(8,128)(2,1)} %refs_8_.3) | copy-start | bytes 6291460
  58.8 4.0 %copy-start.2 = (bf16[1024,1024]{1,0:T(8,128)(2,1)S(1)}, bf16[1024,1024]{1,0:T(8,128)(2,1)}, u32[]{:S(2)}) copy-start(bf16[1024,1024]{1,0:T(8,128)(2,1)} %refs_7_.3) | copy-start | bytes 6291460
  58.9 10.9 %collective-permute-start.18 = (bf16[256,256]{1,0:T(8,128)(2,1)S(1)}, bf16[256,256]{1,0:T(8,128)(2,1)S(1)}, u32[]{:S(2)}, u32[]{:S(2)}) collective-permute-start(bf16[256,256]{1,0:T(8,128)(2,1)S(1)} %after.3.refs_2_), channel_id=1, source_target_pairs={{0,1},{1,2},{2,3},{3,0},{4,5},{5,6},{6,7},{7,4},{8,9},{9,10},{10,1... | collective-permute-start | bytes 393224 | tf_op jit(solution)/shard_map/ppermute | solution.py:33
  60.3 9.5 %collective-permute-start.19 = (bf16[256,256]{1,0:T(8,128)(2,1)S(1)}, bf16[256,256]{1,0:T(8,128)(2,1)S(1)}, u32[]{:S(2)}, u32[]{:S(2)}) collective-permute-start(bf16[256,256]{1,0:T(8,128)(2,1)S(1)} %after.3.refs_2_), channel_id=1, source_target_pairs={{0,2},{1,3},{2,0},{3,1},{4,6},{5,7},{6,4},{7,5},{8,10},{9,11},{10,... | collective-permute-start | bytes 393224 | tf_op jit(solution)/shard_map/ppermute | solution.py:33
  62.8 7.0 %collective-permute-start.20 = (bf16[256,256]{1,0:T(8,128)(2,1)S(1)}, bf16[256,256]{1,0:T(8,128)(2,1)S(1)}, u32[]{:S(2)}, u32[]{:S(2)}) collective-permute-start(bf16[256,256]{1,0:T(8,128)(2,1)S(1)} %after.3.refs_2_), channel_id=1, source_target_pairs={{0,3},{1,0},{2,1},{3,2},{4,7},{5,4},{6,5},{7,6},{8,11},{9,8},{10,9... | collective-permute-start | bytes 393224 | tf_op jit(solution)/shard_map/ppermute | solution.py:33
  66.2 6.9 %collective-permute-start.17 = (bf16[64,1024]{1,0:T(8,128)(2,1)S(1)}, bf16[64,1024]{1,0:T(8,128)(2,1)S(1)}, u32[]{:S(2)}, u32[]{:S(2)}) collective-permute-start(bf16[64,1024]{1,0:T(8,128)(2,1)S(1)} %cross.2.second), channel_id=1, source_target_pairs={{0,4},{4,8},{8,12},{12,16},{16,20},{20,24},{24,28},{28,32},{32,36}... | collective-permute-start | bytes 393224 | tf_op jit(solution)/shard_map/ppermute | solution.py:33
  (1 other events, 4.0 us)

commit v6 on v5

--- a/solution.py
+++ b/solution.py
@@ -169,7 +169,7 @@
     weights = [jnp.exp2((s - m) * EXP2_SCALE) for s, m in zip(scores, tops)]
     mixes = [dot(p.astype(BF), v) for p, (_, _, v) in zip(weights, blocks)]
     totals = [jnp.sum(p, axis=-1, keepdims=True) for p in weights]
-    return [mix / total for mix, total in zip(mixes, totals)]
+    return [mix * (1.0 / total) for mix, total in zip(mixes, totals)]
 
 
 def encode_kernel(x0, x1, x2, x3, wq, wk, wv, first, second, src_out, src, sems):
@@ -271,7 +271,7 @@
     mixes = [dot(p.astype(BF), values[:, c]) for p, c in zip(weights, heads)]
     totals = [jnp.sum(p, axis=-1, keepdims=True) for p in weights]
     for c, mix, total in zip(heads, mixes, totals):
-        out[:, c] = (so[rows, c].astype(F32) + mix / jnp.maximum(total, 1.0)).astype(BF)
+        out[:, c] = (so[rows, c].astype(F32) + mix * (1.0 / jnp.maximum(total, 1.0))).astype(BF)
 
 
 def cross(which, counts, source, attn, wo, wk, wv, cq, so):
@@ -381,7 +381,7 @@
             split = mine.shape[0]
             mixes.append(dot(p[:, :split], mine) + dot(p[:, split:], theirs))
         for z, mix, total in zip(group, mixes, totals):
-            out[turned(z)] = (mix / total).astype(BF)
+            out[turned(z)] = (mix * (1.0 / total)).astype(BF)
 
 
 def attend(own, other):

time: 74.4 us -> 74.4 us (level)
  no operation moved by 1% of the time
where the time goes in v6:
time: 74.4 us; the launch traced here: 73.9 us
  starting transfers between devices  46.5 us (62%)
  Pallas kernels  19.3 us (26%)
  waiting for transfers between devices  7.92 us (11%)
    ppermute x17, starting transfers between devices, shifted(): lax.ppermute(block, axis, [(i, (i + distance) % size) for i in range(size)])  22.2 us
    all_to_all x2, starting transfers between devices, over_z(): lax.all_to_all(blocks, 'seq', 0, 0, axis_index_groups=groups, tiled=True)  16.7 us
    ppermute x17, waiting for transfers between devices, shifted(): lax.ppermute(block, axis, [(i, (i + distance) % size) for i in range(size)])  6.83 us
    pallas_call x2, Pallas kernels, cross(): pl.pallas_call(body, out_shape=sds((SPAN, cols)), in_specs=[SMEM] + [ANY]...  6.72 us
    ppermute x3, starting transfers between devices, core_swap(): return lax.ppermute(block, 'seq', [(i, i ^ 1) for i in range(size)])  5.14 us
    pallas_call x1, Pallas kernels, attend(): pl.pallas_call(attend_kernel, out_shape=sds((N_Z, tok, HEAD_DIM)), in_spe...  2.76 us
    pallas_call x1, Pallas kernels, encode(): pl.pallas_call(encode_kernel, out_shape=[sds((rows // 2, width))] * 2 + [...  2.57 us
    ppermute x1, starting transfers between devices, to_sides(): return lax.ppermute(block, ('seq', 'mp'), route)  2.48 us
  transfers between devices with their start and end apart: 23, of which 6 were waited for; matrix products, arithmetic and copies ran while one was open for 0% of the time, Pallas kernels for 22%

profile of v6, /device:TPU:1, one launch (start us, length us, event | category | flops | bytes accessed | tf_op | source)
XLA Modules:
  0.0 73.9 jit_solution(2139331907107611911)
XLA Ops:
  0.0 2.2 %pack.1 = (bf16[8,384,128]{2,1,0:T(8,128)(2,1)}, s32[4]{0:T(128)S(1)}, bf16[128,1024]{1,0:T(8,128)(2,1)S(1)}) custom-call(bf16[1,128,1024]{2,1,0:T(8,128)(2,1)} %q.1, bf16[1,128,1024]{2,1,0:T(8,128)(2,1)} %k.1, bf16[1,128,1024]{2,1,0:T(8,128)(2,1)} %v.1, bf16[256,1024]{1,0:T(8,128)(2,1)} %w0.1, s32[1,2,2]{2,1,0:T(2,128)} %nbr_rows.1, s32[1,2,2]{2,1,0:T(2,128)} %nbr_owner.1), custom_call_target="tpu_custom_call" | custom-call | flops 1000000000 | bytes 1024 | tf_op jit(solution)/shard_map/pack/pallas_call | solution.py:323
  2.2 9.9 %all-to-all-start = ((bf16[8,384,128]{2,1,0:T(8,128)(2,1)}), bf16[8,384,128]{2,1,0:T(8,128)(2,1)S(1)}, u32[]{:S(2)}, u32[]{:S(2)}) async-start(bf16[8,384,128]{2,1,0:T(8,128)(2,1)} %get-tuple-element.26), calls=%async_computation | async-start | bytes 1572864 | tf_op jit(solution)/shard_map/all_to_all | solution.py:57
  12.1 1.3 %collective-permute-start = (s32[4]{0:T(128)S(1)}, s32[4]{0:T(128)S(1)}, u32[]{:S(2)}, u32[]{:S(2)}) collective-permute-start(s32[4]{0:T(128)S(1)} %get-tuple-element.18.idx0.idx), channel_id=1, source_target_pairs={{0,64},{64,128},{128,192},{192,0},{1,65},{65,129},{129,193},{193,1... | collective-permute-start | bytes 56 | tf_op jit(solution)/shard_map/ppermute | solution.py:33
  13.4 2.6 %collective-permute-start.1 = (s32[4]{0:T(128)S(1)}, s32[4]{0:T(128)S(1)}, u32[]{:S(2)}, u32[]{:S(2)}) collective-permute-start(s32[4]{0:T(128)S(1)} %get-tuple-element.18.idx0.idx), channel_id=1, source_target_pairs={{0,128},{64,192},{128,0},{192,64},{1,129},{65,193},{129,1},{193,65... | collective-permute-start | bytes 56 | tf_op jit(solution)/shard_map/ppermute | solution.py:33
  16.0 1.1 %collective-permute-start.2 = (s32[4]{0:T(128)S(1)}, s32[4]{0:T(128)S(1)}, u32[]{:S(2)}, u32[]{:S(2)}) collective-permute-start(s32[4]{0:T(128)S(1)} %get-tuple-element.18.idx0.idx), channel_id=1, source_target_pairs={{0,192},{64,0},{128,64},{192,128},{1,193},{65,1},{129,65},{193,129... | collective-permute-start | bytes 56 | tf_op jit(solution)/shard_map/ppermute | solution.py:33
  17.1 2.5 %collective-permute-start.12 = (bf16[256,1024]{1,0:T(8,128)(2,1)S(1)}, bf16[256,1024]{1,0:T(8,128)(2,1)S(1)}, u32[]{:S(2)}, u32[]{:S(2)}) collective-permute-start(bf16[256,1024]{1,0:T(8,128)(2,1)S(1)} %copy-done.9), channel_id=1, source_target_pairs={{0,1},{1,2},{2,3},{3,0},{4,7},{5,4},{6,5},{7,6},{8,9},{9,10},{10,1... | collective-permute-start | bytes 1572872 | tf_op jit(solution)/shard_map/ppermute | solution.py:43
  20.1 1.8 %fetch.1 = (bf16[256,256]{1,0:T(8,128)(2,1)S(1)}, bf16[256,256]{1,0:T(8,128)(2,1)S(1)}, bf16[256,256]{1,0:T(8,128)(2,1)S(1)}, bf16[256,256]{1,0:T(8,128)(2,1)S(1)}) custom-call(s32[4]{0:T(128)S(1)} %get-tuple-element.18.idx0.idx, s32[4]{0:T(128)S(1)} %collective-permute-done.idx1, s32[4]{0:T(128)S(1)} %collective-permute-done.1.idx2, ...), custom_call_target="tpu_custom_call" | custom-call | flops 5000000000 | bytes 1024 | tf_op jit(solution)/shard_map/fetch/pallas_call | solution.py:123
  21.9 0.6 collective-permute-start.3
  22.5 1.7 %collective-permute-start.4 = (bf16[256,256]{1,0:T(8,128)(2,1)S(1)}, bf16[256,256]{1,0:T(8,128)(2,1)S(1)}, u32[]{:S(2)}, u32[]{:S(2)}) collective-permute-start(bf16[256,256]{1,0:T(8,128)(2,1)S(1)} %get-tuple-element.21), channel_id=1, source_target_pairs={{0,128},{64,192},{128,0},{192,64},{1,129},{65,193},{129,1},{193,65... | collective-permute-start | bytes 393224 | tf_op jit(solution)/shard_map/ppermute | solution.py:33
  24.2 1.9 %collective-permute-done.3.r1 = bf16[256,256]{1,0:T(8,128)(2,1)S(1)} collective-permute-done((bf16[256,256]{1,0:T(8,128)(2,1)S(1)}, bf16[256,256]{1,0:T(8,128)(2,1)S(1)}, u32[]{:S(2)}, u32[]{:S(2)}) %collective-permute-start.3) | collective-permute-done | bytes 131104 | tf_op jit(solution)/shard_map/ppermute | solution.py:33
  26.1 1.9 %collective-permute-done.4.r2 = bf16[256,256]{1,0:T(8,128)(2,1)S(1)} collective-permute-done((bf16[256,256]{1,0:T(8,128)(2,1)S(1)}, bf16[256,256]{1,0:T(8,128)(2,1)S(1)}, u32[]{:S(2)}, u32[]{:S(2)}) %collective-permute-start.4) | collective-permute-done | bytes 131104 | tf_op jit(solution)/shard_map/ppermute | solution.py:33
  27.9 1.6 %collective-permute-done.5.r3 = bf16[256,256]{1,0:T(8,128)(2,1)S(1)} collective-permute-done((bf16[256,256]{1,0:T(8,128)(2,1)S(1)}, bf16[256,256]{1,0:T(8,128)(2,1)S(1)}, u32[]{:S(2)}, u32[]{:S(2)}) %collective-permute-start.5) | collective-permute-done | bytes 131104 | tf_op jit(solution)/shard_map/ppermute | solution.py:33
  29.5 0.7 compact.1.x0.refs_1_
  30.2 1.1 %collective-permute-done.12.refs_2_.w_near = bf16[256,1024]{1,0:T(8,128)(2,1)S(1)} collective-permute-done((bf16[256,1024]{1,0:T(8,128)(2,1)S(1)}, bf16[256,1024]{1,0:T(8,128)(2,1)S(1)}, u32[]{:S(2)}, u32[]{:S(2)}) %collective-permute-start.12) | collective-permute-done | bytes 524320 | tf_op jit(solution)/shard_map/ppermute | solution.py:43
  31.3 4.2 %collective-permute-start.16 = (bf16[8,384,128]{2,1,0:T(8,128)(2,1)S(1)}, bf16[8,384,128]{2,1,0:T(8,128)(2,1)S(1)}, u32[]{:S(2)}, u32[]{:S(2)}) collective-permute-start(bf16[8,384,128]{2,1,0:T(8,128)(2,1)S(1)} %after.2.own), channel_id=1, source_target_pairs={{0,4},{4,0},{8,12},{12,8},{16,20},{20,16},{24,28},{28,24},{32,36},... | collective-permute-start | bytes 2359304 | tf_op jit(solution)/shard_map/ppermute | solution.py:48
  35.5 2.3 %collective-permute-start.7 = (bf16[512,256]{1,0:T(8,128)(2,1)S(1)}, bf16[512,256]{1,0:T(8,128)(2,1)}, u32[]{:S(2)}, u32[]{:S(2)}) collective-permute-start(bf16[512,256]{1,0:T(8,128)(2,1)S(1)} %compact.1.x0.refs_1_), channel_id=1, source_target_pairs={{0,2},{1,3},{2,0},{3,1},{4,6},{5,7},{6,4},{7,5},{8,10},{9,11},{10,... | collective-permute-start | bytes 786440 | tf_op jit(solution)/shard_map/ppermute | solution.py:33
  37.8 0.9 %collective-permute-start.8 = (bf16[512,256]{1,0:T(8,128)(2,1)S(1)}, bf16[512,256]{1,0:T(8,128)(2,1)}, u32[]{:S(2)}, u32[]{:S(2)}) collective-permute-start(bf16[512,256]{1,0:T(8,128)(2,1)S(1)} %compact.1.x0.refs_1_), channel_id=1, source_target_pairs={{0,3},{1,0},{2,1},{3,2},{4,7},{5,4},{6,5},{7,6},{8,11},{9,8},{10,9... | collective-permute-start | bytes 786440 | tf_op jit(solution)/shard_map/ppermute | solution.py:33
  38.7 0.9 %collective-permute-start.15 = (bf16[128,1024]{1,0:T(8,128)(2,1)S(1)}, bf16[128,1024]{1,0:T(8,128)(2,1)}, u32[]{:S(2)}, u32[]{:S(2)}) collective-permute-start(bf16[128,1024]{1,0:T(8,128)(2,1)S(1)} %collective-permute-done.13.refs_3_.w_half), channel_id=1, source_target_pairs={{0,4},{4,0},{8,12},{12,8},{16,20},{20,16},{24,28},{28,24},{32,36},... | collective-permute-start | bytes 786440 | tf_op jit(solution)/shard_map/ppermute | solution.py:48
  39.7 2.8 %attend.1 = bf16[8,128,128]{2,1,0:T(8,128)(2,1)} custom-call(bf16[8,384,128]{2,1,0:T(8,128)(2,1)S(1)} %after.2.own, bf16[8,384,128]{2,1,0:T(8,128)(2,1)S(1)} %collective-permute-done.16.other), custom_call_target="tpu_custom_call" | custom-call | flops 10000000000 | bytes 1024 | tf_op jit(solution)/shard_map/attend/pallas_call | solution.py:390
  42.4 6.8 %all-to-all-start.1 = ((bf16[8,128,128]{2,1,0:T(8,128)(2,1)}), bf16[8,128,128]{2,1,0:T(8,128)(2,1)S(1)}, u32[]{:S(2)}, u32[]{:S(2)}) async-start(bf16[8,128,128]{2,1,0:T(8,128)(2,1)} %attend.1), calls=%async_computation.1 | async-start | bytes 524288 | tf_op jit(solution)/shard_map/all_to_all | solution.py:57
  49.2 0.8 %collective-permute-done.7.x2 = bf16[512,256]{1,0:T(8,128)(2,1)} collective-permute-done((bf16[512,256]{1,0:T(8,128)(2,1)S(1)}, bf16[512,256]{1,0:T(8,128)(2,1)}, u32[]{:S(2)}, u32[]{:S(2)}) %collective-permute-start.7) | collective-permute-done | bytes 262176 | tf_op jit(solution)/shard_map/ppermute | solution.py:33
  50.0 0.6 collective-permute-done.8.x3
  50.6 2.6 %encode.1 = (bf16[256,256]{1,0:T(8,128)(2,1)S(1)}, bf16[256,256]{1,0:T(8,128)(2,1)S(1)}, bf16[512,1024]{1,0:T(8,128)(2,1)}) custom-call(bf16[512,256]{1,0:T(8,128)(2,1)S(1)} %compact.1.x0.refs_1_, bf16[512,256]{1,0:T(8,128)(2,1)} %collective-permute-done.6.x1, bf16[512,256]{1,0:T(8,128)(2,1)} %collective-permute-done.7.x2, ...), custom_call_target="tpu_custom_call" | custom-call | flops 30000001024 | bytes 1024 | tf_op jit(solution)/shard_map/encode/pallas_call | solution.py:200
  53.2 1.2 %collective-permute-start.10 = (bf16[256,256]{1,0:T(8,128)(2,1)S(1)}, bf16[256,256]{1,0:T(8,128)(2,1)S(1)}, u32[]{:S(2)}, u32[]{:S(2)}) collective-permute-start(bf16[256,256]{1,0:T(8,128)(2,1)S(1)} %get-tuple-element.24.refs_2_), channel_id=1, source_target_pairs={{0,2},{1,3},{2,0},{3,1},{4,6},{5,7},{6,4},{7,5},{8,10},{9,11},{10,... | collective-permute-start | bytes 393224 | tf_op jit(solution)/shard_map/ppermute | solution.py:33
  54.4 2.4 %collective-permute-start.11 = (bf16[256,256]{1,0:T(8,128)(2,1)S(1)}, bf16[256,256]{1,0:T(8,128)(2,1)S(1)}, u32[]{:S(2)}, u32[]{:S(2)}) collective-permute-start(bf16[256,256]{1,0:T(8,128)(2,1)S(1)} %get-tuple-element.24.refs_2_), channel_id=1, source_target_pairs={{0,3},{1,0},{2,1},{3,2},{4,7},{5,4},{6,5},{7,6},{8,11},{9,8},{10,9... | collective-permute-start | bytes 393224 | tf_op jit(solution)/shard_map/ppermute | solution.py:33
  57.0 1.8 %load.1 = (bf16[1024,1024]{1,0:T(8,128)(2,1)S(1)}, bf16[128,1024]{1,0:T(8,128)(2,1)S(1)}, bf16[128,1024]{1,0:T(8,128)(2,1)S(1)}) custom-call(bf16[256,1024]{1,0:T(8,128)(2,1)} %w0.1, bf16[256,1024]{1,0:T(8,128)(2,1)} %copy-done, bf16[128,1024]{1,0:T(8,128)(2,1)} %copy-done.1, bf16[256,1024]{1,0:T(8,128)(2,1)} %collective-permute-done.14.s_near, ...), custom_call_target="tpu_custom_call" | custom-call | flops 3000000000 | bytes 1024 | tf_op jit(solution)/shard_map/load/pallas_call | solution.py:235
  58.8 1.5 %collective-permute-start.18 = (bf16[256,256]{1,0:T(8,128)(2,1)S(1)}, bf16[256,256]{1,0:T(8,128)(2,1)S(1)}, u32[]{:S(2)}, u32[]{:S(2)}) collective-permute-start(bf16[256,256]{1,0:T(8,128)(2,1)S(1)} %after.3.refs_2_), channel_id=1, source_target_pairs={{0,1},{1,2},{2,3},{3,0},{4,5},{5,6},{6,7},{7,4},{8,9},{9,10},{10,1... | collective-permute-start | bytes 393224 | tf_op jit(solution)/shard_map/ppermute | solution.py:33
  60.3 2.3 %collective-permute-start.19 = (bf16[256,256]{1,0:T(8,128)(2,1)S(1)}, bf16[256,256]{1,0:T(8,128)(2,1)S(1)}, u32[]{:S(2)}, u32[]{:S(2)}) collective-permute-start(bf16[256,256]{1,0:T(8,128)(2,1)S(1)} %after.3.refs_2_), channel_id=1, source_target_pairs={{0,2},{1,3},{2,0},{3,1},{4,6},{5,7},{6,4},{7,5},{8,10},{9,11},{10,... | collective-permute-start | bytes 393224 | tf_op jit(solution)/shard_map/ppermute | solution.py:33
  62.9 3.4 %cross.2.second = bf16[64,1024]{1,0:T(8,128)(2,1)S(1)} custom-call(s32[1,32]{1,0:T(1,128)S(1)} %copy-done.8, bf16[512,1024]{1,0:T(8,128)(2,1)} %get-tuple-element.23.refs_1_, bf16[256,256]{1,0:T(8,128)(2,1)S(1)} %get-tuple-element.24.refs_2_, bf16[256,256]{1,0:T(8,128)(2,1)S(1)} %collective-permute-done.9.refs_3_, ...), custom_call_target="tpu_custom_call" | custom-call | flops 5000000000 | bytes 1024 | tf_op jit(solution)/shard_map/cross/pallas_call | solution.py:284
  66.2 3.5 %collective-permute-start.17 = (bf16[64,1024]{1,0:T(8,128)(2,1)S(1)}, bf16[64,1024]{1,0:T(8,128)(2,1)S(1)}, u32[]{:S(2)}, u32[]{:S(2)}) collective-permute-start(bf16[64,1024]{1,0:T(8,128)(2,1)S(1)} %cross.2.second), channel_id=1, source_target_pairs={{0,4},{4,8},{8,12},{12,16},{16,20},{20,24},{24,28},{28,32},{32,36}... | collective-permute-start | bytes 393224 | tf_op jit(solution)/shard_map/ppermute | solution.py:33
  69.8 3.4 %cross.3.first = bf16[64,1024]{1,0:T(8,128)(2,1)S(1)} custom-call(s32[1,32]{1,0:T(1,128)S(1)} %copy-done.8, bf16[512,1024]{1,0:T(8,128)(2,1)} %get-tuple-element.23.refs_1_, bf16[256,256]{1,0:T(8,128)(2,1)S(1)} %after.3.refs_2_, bf16[256,256]{1,0:T(8,128)(2,1)S(1)} %collective-permute-done.18.refs_3_, bf16[256,256]{1,0:T(8,128)(2,1)S(1)} %collective-permute-done.19.refs_4_, ...), custom_call_target="tpu_custom_call" | custom-call | flops 5000000000 | bytes 1024 | tf_op jit(solution)/shard_map/cross/pallas_call | solution.py:284
  73.2 0.8 %place.1 = bf16[1,128,1024]{2,1,0:T(8,128)(2,1)} custom-call(bf16[64,1024]{1,0:T(8,128)(2,1)S(1)} %collective-permute-done.17.received, bf16[64,1024]{1,0:T(8,128)(2,1)S(1)} %cross.3.first, bf16[64,1024]{1,0:T(8,128)(2,1)S(1)} %cross.2.second), custom_call_target="tpu_custom_call" | custom-call | flops 1000000000 | bytes 1024 | tf_op jit(solution)/shard_map/place/pallas_call | solution.py:408
  (45 shorter events, 0.9 us)
Async XLA Ops:
  0.0 17.1 %copy-start.9 = (bf16[256,1024]{1,0:T(8,128)(2,1)S(1)}, bf16[256,1024]{1,0:T(8,128)(2,1)}, u32[]{:S(2)}) copy-start(bf16[256,1024]{1,0:T(8,128)(2,1)} %w0.1) | copy-start | bytes 1572868
  2.2 29.1 %all-to-all-start = ((bf16[8,384,128]{2,1,0:T(8,128)(2,1)}), bf16[8,384,128]{2,1,0:T(8,128)(2,1)S(1)}, u32[]{:S(2)}, u32[]{:S(2)}) async-start(bf16[8,384,128]{2,1,0:T(8,128)(2,1)} %get-tuple-element.26), calls=%async_computation | async-start | bytes 1572864 | tf_op jit(solution)/shard_map/all_to_all | solution.py:57
  12.1 8.0 %collective-permute-start = (s32[4]{0:T(128)S(1)}, s32[4]{0:T(128)S(1)}, u32[]{:S(2)}, u32[]{:S(2)}) collective-permute-start(s32[4]{0:T(128)S(1)} %get-tuple-element.18.idx0.idx), channel_id=1, source_target_pairs={{0,64},{64,128},{128,192},{192,0},{1,65},{65,129},{129,193},{193,1... | collective-permute-start | bytes 56 | tf_op jit(solution)/shard_map/ppermute | solution.py:33
  13.4 6.7 %collective-permute-start.1 = (s32[4]{0:T(128)S(1)}, s32[4]{0:T(128)S(1)}, u32[]{:S(2)}, u32[]{:S(2)}) collective-permute-start(s32[4]{0:T(128)S(1)} %get-tuple-element.18.idx0.idx), channel_id=1, source_target_pairs={{0,128},{64,192},{128,0},{192,64},{1,129},{65,193},{129,1},{193,65... | collective-permute-start | bytes 56 | tf_op jit(solution)/shard_map/ppermute | solution.py:33
  16.0 4.1 %collective-permute-start.2 = (s32[4]{0:T(128)S(1)}, s32[4]{0:T(128)S(1)}, u32[]{:S(2)}, u32[]{:S(2)}) collective-permute-start(s32[4]{0:T(128)S(1)} %get-tuple-element.18.idx0.idx), channel_id=1, source_target_pairs={{0,192},{64,0},{128,64},{192,128},{1,193},{65,1},{129,65},{193,129... | collective-permute-start | bytes 56 | tf_op jit(solution)/shard_map/ppermute | solution.py:33
  17.1 14.2 %collective-permute-start.12 = (bf16[256,1024]{1,0:T(8,128)(2,1)S(1)}, bf16[256,1024]{1,0:T(8,128)(2,1)S(1)}, u32[]{:S(2)}, u32[]{:S(2)}) collective-permute-start(bf16[256,1024]{1,0:T(8,128)(2,1)S(1)} %copy-done.9), channel_id=1, source_target_pairs={{0,1},{1,2},{2,3},{3,0},{4,7},{5,4},{6,5},{7,6},{8,9},{9,10},{10,1... | collective-permute-start | bytes 1572872 | tf_op jit(solution)/shard_map/ppermute | solution.py:43
  19.5 10.6 %collective-permute-start.13 = (bf16[128,1024]{1,0:T(8,128)(2,1)S(1)}, bf16[128,1024]{1,0:T(8,128)(2,1)S(1)}, u32[]{:S(2)}, u32[]{:S(2)}) collective-permute-start(bf16[128,1024]{1,0:T(8,128)(2,1)S(1)} %get-tuple-element.25), channel_id=1, source_target_pairs={{0,2},{1,3},{2,0},{3,1},{4,6},{5,7},{6,4},{7,5},{8,10},{9,11},{10,... | collective-permute-start | bytes 786440 | tf_op jit(solution)/shard_map/ppermute | solution.py:33
  21.9 4.2 %collective-permute-start.3 = (bf16[256,256]{1,0:T(8,128)(2,1)S(1)}, bf16[256,256]{1,0:T(8,128)(2,1)S(1)}, u32[]{:S(2)}, u32[]{:S(2)}) collective-permute-start(bf16[256,256]{1,0:T(8,128)(2,1)S(1)} %get-tuple-element.20), channel_id=1, source_target_pairs={{0,192},{64,0},{128,64},{192,128},{1,193},{65,1},{129,65},{193,129... | collective-permute-start | bytes 393224 | tf_op jit(solution)/shard_map/ppermute | solution.py:33
  22.5 5.5 %collective-permute-start.4 = (bf16[256,256]{1,0:T(8,128)(2,1)S(1)}, bf16[256,256]{1,0:T(8,128)(2,1)S(1)}, u32[]{:S(2)}, u32[]{:S(2)}) collective-permute-start(bf16[256,256]{1,0:T(8,128)(2,1)S(1)} %get-tuple-element.21), channel_id=1, source_target_pairs={{0,128},{64,192},{128,0},{192,64},{1,129},{65,193},{129,1},{193,65... | collective-permute-start | bytes 393224 | tf_op jit(solution)/shard_map/ppermute | solution.py:33
  24.2 5.3 %collective-permute-start.5 = (bf16[256,256]{1,0:T(8,128)(2,1)S(1)}, bf16[256,256]{1,0:T(8,128)(2,1)S(1)}, u32[]{:S(2)}, u32[]{:S(2)}) collective-permute-start(bf16[256,256]{1,0:T(8,128)(2,1)S(1)} %get-tuple-element.22), channel_id=1, source_target_pairs={{0,64},{64,128},{128,192},{192,0},{1,65},{65,129},{129,193},{193,1... | collective-permute-start | bytes 393224 | tf_op jit(solution)/shard_map/ppermute | solution.py:33
  30.2 12.2 %copy-start.1 = (bf16[128,1024]{1,0:T(8,128)(2,1)}, bf16[128,1024]{1,0:T(8,128)(2,1)S(1)}, u32[]{:S(2)}) copy-start(bf16[128,1024]{1,0:T(8,128)(2,1)S(1)} %collective-permute-done.13.refs_3_.w_half) | copy-start | bytes 786436
  31.3 11.1 %copy-start = (bf16[256,1024]{1,0:T(8,128)(2,1)}, bf16[256,1024]{1,0:T(8,128)(2,1)S(1)}, u32[]{:S(2)}) copy-start(bf16[256,1024]{1,0:T(8,128)(2,1)S(1)} %collective-permute-done.12.refs_2_.w_near) | copy-start | bytes 1572868
  31.3 19.3 %copy-start.4 = (bf16[1024,256]{1,0:T(8,128)(2,1)S(1)}, bf16[1024,256]{1,0:T(8,128)(2,1)}, u32[]{:S(2)}) copy-start(bf16[1024,256]{1,0:T(8,128)(2,1)} %wq.2) | copy-start | bytes 1572868
  31.3 19.3 %copy-start.5 = (bf16[1024,256]{1,0:T(8,128)(2,1)S(1)}, bf16[1024,256]{1,0:T(8,128)(2,1)}, u32[]{:S(2)}) copy-start(bf16[1024,256]{1,0:T(8,128)(2,1)} %wk.1) | copy-start | bytes 1572868
  31.3 19.3 %copy-start.6 = (bf16[1024,256]{1,0:T(8,128)(2,1)S(1)}, bf16[1024,256]{1,0:T(8,128)(2,1)}, u32[]{:S(2)}) copy-start(bf16[1024,256]{1,0:T(8,128)(2,1)} %wv.1) | copy-start | bytes 1572868
  31.3 8.3 %collective-permute-start.16 = (bf16[8,384,128]{2,1,0:T(8,128)(2,1)S(1)}, bf16[8,384,128]{2,1,0:T(8,128)(2,1)S(1)}, u32[]{:S(2)}, u32[]{:S(2)}) collective-permute-start(bf16[8,384,128]{2,1,0:T(8,128)(2,1)S(1)} %after.2.own), channel_id=1, source_target_pairs={{0,4},{4,0},{8,12},{12,8},{16,20},{20,16},{24,28},{28,24},{32,36},... | collective-permute-start | bytes 2359304 | tf_op jit(solution)/shard_map/ppermute | solution.py:48
  35.5 13.7 %collective-permute-start.6 = (bf16[512,256]{1,0:T(8,128)(2,1)S(1)}, bf16[512,256]{1,0:T(8,128)(2,1)}, u32[]{:S(2)}, u32[]{:S(2)}) collective-permute-start(bf16[512,256]{1,0:T(8,128)(2,1)S(1)} %compact.1.x0.refs_1_), channel_id=1, source_target_pairs={{0,1},{1,2},{2,3},{3,0},{4,5},{5,6},{6,7},{7,4},{8,9},{9,10},{10,1... | collective-permute-start | bytes 786440 | tf_op jit(solution)/shard_map/ppermute | solution.py:33
  35.5 14.5 %collective-permute-start.7 = (bf16[512,256]{1,0:T(8,128)(2,1)S(1)}, bf16[512,256]{1,0:T(8,128)(2,1)}, u32[]{:S(2)}, u32[]{:S(2)}) collective-permute-start(bf16[512,256]{1,0:T(8,128)(2,1)S(1)} %compact.1.x0.refs_1_), channel_id=1, source_target_pairs={{0,2},{1,3},{2,0},{3,1},{4,6},{5,7},{6,4},{7,5},{8,10},{9,11},{10,... | collective-permute-start | bytes 786440 | tf_op jit(solution)/shard_map/ppermute | solution.py:33
  37.8 12.8 %collective-permute-start.8 = (bf16[512,256]{1,0:T(8,128)(2,1)S(1)}, bf16[512,256]{1,0:T(8,128)(2,1)}, u32[]{:S(2)}, u32[]{:S(2)}) collective-permute-start(bf16[512,256]{1,0:T(8,128)(2,1)S(1)} %compact.1.x0.refs_1_), channel_id=1, source_target_pairs={{0,3},{1,0},{2,1},{3,2},{4,7},{5,4},{6,5},{7,6},{8,11},{9,8},{10,9... | collective-permute-start | bytes 786440 | tf_op jit(solution)/shard_map/ppermute | solution.py:33
  38.7 18.2 %collective-permute-start.15 = (bf16[128,1024]{1,0:T(8,128)(2,1)S(1)}, bf16[128,1024]{1,0:T(8,128)(2,1)}, u32[]{:S(2)}, u32[]{:S(2)}) collective-permute-start(bf16[128,1024]{1,0:T(8,128)(2,1)S(1)} %collective-permute-done.13.refs_3_.w_half), channel_id=1, source_target_pairs={{0,4},{4,0},{8,12},{12,8},{16,20},{20,16},{24,28},{28,24},{32,36},... | collective-permute-start | bytes 786440 | tf_op jit(solution)/shard_map/ppermute | solution.py:48
  39.7 17.3 %collective-permute-start.14 = (bf16[256,1024]{1,0:T(8,128)(2,1)S(1)}, bf16[256,1024]{1,0:T(8,128)(2,1)}, u32[]{:S(2)}, u32[]{:S(2)}) collective-permute-start(bf16[256,1024]{1,0:T(8,128)(2,1)S(1)} %collective-permute-done.12.refs_2_.w_near), channel_id=1, source_target_pairs={{0,4},{4,0},{8,12},{12,8},{16,20},{20,16},{24,28},{28,24},{32,36},... | collective-permute-start | bytes 1572872 | tf_op jit(solution)/shard_map/ppermute | solution.py:48
  42.4 14.5 %all-to-all-start.1 = ((bf16[8,128,128]{2,1,0:T(8,128)(2,1)}), bf16[8,128,128]{2,1,0:T(8,128)(2,1)S(1)}, u32[]{:S(2)}, u32[]{:S(2)}) async-start(bf16[8,128,128]{2,1,0:T(8,128)(2,1)} %attend.1), calls=%async_computation.1 | async-start | bytes 524288 | tf_op jit(solution)/shard_map/all_to_all | solution.py:57
  49.2 7.7 %copy-start.7 = (bf16[8,128,128]{2,1,0:T(8,128)(2,1)S(1)}, bf16[8,128,128]{2,1,0:T(8,128)(2,1)}, u32[]{:S(2)}) copy-start(bf16[8,128,128]{2,1,0:T(8,128)(2,1)} %wq.3) | copy-start | bytes 786436
  53.2 9.4 %collective-permute-start.10 = (bf16[256,256]{1,0:T(8,128)(2,1)S(1)}, bf16[256,256]{1,0:T(8,128)(2,1)S(1)}, u32[]{:S(2)}, u32[]{:S(2)}) collective-permute-start(bf16[256,256]{1,0:T(8,128)(2,1)S(1)} %get-tuple-element.24.refs_2_), channel_id=1, source_target_pairs={{0,2},{1,3},{2,0},{3,1},{4,6},{5,7},{6,4},{7,5},{8,10},{9,11},{10,... | collective-permute-start | bytes 393224 | tf_op jit(solution)/shard_map/ppermute | solution.py:33
  54.4 8.4 %collective-permute-start.11 = (bf16[256,256]{1,0:T(8,128)(2,1)S(1)}, bf16[256,256]{1,0:T(8,128)(2,1)S(1)}, u32[]{:S(2)}, u32[]{:S(2)}) collective-permute-start(bf16[256,256]{1,0:T(8,128)(2,1)S(1)} %get-tuple-element.24.refs_2_), channel_id=1, source_target_pairs={{0,3},{1,0},{2,1},{3,2},{4,7},{5,4},{6,5},{7,6},{8,11},{9,8},{10,9... | collective-permute-start | bytes 393224 | tf_op jit(solution)/shard_map/ppermute | solution.py:33
  56.9 6.0 %collective-permute-start.9 = (bf16[256,256]{1,0:T(8,128)(2,1)S(1)}, bf16[256,256]{1,0:T(8,128)(2,1)S(1)}, u32[]{:S(2)}, u32[]{:S(2)}) collective-permute-start(bf16[256,256]{1,0:T(8,128)(2,1)S(1)} %get-tuple-element.24.refs_2_), channel_id=1, source_target_pairs={{0,1},{1,2},{2,3},{3,0},{4,5},{5,6},{6,7},{7,4},{8,9},{9,10},{10,1... | collective-permute-start | bytes 393224 | tf_op jit(solution)/shard_map/ppermute | solution.py:33
  57.0 5.9 %copy-start.3 = (bf16[1024,1024]{1,0:T(8,128)(2,1)S(1)}, bf16[1024,1024]{1,0:T(8,128)(2,1)}, u32[]{:S(2)}) copy-start(bf16[1024,1024]{1,0:T(8,128)(2,1)} %refs_8_.3) | copy-start | bytes 6291460
  58.7 4.1 %copy-start.2 = (bf16[1024,1024]{1,0:T(8,128)(2,1)S(1)}, bf16[1024,1024]{1,0:T(8,128)(2,1)}, u32[]{:S(2)}) copy-start(bf16[1024,1024]{1,0:T(8,128)(2,1)} %refs_7_.3) | copy-start | bytes 6291460
  58.8 11.0 %collective-permute-start.18 = (bf16[256,256]{1,0:T(8,128)(2,1)S(1)}, bf16[256,256]{1,0:T(8,128)(2,1)S(1)}, u32[]{:S(2)}, u32[]{:S(2)}) collective-permute-start(bf16[256,256]{1,0:T(8,128)(2,1)S(1)} %after.3.refs_2_), channel_id=1, source_target_pairs={{0,1},{1,2},{2,3},{3,0},{4,5},{5,6},{6,7},{7,4},{8,9},{9,10},{10,1... | collective-permute-start | bytes 393224 | tf_op jit(solution)/shard_map/ppermute | solution.py:33
  60.3 9.5 %collective-permute-start.19 = (bf16[256,256]{1,0:T(8,128)(2,1)S(1)}, bf16[256,256]{1,0:T(8,128)(2,1)S(1)}, u32[]{:S(2)}, u32[]{:S(2)}) collective-permute-start(bf16[256,256]{1,0:T(8,128)(2,1)S(1)} %after.3.refs_2_), channel_id=1, source_target_pairs={{0,2},{1,3},{2,0},{3,1},{4,6},{5,7},{6,4},{7,5},{8,10},{9,11},{10,... | collective-permute-start | bytes 393224 | tf_op jit(solution)/shard_map/ppermute | solution.py:33
  62.6 7.1 %collective-permute-start.20 = (bf16[256,256]{1,0:T(8,128)(2,1)S(1)}, bf16[256,256]{1,0:T(8,128)(2,1)S(1)}, u32[]{:S(2)}, u32[]{:S(2)}) collective-permute-start(bf16[256,256]{1,0:T(8,128)(2,1)S(1)} %after.3.refs_2_), channel_id=1, source_target_pairs={{0,3},{1,0},{2,1},{3,2},{4,7},{5,4},{6,5},{7,6},{8,11},{9,8},{10,9... | collective-permute-start | bytes 393224 | tf_op jit(solution)/shard_map/ppermute | solution.py:33
  66.2 6.9 %collective-permute-start.17 = (bf16[64,1024]{1,0:T(8,128)(2,1)S(1)}, bf16[64,1024]{1,0:T(8,128)(2,1)S(1)}, u32[]{:S(2)}, u32[]{:S(2)}) collective-permute-start(bf16[64,1024]{1,0:T(8,128)(2,1)S(1)} %cross.2.second), channel_id=1, source_target_pairs={{0,4},{4,8},{8,12},{12,16},{16,20},{20,24},{24,28},{28,32},{32,36}... | collective-permute-start | bytes 393224 | tf_op jit(solution)/shard_map/ppermute | solution.py:33
  (1 other events, 4.1 us)
